TPU v7x, 256 devices: a whole 4x4x8 slice. The times are simulated.
256 devices in a mesh: ctx: 16 (over z, y_hi), head: 16 (over y_lo, x, core).
Axes of the slice: x: 4, y: 4 (y_hi: 2, y_lo: 2; y = y_hi * 2 + y_lo), z: 8, core: 2. Of those that a mesh axis runs over, the one named last changes fastest.
Arguments:
- asker_vectors: bfloat16 [4096, 64, 128], P('ctx', 'head'), may hold values from -15 to 15
- asker_memory_pairs: bfloat16 [4096, 16, 128], P('ctx'), may hold values from -9 to 9
- leading_memory_pairs: bfloat16 [1024, 16, 128], P('ctx'), may hold values from -9 to 9
- document_memory_pairs: bfloat16 [16384, 16, 128], P(('ctx', 'head')), may hold values from -200 to 200
- document_valid_extent: int32 [64], replicated, may hold values from 1 to 256, as said below
- softening_factor: float32 [64], P('head'), may hold values from 0.5 to 1
Outputs:
- attended: bfloat16 [4096, 64, 128], P('ctx', 'head')
Inputs may be any that keep to these rules, and one draw needn't show every extreme that they name: `document_valid_extent`: passages are padded to tiles of 256 rows: each tile is full or is the last tile of a passage; tile 0 is full.
All inputs are finite; a program needn't handle non-finite values.
Results may differ from a plain program's by a relative error of at most 0.0045.
Values may be sent and summed in bfloat16 or wider, within the bound.
No kernel may reach another device: no remote copies, remote signals or barrier semaphores. Data moves between devices by JAX's collectives and lax.ppermute only.
A program may use at most 64 MiB of HBM per device.

v0:
```python
import math

import jax
import jax.numpy as jnp
from jax import lax
from jax.sharding import PartitionSpec as P

ASKER_COUNT = 64
KVH = 8
TILE = 256


MASKED_SCORE = -1e30


def block_width(length):
    chosen = 1
    aligned = 0
    for candidate in range(1, min(length, 512) + 1):
        if length % candidate == 0:
            chosen = candidate
            if candidate % 128 == 0:
                aligned = candidate
    if aligned > 0:
        return aligned
    return chosen


def run_segment(running, own_rows, query_index, factor, key_rows, value_rows, marks, kind):
    count = key_rows.shape[0]
    width = block_width(count)
    blocks = count // width
    key_blocks = key_rows.reshape((blocks, width) + key_rows.shape[1:])
    value_blocks = value_rows.reshape((blocks, width) + value_rows.shape[1:])
    mark_blocks = marks.reshape(blocks, width)

    def step(state, inputs):
        key_block, value_block, mark_block = inputs
        run_peak, run_total, run_acc = state
        scores = jnp.einsum("grd,ngd->grn", own_rows, key_block, preferred_element_type=jnp.float32)
        if kind == "passage":
            scores = scores * factor[:, :, None]
            allowed = jnp.broadcast_to((mark_block > 0)[None, None, :], scores.shape)
        elif kind == "prefix":
            scores = scores * factor
            allowed = None
        else:
            scores = scores * factor
            allowed = mark_block[None, None, :] <= query_index[None, :, None]
        if allowed is None:
            new_peak = jnp.maximum(run_peak, scores.max(axis=-1))
            weights = jnp.exp(scores - new_peak[..., None])
        else:
            masked = jnp.where(allowed, scores, MASKED_SCORE)
            new_peak = jnp.maximum(run_peak, masked.max(axis=-1))
            weights = jnp.where(allowed, jnp.exp(masked - new_peak[..., None]), 0.0)
        shrink = jnp.exp(run_peak - new_peak)
        new_total = run_total * shrink + weights.sum(axis=-1)
        new_acc = run_acc * shrink[..., None] + jnp.einsum(
            "grn,ngd->grd",
            weights.astype(jnp.bfloat16),
            value_block,
            preferred_element_type=jnp.float32,
        )
        return ((new_peak, new_total, new_acc), None)

    result, _ = lax.scan(step, running, (key_blocks, value_blocks, mark_blocks))
    return result


def attend_keys(
    carried,
    own_rows,
    query_index,
    passage_factor,
    key_rows,
    value_rows,
    layout,
    document_valid_extent,
):
    pref_rows, pass_rows, query_rows = layout
    per_device = pref_rows + pass_rows + query_rows
    shard_count = key_rows.shape[0] // per_device
    resident_memory_pairs = key_rows.shape[1]
    head_dim = key_rows.shape[2]
    reciprocal_sqrt_dimension = 1.0 / math.sqrt(own_rows.shape[-1])
    key_shards = key_rows.reshape(shard_count, per_device, resident_memory_pairs, head_dim)
    value_shards = value_rows.reshape(shard_count, per_device, resident_memory_pairs, head_dim)

    def segment(shards, low, high):
        return shards[:, low:high].reshape(
            shard_count * (high - low), resident_memory_pairs, head_dim
        )

    shard_ids = jnp.arange(shard_count, dtype=jnp.int32)
    pass_pos = (
        shard_ids[:, None] * pass_rows + jnp.arange(pass_rows, dtype=jnp.int32)[None, :]
    ).reshape(-1)
    tile_index = pass_pos // TILE
    matches = (
        tile_index[:, None] == jnp.arange(document_valid_extent.shape[0], dtype=jnp.int32)[None, :]
    )
    live_len = jnp.sum(jnp.where(matches, document_valid_extent[None, :], 0), axis=1)
    live_marks = (pass_pos % TILE < live_len).astype(jnp.int32)
    query_marks = (
        shard_ids[:, None] * query_rows + jnp.arange(query_rows, dtype=jnp.int32)[None, :]
    ).reshape(-1)
    prefix_marks = jnp.zeros((shard_count * pref_rows,), jnp.int32)
    state = run_segment(
        carried,
        own_rows,
        query_index,
        reciprocal_sqrt_dimension,
        segment(key_shards, 0, pref_rows),
        segment(value_shards, 0, pref_rows),
        prefix_marks,
        "prefix",
    )
    state = run_segment(
        state,
        own_rows,
        query_index,
        passage_factor,
        segment(key_shards, pref_rows, pref_rows + pass_rows),
        segment(value_shards, pref_rows, pref_rows + pass_rows),
        live_marks,
        "passage",
    )
    state = run_segment(
        state,
        own_rows,
        query_index,
        reciprocal_sqrt_dimension,
        segment(key_shards, pref_rows + pass_rows, per_device),
        segment(value_shards, pref_rows + pass_rows, per_device),
        query_marks,
        "query",
    )
    return state


def to_rows(query_block, resident_memory_pairs):
    tokens, q_local, head_dim = query_block.shape
    askers_sharing_memory = q_local // resident_memory_pairs
    return (
        query_block.reshape(tokens, resident_memory_pairs, askers_sharing_memory, head_dim)
        .transpose(1, 0, 2, 3)
        .reshape(resident_memory_pairs, tokens * askers_sharing_memory, head_dim)
    )


def body(
    asker_vectors,
    asker_memory_pairs,
    leading_memory_pairs,
    document_memory_pairs,
    document_valid_extent,
    softening_factor,
):
    query_token_rows, q_local, head_dim = asker_vectors.shape
    ctx_pos = lax.axis_index("ctx")
    head_pos = lax.axis_index("head")
    head_count = lax.axis_size("head")
    copies = max(1, head_count // KVH)
    passage_rows = document_memory_pairs.shape[0]
    widened = jnp.repeat(
        document_memory_pairs.reshape(passage_rows, KVH, 2, head_dim), copies, axis=1
    ).reshape(passage_rows, 2 * KVH * copies, head_dim)
    moved = lax.all_to_all(widened, "head", split_axis=1, concat_axis=0, tiled=True)
    kv_local = max(1, q_local * KVH // ASKER_COUNT)
    first_slot = 2 * (head_pos * q_local // (ASKER_COUNT // KVH))
    own_leading = lax.dynamic_slice_in_dim(leading_memory_pairs, first_slot, 2 * kv_local, 1)
    own_asker = lax.dynamic_slice_in_dim(asker_memory_pairs, first_slot, 2 * kv_local, 1)
    cache_parts = (own_leading, moved, own_asker)
    key_rows = jnp.concatenate([own_part[:, 0::2] for own_part in cache_parts], axis=0)
    value_rows = jnp.concatenate([own_part[:, 1::2] for own_part in cache_parts], axis=0)
    resident_memory_pairs = key_rows.shape[1]
    askers_sharing_memory = q_local // resident_memory_pairs
    layout = (own_leading.shape[0], moved.shape[0], query_token_rows)
    row_count = query_token_rows * askers_sharing_memory
    reciprocal_sqrt_dimension = 1.0 / math.sqrt(head_dim)
    passage_factor = jnp.broadcast_to(
        (reciprocal_sqrt_dimension / softening_factor).reshape(
            resident_memory_pairs, 1, askers_sharing_memory
        ),
        (resident_memory_pairs, query_token_rows, askers_sharing_memory),
    ).reshape(resident_memory_pairs, row_count)
    token_rows = jnp.repeat(jnp.arange(query_token_rows, dtype=jnp.int32), askers_sharing_memory)
    start_state = (
        jnp.full((resident_memory_pairs, row_count), MASKED_SCORE, jnp.float32),
        jnp.zeros((resident_memory_pairs, row_count), jnp.float32),
        jnp.zeros((resident_memory_pairs, row_count, head_dim), jnp.float32),
    )
    own_rows = to_rows(asker_vectors, resident_memory_pairs)
    query_index = ctx_pos * query_token_rows + token_rows
    run_peak, run_total, run_acc = attend_keys(
        start_state,
        own_rows,
        query_index,
        passage_factor,
        lax.all_gather(key_rows, "ctx", axis=0, tiled=True),
        lax.all_gather(value_rows, "ctx", axis=0, tiled=True),
        layout,
        document_valid_extent,
    )
    result = (
        (run_acc / run_total[..., None])
        .reshape(resident_memory_pairs, query_token_rows, askers_sharing_memory, head_dim)
        .transpose(1, 0, 2, 3)
        .reshape(query_token_rows, q_local, head_dim)
    )
    return result.astype(jnp.bfloat16)


def solution(mesh):
    return jax.shard_map(
        body,
        mesh=mesh,
        in_specs=(
            P("ctx", "head", None),
            P("ctx", None, None),
            P("ctx", None, None),
            P(("ctx", "head"), None, None),
            P(),
            P("head"),
        ),
        out_specs=P("ctx", "head", None),
        check_vma=False,
    )
```

profile of v0, /device:TPU:1, one launch (start us, length us, event | category | flops | bytes accessed | tf_op | source)
XLA Modules:
  0.0 434.3 jit_solution(8079176675676737109)
XLA Ops:
  8.5 6.8 %all-to-all-start = ((bf16[64,32,128]{2,0,1:T(8,128)(2,1)}), bf16[64,32,128]{2,0,1:T(8,128)(2,1)S(1)}, u32[]{:S(2)}, u32[]{:S(2)}) async-start(bf16[64,32,128]{2,0,1:T(8,128)(2,1)} %bitcast.1), calls=%async_computation | async-start | bytes 1048576 | tf_op jit(solution)/shard_map/all_to_all | solution.py:169
  16.4 1.5 constant_dynamic-slice_fusion.3
  17.9 7.2 %all-to-all-done = bf16[64,32,128]{2,0,1:T(8,128)(2,1)S(1)} async-done(((bf16[64,32,128]{2,0,1:T(8,128)(2,1)}), bf16[64,32,128]{2,0,1:T(8,128)(2,1)S(1)}, u32[]{:S(2)}, u32[]{:S(2)}) %all-to-all-start) | async-done | bytes 524320 | tf_op jit(solution)/shard_map/all_to_all | solution.py:169
  29.0 104.8 %all-gather.3.cloned.1.call-done = bf16[21504,1,128]{2,0,1:T(8,128)(2,1)} async-done(((bf16[1344,1,128]{2,0,1:T(8,128)(2,1)}), bf16[21504,1,128]{2,0,1:T(8,128)(2,1)}) %all-gather.3.cloned.1.call-update) | async-done | bytes 5505040 | tf_op jit(solution)/shard_map/all_gather | solution.py:201
  136.0 4.6 %slice.58 = bf16[16,1024,1,128]{3,1,0,2:T(8,128)(2,1)} slice(bf16[16,1344,1,128]{3,1,0,2:T(8,128)(2,1)} %bitcast.171), slice={[0:16], [64:1088], [0:1], [0:128]} | slice | bytes 8388608 | tf_op jit(solution)/shard_map/slice | solution.py:91
  140.6 102.0 %all-gather.5.cloned.1.call-done = bf16[21504,1,128]{2,0,1:T(8,128)(2,1)} async-done(((bf16[1344,1,128]{2,0,1:T(8,128)(2,1)}), bf16[21504,1,128]{2,0,1:T(8,128)(2,1)}) %all-gather.5.cloned.1.call-update) | async-done | bytes 5505040 | tf_op jit(solution)/shard_map/all_gather | solution.py:202
  244.9 4.7 %slice.59 = bf16[16,1024,1,128]{3,1,0,2:T(8,128)(2,1)} slice(bf16[16,1344,1,128]{3,1,0,2:T(8,128)(2,1)} %bitcast.174), slice={[0:16], [64:1088], [0:1], [0:128]} | slice | bytes 8388608 | tf_op jit(solution)/shard_map/slice | solution.py:91
  249.5 3.1 while.47
  252.6 150.3 %while.45 = (s32[]{:T(128)}, f32[1,1024]{1,0:T(1,128)S(1)}, f32[1,1024]{1,0:T(1,128)S(1)}, f32[1,1024,128]{2,1,0:T(8,128)S(1)}, s32[32,512]{1,0:T(8,128)S(1)}, /...) while((s32[]{:T(128)}, f32[1,1024]{1,0:T(1,128)S(1)}, ...), condition=%wide.region_8.9_spmd.clone, body=%wide.region_5.8_spmd.clone.sunk | while | flops 275515904 | bytes 8483009 | solution.py:67
  255.4 1.9 fusion.88
  258.1 1.4 fusion.86
  260.1 1.9 fusion.88
  264.8 1.9 fusion.88
  269.5 1.9 fusion.88
  274.2 1.9 fusion.88
  278.9 1.9 fusion.88
  281.6 1.4 fusion.86
  283.6 1.9 fusion.88
  288.3 1.9 fusion.88
  293.0 1.9 fusion.88
  297.7 1.9 fusion.88
  302.4 1.9 fusion.88
  305.1 1.4 fusion.86
  307.1 1.9 fusion.88
  311.8 1.9 fusion.88
  316.5 1.9 fusion.88
  321.1 1.9 fusion.88
  325.8 1.9 fusion.88
  328.6 1.4 fusion.86
  330.5 1.9 fusion.88
  335.2 1.9 fusion.88
  339.9 1.9 fusion.88
  344.6 1.9 fusion.88
  349.3 1.9 fusion.88
  352.0 1.4 fusion.86
  354.0 1.9 fusion.88
  358.7 1.9 fusion.88
  363.4 1.9 fusion.88
  368.1 1.9 fusion.88
  372.8 1.9 fusion.88
  377.5 1.9 fusion.88
  382.2 1.9 fusion.88
  386.9 1.9 fusion.88
  391.6 1.9 fusion.88
  396.3 1.9 fusion.88
  399.0 1.4 fusion.86
  401.0 1.9 fusion.88
  402.9 23.6 %while.46 = (s32[]{:T(128)}, f32[1,1024]{1,0:T(1,128)S(1)}, f32[1,1024]{1,0:T(1,128)S(1)}, f32[1,1024,128]{2,1,0:T(8,128)S(1)}, s32[8,512]{1,0:T(8,128)}, /*inde...) while((s32[]{:T(128)}, f32[1,1024]{1,0:T(1,128)S(1)}, ...), condition=%wide.region_12.13_spmd.clone, body=%wide.region_9.12_spmd.clone.sunk | while | flops 277089280 | bytes 7964797 | solution.py:67
  (509 shorter events, 117.5 us)
Async XLA Ops:
  8.5 16.7 %all-to-all-start = ((bf16[64,32,128]{2,0,1:T(8,128)(2,1)}), bf16[64,32,128]{2,0,1:T(8,128)(2,1)S(1)}, u32[]{:S(2)}, u32[]{:S(2)}) async-start(bf16[64,32,128]{2,0,1:T(8,128)(2,1)} %bitcast.1), calls=%async_computation | async-start | bytes 1048576 | tf_op jit(solution)/shard_map/all_to_all | solution.py:169
  15.3 118.4 %all-gather.3.cloned.1.call-start = ((), (), s32[]{:S(2)}) async-start(), calls=%async_computation.1 | async-start | bytes 5849088 | tf_op jit(solution)/shard_map/all_gather | solution.py:201
  25.2 2.2 copy-start.3
  25.2 3.0 copy-start.4
  26.1 216.5 %all-gather.5.cloned.1.call-start = ((), (), s32[]{:S(2)}) async-start(), calls=%async_computation.2 | async-start | bytes 5849088 | tf_op jit(solution)/shard_map/all_gather | solution.py:202
  244.9 4.7 %copy-start = (bf16[256,4,128]{2,1,0:T(4,128)(2,1)S(1)}, bf16[256,4,128]{2,1,0:T(4,128)(2,1)}, u32[]{:S(2)}) copy-start(bf16[256,4,128]{2,1,0:T(4,128)(2,1)} %param.12) | copy-start | bytes 786436
  252.6 0.6 copy-start.1
  255.4 1.9 copy-start.2
  257.3 0.6 copy-start.1
  260.1 1.9 copy-start.2
  264.8 1.9 copy-start.2
  269.5 1.9 copy-start.2
  274.2 1.9 copy-start.2
  278.9 1.9 copy-start.2
  283.6 1.9 copy-start.2
  288.3 1.9 copy-start.2
  290.2 0.6 copy-start.1
  293.0 1.9 copy-start.2
  294.9 0.6 copy-start.1
  297.7 1.9 copy-start.2
  302.4 1.9 copy-start.2
  307.1 1.9 copy-start.2
  309.0 0.6 copy-start.1
  311.7 1.9 copy-start.2
  316.4 1.9 copy-start.2
  321.1 1.9 copy-start.2
  325.8 1.9 copy-start.2
  327.8 0.6 copy-start.1
  330.5 1.9 copy-start.2
  335.2 1.9 copy-start.2
  339.9 1.9 copy-start.2
  344.6 1.9 copy-start.2
  346.5 0.6 copy-start.1
  349.3 1.9 copy-start.2
  354.0 1.9 copy-start.2
  358.7 1.9 copy-start.2
  363.4 1.9 copy-start.2
  365.3 0.6 copy-start.1
  368.1 1.9 copy-start.2
  372.8 1.9 copy-start.2
  377.5 1.9 copy-start.2
  379.4 0.6 copy-start.1
  382.2 1.9 copy-start.2
  384.1 0.6 copy-start.1
  386.9 1.9 copy-start.2
  391.6 1.9 copy-start.2
  396.3 1.9 copy-start.2
  401.0 1.9 copy-start.2
  (22 other events, 13.9 us)
Sparse Core Ops, SparseCore 0:
  26.2 107.4 all-gather.2
  136.3 106.2 all-gather.4
where the time goes:
time: 438 us; the launch traced here: 434 us
  waiting for transfers between devices  214 us (49%)
  matrix products  117 us (27%)
  local copies, waits for them, and re-layouts  49.9 us (11%)
  other arithmetic  29.8 us (7%)
  between operations  13.7 us (3%)
  starting transfers between devices  6.91 us (2%)
    all_gather x1, waiting for transfers between devices, body(): lax.all_gather(key_rows, 'ctx', axis=0, tiled=True)  105 us
    all_gather x1, waiting for transfers between devices, body(): lax.all_gather(value_rows, 'ctx', axis=0, tiled=True)  102 us
    dot_general x42, matrix products, step(): jnp.einsum('grn,ngd->grd', weights.astype(jnp.bfloat16), value_block, pre...  68.7 us
    dot_general x42, matrix products, step(): jnp.einsum('grd,ngd->grn', own_rows, key_block, preferred_element_type=jn...  48 us
    reduce_sum x42, other arithmetic, step(): new_total = run_total * shrink + weights.sum(axis=-1)  23.5 us
    while x170, local copies, waits for them, and re-layouts  20.3 us
    slice x6, local copies, waits for them, and re-layouts, segment(): shards[:, low:high]  13.8 us
  transfers between devices with their start and end apart: 3, of which 3 were waited for; matrix products, arithmetic and copies ran while one was open for 3% of the time, Pallas kernels for 0%

commit v1 on v0

v1 whole, which is shorter than its diff:
```python
import functools
import math

import jax
import jax.numpy as jnp
from jax import lax
from jax.experimental import pallas as pl
from jax.experimental.pallas import tpu as pltpu
from jax.sharding import Mesh
from jax.sharding import PartitionSpec as P

F32 = jnp.float32
BF16 = jnp.bfloat16
KVH = 8
HD = 128
TILE = 256
RING = 8
SEND = 64
ROWS = 1024
BLOCKS = 4
AUX = 16
SUB = 512
MASKED = -1e30
HEADROOM = 100.0
LOG2E = math.log2(math.e)
SCALE2 = LOG2E / math.sqrt(HD)
VMEM_LIMIT = 48 * 2**20


def shift(count, step):
    return [(i, (i + step) % count) for i in range(count)]


def params():
    return pltpu.CompilerParams(vmem_limit_bytes=VMEM_LIMIT)


def whole(shape):
    return pl.BlockSpec(shape, lambda *_: (0,) * len(shape))


def split3(x):
    hi = x.astype(BF16)
    rest = x - hi.astype(F32)
    mid = rest.astype(BF16)
    low = (rest - mid.astype(F32)).astype(BF16)
    return hi, mid, low


def join3(rows):
    r = rows.astype(F32)
    return r[0:1] + r[1:2] + r[2:3]


def aux_rows(x):
    hi, mid, low = split3(x)
    pad = jnp.zeros((AUX - 3, x.shape[1]), F32)
    parts = [hi.astype(F32), mid.astype(F32), low.astype(F32), pad]
    return jnp.concatenate(parts, axis=0).astype(BF16)


def prepare_queries(soft_ref, q_ref, out_ref):
    tokens, heads, _ = q_ref.shape
    for h in range(heads):
        cols = slice(h * tokens, (h + 1) * tokens)
        out_ref[:HD, cols] = q_ref[:, h, :].astype(F32).T.astype(BF16)
        factor = jnp.full((1, tokens), 1.0, F32) / soft_ref[h] * SCALE2
        out_ref[HD:, cols] = aux_rows(factor)


def query_block(asker_vectors, softening_factor):
    tokens, heads, _ = asker_vectors.shape
    return pl.pallas_call(
        prepare_queries,
        in_specs=[pl.BlockSpec(memory_space=pltpu.SMEM), pl.BlockSpec(memory_space=pltpu.VMEM)],
        out_shape=jax.ShapeDtypeStruct((HD + AUX, tokens * heads), BF16),
        compiler_params=params(),
        name="queries",
    )(softening_factor, asker_vectors)


def prepare_documents(live_ref, doc_ref, out_ref):
    rows = doc_ref.shape[0]
    keep = lax.broadcasted_iota(jnp.int32, (rows, HD), 0) < live_ref[0]
    for g in range(KVH):
        for s in range(2):
            out_ref[g, s] = jnp.where(keep, doc_ref[:, 2 * g + s, :].astype(F32), 0.0).astype(BF16)


def document_blocks(document_memory_pairs, live_count):
    rows = document_memory_pairs.shape[0]
    return pl.pallas_call(
        prepare_documents,
        in_specs=[pl.BlockSpec(memory_space=pltpu.SMEM), pl.BlockSpec(memory_space=pltpu.VMEM)],
        out_shape=jax.ShapeDtypeStruct((KVH, 2, rows, HD), BF16),
        compiler_params=params(),
        name="documents",
    )(live_count.reshape(1), document_memory_pairs)


def lazy_pass(k_ref, v_ref, q_ref, scores_of, m, l, acc, out):
    m_out, l_out, acc_out = out
    width = q_ref.shape[1]
    excess = None
    for i in range(width // SUB):
        cols = slice(i * SUB, (i + 1) * SUB)
        s = scores_of(jnp.dot(k_ref[...], q_ref[:HD, cols], preferred_element_type=F32), cols)
        base = m[:, cols]
        over = jnp.max(s, axis=0, keepdims=True) - base
        excess = over if excess is None else jnp.maximum(excess, over)
        p = jnp.exp2(s - base).astype(BF16)
        o = jnp.dot(v_ref[...], p, preferred_element_type=F32)
        m_out[:, cols] = base
        l_out[:, cols] = l[:, cols] + o[HD : HD + 1]
        acc_out[:, cols] = acc[:, cols] + o[:HD]
    return jnp.max(excess) > HEADROOM


def exact_pass(k_ref, v_ref, q_ref, scores_of, m, l, acc, out):
    m_out, l_out, acc_out = out

    def step(i, carry):
        cols = pl.ds(pl.multiple_of(i * 128, 128), 128)
        s = scores_of(jnp.dot(k_ref[...], q_ref[:HD, cols], preferred_element_type=F32), cols)
        base = m[:, cols]
        peak = jnp.maximum(base, jnp.max(s, axis=0, keepdims=True))
        shrink = jnp.exp2(base - peak)
        p = jnp.exp2(s - peak).astype(BF16)
        o = jnp.dot(v_ref[...], p, preferred_element_type=F32)
        m_out[:, cols] = peak
        l_out[:, cols] = l[:, cols] * shrink + o[HD : HD + 1]
        acc_out[:, cols] = acc[:, cols] * shrink + o[:HD]
        return carry

    lax.fori_loop(0, q_ref.shape[1] // 128, step, 0)


def passage_kernel(shards, first, *refs):
    refs = list(refs)
    q_ref = refs.pop(0)
    if first:
        pre_ref = refs.pop(0)
        m0, l0, acc0 = refs[-3:]
        refs = refs[:-3]
    else:
        m0, l0, acc0 = refs[:3]
        refs = refs[3:]
    pay = refs[:shards]
    live = refs[shards : 2 * shards]
    m_out, l_out, acc_out, k_ref, v_ref = refs[2 * shards :]

    @pl.when(pl.program_id(0) == 0)
    def _():
        at = 0
        for r, lv in zip(pay, live):
            span = r.shape[0] * SEND
            values = []
            for j in range(r.shape[0]):
                k_ref[at + j * SEND : at + (j + 1) * SEND, :] = r[j, 0]
                values.append(r[j, 1])
            stacked = jnp.concatenate(values, axis=0).astype(F32)
            v_ref[:HD, at : at + span] = stacked.T.astype(BF16)
            v_ref[HD:, at : at + span] = lv[...]
            at += span

    if first:
        s = jnp.dot(pre_ref[...], q_ref[:HD, :], preferred_element_type=F32) * SCALE2
        m0[...] = jnp.max(s, axis=0, keepdims=True)
        l0[...] = jnp.zeros_like(l0)
        acc0[...] = jnp.zeros_like(acc0)

    def factor(cols):
        return join3(q_ref[HD : HD + 3, cols])

    out = (m_out, l_out, acc_out)
    redo = lazy_pass(k_ref, v_ref, q_ref, lambda s, cols: s * factor(cols), m0, l0, acc0, out)

    @pl.when(redo)
    def _():
        count = k_ref.shape[0]
        alive = jnp.broadcast_to(v_ref[HD : HD + 1, :].astype(F32), (128, count)).T

        def scores(s, cols):
            return jnp.where(alive > 0.5, s * factor(cols), MASKED)

        exact_pass(k_ref, v_ref, q_ref, scores, m0, l0, acc0, out)


def state_shapes(width):
    return [
        jax.ShapeDtypeStruct((1, width), F32),
        jax.ShapeDtypeStruct((1, width), F32),
        jax.ShapeDtypeStruct((HD, width), F32),
    ]


def row_spec(height):
    return pl.BlockSpec((height, ROWS), lambda i: (0, i))


def state_specs():
    return [row_spec(1), row_spec(1), row_spec(HD)]


def passages(queries, state, pays, lives, prefix_keys=None):
    first = state is None
    width = queries.shape[1]
    keys = sum(p.shape[0] * SEND for p in pays)
    args = [queries]
    specs = [row_spec(HD + AUX)]
    scratch = [pltpu.VMEM((keys, HD), BF16), pltpu.VMEM((HD + AUX, keys), BF16)]
    if first:
        args.append(prefix_keys)
        specs.append(whole(prefix_keys.shape))
        scratch += [pltpu.VMEM((1, ROWS), F32), pltpu.VMEM((1, ROWS), F32), pltpu.VMEM((HD, ROWS), F32)]
    else:
        args += list(state)
        specs += state_specs()
    args += list(pays) + list(lives)
    specs += [whole(p.shape) for p in pays] + [whole(v.shape) for v in lives]
    return pl.pallas_call(
        functools.partial(passage_kernel, len(pays), first),
        grid=(width // ROWS,),
        in_specs=specs,
        out_specs=state_specs(),
        out_shape=state_shapes(width),
        scratch_shapes=scratch,
        compiler_params=params(),
        name="passages",
    )(*args)


def direct_kernel(info_ref, q_ref, m0, l0, acc0, cache_ref, m_out, l_out, acc_out, k_ref, v_ref):
    pre = cache_ref.shape[2] - 128
    block = pl.program_id(0)

    @pl.when(block == 0)
    def _():
        values = []
        for z in range(RING):
            k_ref[z * 128 : (z + 1) * 128, :] = cache_ref[z, 0, :128]
            k_ref[RING * 128 + z * pre : RING * 128 + (z + 1) * pre, :] = cache_ref[z, 0, 128:]
        for z in range(RING):
            values.append(cache_ref[z, 1, :128])
        for z in range(RING):
            values.append(cache_ref[z, 1, 128:])
        stacked = jnp.concatenate(values, axis=0).astype(F32)
        v_ref[:HD, :] = stacked.T.astype(BF16)
        v_ref[HD:, :] = jnp.ones((AUX, v_ref.shape[1]), BF16)

    zpos, ypos, cpos = info_ref[0], info_ref[1], info_ref[2]
    tokens = TILE
    yrow = jnp.where(block % 2 == 0, ypos, 1 - ypos)
    asked = RING * 128

    def scores(s, cols):
        n = s.shape[1]
        if isinstance(cols, slice):
            start = cols.start
        else:
            start = cols.start
        token = (lax.broadcasted_iota(jnp.int32, (1, n), 1) + start) % tokens
        query = (2 * zpos + yrow) * tokens + token
        row = lax.broadcasted_iota(jnp.int32, (asked, 1), 0)
        key = (2 * (row // 128) + ypos) * tokens + cpos * 128 + row % 128
        s = s * SCALE2
        head = jnp.where(key <= query, s[:asked], MASKED)
        return jnp.concatenate([head, s[asked:]], axis=0)

    out = (m_out, l_out, acc_out)
    redo = lazy_pass(k_ref, v_ref, q_ref, scores, m0, l0, acc0, out)

    @pl.when(redo)
    def _():
        exact_pass(k_ref, v_ref, q_ref, scores, m0, l0, acc0, out)


def direct(queries, state, cache, info):
    width = queries.shape[1]
    keys = cache.shape[0] * cache.shape[2]
    return pl.pallas_call(
        direct_kernel,
        grid=(width // ROWS,),
        in_specs=[pl.BlockSpec(memory_space=pltpu.SMEM), row_spec(HD + AUX)] + state_specs() + [whole(cache.shape)],
        out_specs=state_specs(),
        out_shape=state_shapes(width),
        scratch_shapes=[pltpu.VMEM((keys, HD), BF16), pltpu.VMEM((HD + AUX, keys), BF16)],
        compiler_params=params(),
        name="direct",
    )(info, queries, *state, cache)


def pack(m, l, acc):
    total = m + jnp.log2(l)
    return jnp.concatenate([(acc / l).astype(BF16), aux_rows(total)], axis=0)


def pack_kernel(m, l, acc, out_ref):
    out_ref[...] = pack(m[...], l[...], acc[...])


def pack_blocks(state, low, high):
    width = (high - low) * ROWS

    def spec(height):
        return pl.BlockSpec((height, ROWS), lambda i: (0, i + low))

    return pl.pallas_call(
        pack_kernel,
        grid=(high - low,),
        in_specs=[spec(1), spec(1), spec(HD)],
        out_specs=row_spec(HD + AUX),
        out_shape=jax.ShapeDtypeStruct((HD + AUX, width), BF16),
        compiler_params=params(),
        name="pack",
    )(*state)


def fold(m, l, acc, received):
    other = join3(received[HD : HD + 3])
    peak = jnp.maximum(m, other)
    mine = jnp.exp2(m - peak)
    theirs = jnp.exp2(other - peak)
    return peak, l * mine + theirs, acc * mine + received[:HD].astype(F32) * theirs


def merge_kernel(m, l, acc, rec, m_out, l_out, acc_out, send_ref):
    total = m[...] + jnp.log2(l[...])
    m1, l1, acc1 = fold(total, jnp.ones_like(total), acc[...] / l[...], rec[...])

    @pl.when(pl.program_id(0) == 0)
    def _():
        send_ref[...] = pack(m1, l1, acc1)

    @pl.when(pl.program_id(0) == 1)
    def _():
        m_out[...] = m1
        l_out[...] = l1
        acc_out[...] = acc1


def merge_cores(state, received):
    def spec(height):
        return pl.BlockSpec((height, ROWS), lambda i: (0, 1 - i))

    def fixed(height):
        return pl.BlockSpec((height, ROWS), lambda i: (0, 0))

    return pl.pallas_call(
        merge_kernel,
        grid=(2,),
        in_specs=[spec(1), spec(1), spec(HD), spec(HD + AUX)],
        out_specs=[fixed(1), fixed(1), fixed(HD), fixed(HD + AUX)],
        out_shape=state_shapes(ROWS) + [jax.ShapeDtypeStruct((HD + AUX, ROWS), BF16)],
        compiler_params=params(),
        name="merge",
    )(*state, received)


def finish_kernel(m, l, acc, rec, out_ref):
    _, l1, acc1 = fold(m[...], l[...], acc[...], rec[...])
    result = acc1 / l1
    tokens, heads, _ = out_ref.shape
    for h in range(heads):
        out_ref[:, h, :] = result[:, h * tokens : (h + 1) * tokens].T.astype(BF16)


def finish(state, received, shape):
    return pl.pallas_call(
        finish_kernel,
        out_shape=jax.ShapeDtypeStruct(shape, BF16),
        compiler_params=params(),
        name="finish",
    )(*state, received)


def body(
    asker_vectors,
    asker_memory_pairs,
    leading_memory_pairs,
    document_memory_pairs,
    document_valid_extent,
    softening_factor,
):
    zpos, ypos, cpos = lax.axis_index("z"), lax.axis_index("yh"), lax.axis_index("c")
    group = lax.axis_index("yl") * 4 + lax.axis_index("x")
    ctx = 2 * zpos + ypos

    extent = document_valid_extent.reshape(RING, 2, 4)
    extent = lax.dynamic_index_in_dim(extent, ypos, 1, keepdims=False)
    offset = jnp.arange(2, dtype=jnp.int32) * 128 + cpos * SEND
    counts = (extent[:, :, None] - offset[None, None, :]).reshape(RING, KVH)
    counts = jnp.roll(counts, -zpos, axis=0)
    live = jnp.arange(SEND, dtype=jnp.int32)[None, None, :] < counts[:, :, None]
    live = live.astype(BF16).reshape(RING, 1, KVH * SEND)
    live = jnp.broadcast_to(live, (RING, AUX, KVH * SEND))
    own_count = lax.dynamic_index_in_dim(counts[0], group, 0, keepdims=False)

    sending = document_blocks(document_memory_pairs, own_count)
    own = lax.all_to_all(sending, ("yl", "x"), 0, 0, tiled=True)

    q0 = query_block(asker_vectors, softening_factor)
    q1 = lax.ppermute(q0, "yh", shift(2, 1))
    q2 = lax.ppermute(q0, "c", shift(2, 1))
    q3 = lax.ppermute(q1, "c", shift(2, 1))
    queries = jnp.concatenate([q0, q1, q2, q3], axis=1)

    half = asker_memory_pairs.shape[0] // 2
    lead = leading_memory_pairs.shape[0] // 2
    mine = lax.dynamic_slice(asker_memory_pairs, (cpos * half, 2 * group, 0), (half, 2, HD))
    led = lax.dynamic_slice(leading_memory_pairs, (cpos * lead, 2 * group, 0), (lead, 2, HD))
    cache_own = jnp.concatenate([mine, led], axis=0).transpose(1, 0, 2)
    cache = lax.all_gather(cache_own, "z", axis=0, tiled=False)
    prefix_keys = cache_own[0, half:]

    up, down = shift(RING, 1), shift(RING, -1)
    f1 = lax.ppermute(own, "z", up)
    b1 = lax.ppermute(own, "z", down)
    state = passages(queries, None, [own], [live[0]], prefix_keys)
    info = jnp.stack([zpos, ypos, cpos]).astype(jnp.int32)
    state = direct(queries, state, cache, info)
    f2 = lax.ppermute(f1, "z", up)
    b2 = lax.ppermute(b1, "z", down)
    state = passages(queries, state, [f1, b1], [live[7], live[1]])
    f3 = lax.ppermute(f2, "z", up)
    b3 = lax.ppermute(b2, "z", down)
    state = passages(queries, state, [f2, b2], [live[6], live[2]])
    f4 = lax.ppermute(f3[:4], "z", up)
    b4 = lax.ppermute(b3[4:], "z", down)
    state = passages(queries, state, [f3, b3], [live[5], live[3]])
    far = live[4]
    state = passages(queries, state, [f4, b4], [far[:, :256], far[:, 256:]])

    received = lax.ppermute(pack_blocks(state, 2, 4), "c", shift(2, 1))
    *kept, send = merge_cores(state, received)
    last = lax.ppermute(send, "yh", shift(2, 1))
    return finish(kept, last, asker_vectors.shape)


def solution(mesh):
    fine = Mesh(mesh.devices.reshape(8, 2, 2, 4, 2), ("z", "yh", "yl", "x", "c"))
    ctx, head = ("z", "yh"), ("yl", "x", "c")
    return jax.shard_map(
        body,
        mesh=fine,
        in_specs=(
            P(ctx, head, None),
            P(ctx, None, None),
            P(ctx, None, None),
            P(ctx + head, None, None),
            P(),
            P(head),
        ),
        out_specs=P(ctx, head, None),
        check_vma=False,
    )
```

time: 438 us -> 212 us (0.48)
  waiting for transfers between devices: 214 us -> 24.5 us
  Pallas kernels: 0 us -> 126 us
  matrix products: 117 us -> 0 us
  local copies, waits for them, and re-layouts: 49.9 us -> 5.61 us
  other arithmetic: 29.8 us -> 0.33 us
  starting transfers between devices: 6.91 us -> 34.4 us
  blocking collectives: 0 us -> 20.8 us
  between operations: 13.7 us -> 0.28 us
    all_gather x2 -> x0, waiting for transfers between devices: 207 us -> none  [the longest x1 105 us: body(): lax.all_gather(key_rows, 'ctx', axis=0, tiled=True)]
    pallas_call x0 -> x11, Pallas kernels: none -> 126 us  [the longest x5 112 us: passages(): pl.pallas_call(functools.partial(passage_kernel, len(pays), first), grid=...]
    dot_general x84 -> x0, matrix products: 117 us -> none  [the longest x42 68.7 us: step(): jnp.einsum('grn,ngd->grd', weights.astype(jnp.bfloat16), value_block, pre...]
    ppermute x0 -> x13, starting transfers between devices: none -> 30.2 us  [the longest x1 8.61 us: body(): received = lax.ppermute(pack_blocks(state, 2, 4), 'c', shift(2, 1))]
    reduce_sum x43 -> x0, other arithmetic: 24.2 us -> none  [the longest x42 23.5 us: step(): new_total = run_total * shrink + weights.sum(axis=-1)]
    all_gather x0 -> x1, blocking collectives: none -> 20.8 us  [body(): cache = lax.all_gather(cache_own, 'z', axis=0, tiled=False)]
    while x170 -> x0, local copies, waits for them, and re-layouts: 20.3 us -> none
    ppermute x0 -> x13, waiting for transfers between devices: none -> 18.5 us  [the longest x1 8.17 us: body(): last = lax.ppermute(send, 'yh', shift(2, 1))]
  transfers between devices with their start and end apart: 3 -> 14, of which waited for: 3 -> 5; matrix products, arithmetic and copies ran while one was open for 3% -> 2% of each run, Pallas kernels for 0% -> 49%
where the time goes in v1:
time: 212 us
  Pallas kernels  126 us (59%)
  starting transfers between devices  34.4 us (16%)
  waiting for transfers between devices  24.5 us (12%)
  blocking collectives  20.8 us (10%)
  local copies, waits for them, and re-layouts  5.61 us (3%)
    pallas_call x5, Pallas kernels, passages(): pl.pallas_call(functools.partial(passage_kernel, len(pays), first), grid=...  112 us
    all_gather x1, blocking collectives, body(): cache = lax.all_gather(cache_own, 'z', axis=0, tiled=False)  20.8 us
    ppermute x1, starting transfers between devices, body(): received = lax.ppermute(pack_blocks(state, 2, 4), 'c', shift(2, 1))  8.61 us
    pallas_call x1, Pallas kernels, direct(): pl.pallas_call(direct_kernel, grid=(width // ROWS,), in_specs=[pl.BlockSp...  8.48 us
    ppermute x1, waiting for transfers between devices, body(): last = lax.ppermute(send, 'yh', shift(2, 1))  8.17 us
    all_to_all x1, waiting for transfers between devices, body(): own = lax.all_to_all(sending, ('yl', 'x'), 0, 0, tiled=True)  6.07 us
    ppermute x1, waiting for transfers between devices, body(): f1 = lax.ppermute(own, 'z', up)  5.86 us
  transfers between devices with their start and end apart: 14, of which 5 were waited for; matrix products, arithmetic and copies ran while one was open for 2% of the time, Pallas kernels for 49%

profile of v1, /device:TPU:1, one launch (start us, length us, event | category | flops | bytes accessed | tf_op | source)
XLA Modules:
  0.0 212.0 jit_solution(804929701646489147)
XLA Ops:
  0.0 1.0 copy-done.1
  1.0 0.7 copy-done.3
  1.7 1.0 queries.1
  2.7 3.8 %collective-permute-start = (bf16[144,1024]{1,0:T(8,128)(2,1)S(1)}, bf16[144,1024]{1,0:T(8,128)(2,1)S(1)}, u32[]{:S(2)}, u32[]{:S(2)}) collective-permute-start(bf16[144,1024]{1,0:T(8,128)(2,1)S(1)} %queries.1), channel_id=1, source_target_pairs={{0,16},{16,0},{1,17},{17,1},{2,18},{18,2},{3,19},{19,3},{4,20},{20... | collective-permute-start | bytes 884744 | tf_op jit(solution)/shard_map/ppermute | solution.py:403
  6.5 1.0 collective-permute-start.1
  7.5 0.7 reshape.80
  8.3 0.1 copy.17
  8.4 0.1 sub.30
  8.4 0.1 broadcast_subtract_fusion
  8.5 0.1 pad_add_fusion
  8.6 0.1 constant_dynamic-slice_fusion.1
  8.7 0.5 constant_dynamic-slice_fusion
  9.2 0.9 copy-done.2
  10.2 1.7 documents.1
  11.9 4.1 %all-to-all-start = ((bf16[8,2,64,128]{3,2,1,0:T(8,128)(2,1)}), bf16[8,2,64,128]{3,2,1,0:T(8,128)(2,1)S(1)}, u32[]{:S(2)}, u32[]{:S(2)}) async-start(bf16[8,2,64,128]{3,2,1,0:T(8,128)(2,1)} %documents.1), calls=%async_computation | async-start | bytes 524288 | tf_op jit(solution)/shard_map/all_to_all | solution.py:400
  16.0 0.1 constant_dynamic-slice_fusion.4
  16.1 0.9 constant_dynamic-slice_fusion.3
  17.0 0.1 copy.18
  17.1 0.1 lt.66
  17.1 0.1 lt.67
  17.2 0.1 lt.64
  17.4 6.1 %all-to-all-done.refs_2_ = bf16[8,2,64,128]{3,2,1,0:T(8,128)(2,1)S(1)} async-done(((bf16[8,2,64,128]{3,2,1,0:T(8,128)(2,1)}), bf16[8,2,64,128]{3,2,1,0:T(8,128)(2,1)S(1)}, u32[]{:S(2)}, u32[]{:S(2)}) %all-to-all-start) | async-done | bytes 262176 | tf_op jit(solution)/shard_map/all_to_all | solution.py:400
  23.5 1.6 collective-permute-start.3
  25.1 3.9 %collective-permute-start.4 = (bf16[8,2,64,128]{3,2,1,0:T(8,128)(2,1)S(1)}, bf16[8,2,64,128]{3,2,1,0:T(8,128)(2,1)S(1)}, u32[]{:S(2)}, u32[]{:S(2)}) collective-permute-start(bf16[8,2,64,128]{3,2,1,0:T(8,128)(2,1)S(1)} %all-to-all-done.refs_2_), channel_id=1, source_target_pairs={{0,224},{32,0},{64,32},{96,64},{128,96},{160,128},{192,160},{224,1... | collective-permute-start | bytes 786440 | tf_op jit(solution)/shard_map/ppermute | solution.py:418
  29.0 5.9 %collective-permute-done.3.refs_4_ = bf16[8,2,64,128]{3,2,1,0:T(8,128)(2,1)S(1)} collective-permute-done((bf16[8,2,64,128]{3,2,1,0:T(8,128)(2,1)S(1)}, bf16[8,2,64,128]{3,2,1,0:T(8,128)(2,1)S(1)}, u32[]{:S(2)}, u32[]{:S(2)}) %collective-permute-start.3) | collective-permute-done | bytes 262176 | tf_op jit(solution)/shard_map/ppermute | solution.py:417
  34.9 2.7 %collective-permute-start.6 = (bf16[8,2,64,128]{3,2,1,0:T(8,128)(2,1)S(1)}, bf16[8,2,64,128]{3,2,1,0:T(8,128)(2,1)S(1)}, u32[]{:S(2)}, u32[]{:S(2)}) collective-permute-start(bf16[8,2,64,128]{3,2,1,0:T(8,128)(2,1)S(1)} %collective-permute-done.4.refs_5_), channel_id=1, source_target_pairs={{0,224},{32,0},{64,32},{96,64},{128,96},{160,128},{192,160},{224,1... | collective-permute-start | bytes 786440 | tf_op jit(solution)/shard_map/ppermute | solution.py:423
  37.6 0.1 slice_reduce_fusion
  37.7 2.0 collective-permute-start.2
  39.7 0.1 pad_add_fusion.1.info_ref
  39.8 2.8 %collective-permute-done.5.refs_4_ = bf16[8,2,64,128]{3,2,1,0:T(8,128)(2,1)S(1)} collective-permute-done((bf16[8,2,64,128]{3,2,1,0:T(8,128)(2,1)S(1)}, bf16[8,2,64,128]{3,2,1,0:T(8,128)(2,1)S(1)}, u32[]{:S(2)}, u32[]{:S(2)}) %collective-permute-start.5) | collective-permute-done | bytes 262176 | tf_op jit(solution)/shard_map/ppermute | solution.py:422
  42.5 2.7 %collective-permute-start.8 = (bf16[8,2,64,128]{3,2,1,0:T(8,128)(2,1)S(1)}, bf16[8,2,64,128]{3,2,1,0:T(8,128)(2,1)S(1)}, u32[]{:S(2)}, u32[]{:S(2)}) collective-permute-start(bf16[8,2,64,128]{3,2,1,0:T(8,128)(2,1)S(1)} %collective-permute-done.6.refs_5_), channel_id=1, source_target_pairs={{0,224},{32,0},{64,32},{96,64},{128,96},{160,128},{192,160},{224,1... | collective-permute-start | bytes 786440 | tf_op jit(solution)/shard_map/ppermute | solution.py:426
  45.2 20.8 %all-gather = bf16[16,160,128]{2,1,0:T(8,128)(2,1)S(1)} all-gather(bf16[2,160,128]{2,1,0:T(8,128)(2,1)S(1)} %maximum_bitcast_fusion), channel_id=2, replica_groups=mesh['z'=8,'yh'=2,'yl'=2,'x'=4,'c'=2] {'z'}, dimensions={0}, use_global_device_ids=true | all-gather | bytes 737280 | tf_op jit(solution)/shard_map/all_gather | solution.py:413
  66.1 2.0 collective-permute-start.10
  68.1 0.3 collective-permute-start.9
  68.3 0.1 pad_maximum_fusion.refs_0_.q_ref
  68.4 18.6 %passages.5 = (f32[1,4096]{1,0:T(1,128)S(1)}, f32[1,4096]{1,0:T(1,128)S(1)}, f32[128,4096]{1,0:T(8,128)S(1)}) custom-call(bf16[144,4096]{1,0:T(8,128)(2,1)S(1)} %pad_maximum_fusion.refs_0_.q_ref, bf16[32,128]{1,0:T(8,128)(2,1)S(1)} %slice_bitcast_fusion.refs_1_, bf16[8,2,64,128]{3,2,1,0:T(8,128)(2,1)S(1)} %all-to-all-done.refs_2_, ...), custom_call_target="tpu_custom_call" | custom-call | tf_op jit(solution)/shard_map/passages/pallas_call | solution.py:221
  87.0 8.5 %direct.1 = (f32[1,4096]{1,0:T(1,128)S(1)}, f32[1,4096]{1,0:T(1,128)S(1)}, f32[128,4096]{1,0:T(8,128)S(1)}) custom-call(s32[3]{0:T(128)S(1)} %pad_add_fusion.1.info_ref, bf16[144,4096]{1,0:T(8,128)(2,1)S(1)} %pad_maximum_fusion.refs_0_.q_ref, f32[1,4096]{1,0:T(1,128)S(1)} %get-tuple-element.27.m0, f32[1,4096]{1,0:T(1,128)S(1)} %get-tuple-element.28.l0, ...), custom_call_target="tpu_custom_call" | custom-call | tf_op jit(solution)/shard_map/direct/pallas_call | solution.py:281
  95.5 25.1 %passages.6 = (f32[1,4096]{1,0:T(1,128)S(1)}, f32[1,4096]{1,0:T(1,128)S(1)}, f32[128,4096]{1,0:T(8,128)S(1)}) custom-call(bf16[144,4096]{1,0:T(8,128)(2,1)S(1)} %pad_maximum_fusion.refs_0_.q_ref, f32[1,4096]{1,0:T(1,128)S(1)} %get-tuple-element.30.refs_1_, f32[1,4096]{1,0:T(1,128)S(1)} %get-tuple-element.31.refs_2_, ...), custom_call_target="tpu_custom_call" | custom-call | tf_op jit(solution)/shard_map/passages/pallas_call | solution.py:221
  120.7 25.1 %passages.7 = (f32[1,4096]{1,0:T(1,128)S(1)}, f32[1,4096]{1,0:T(1,128)S(1)}, f32[128,4096]{1,0:T(8,128)S(1)}) custom-call(bf16[144,4096]{1,0:T(8,128)(2,1)S(1)} %pad_maximum_fusion.refs_0_.q_ref, f32[1,4096]{1,0:T(1,128)S(1)} %get-tuple-element.33.refs_1_, f32[1,4096]{1,0:T(1,128)S(1)} %get-tuple-element.34.refs_2_, ...), custom_call_target="tpu_custom_call" | custom-call | tf_op jit(solution)/shard_map/passages/pallas_call | solution.py:221
  145.9 25.1 %passages.8 = (f32[1,4096]{1,0:T(1,128)S(1)}, f32[1,4096]{1,0:T(1,128)S(1)}, f32[128,4096]{1,0:T(8,128)S(1)}) custom-call(bf16[144,4096]{1,0:T(8,128)(2,1)S(1)} %pad_maximum_fusion.refs_0_.q_ref, f32[1,4096]{1,0:T(1,128)S(1)} %get-tuple-element.36.refs_1_, f32[1,4096]{1,0:T(1,128)S(1)} %get-tuple-element.37.refs_2_, ...), custom_call_target="tpu_custom_call" | custom-call | tf_op jit(solution)/shard_map/passages/pallas_call | solution.py:221
  171.0 18.5 %passages.9 = (f32[1,4096]{1,0:T(1,128)S(1)}, f32[1,4096]{1,0:T(1,128)S(1)}, f32[128,4096]{1,0:T(8,128)S(1)}) custom-call(bf16[144,4096]{1,0:T(8,128)(2,1)S(1)} %pad_maximum_fusion.refs_0_.q_ref, f32[1,4096]{1,0:T(1,128)S(1)} %get-tuple-element.39.refs_1_, f32[1,4096]{1,0:T(1,128)S(1)} %get-tuple-element.40.refs_2_, ...), custom_call_target="tpu_custom_call" | custom-call | tf_op jit(solution)/shard_map/passages/pallas_call | solution.py:221
  189.6 0.3 pack.1
  189.9 8.6 %collective-permute-start.11 = (bf16[144,2048]{1,0:T(8,128)(2,1)S(1)}, bf16[144,2048]{1,0:T(8,128)(2,1)S(1)}, u32[]{:S(2)}, u32[]{:S(2)}) collective-permute-start(bf16[144,2048]{1,0:T(8,128)(2,1)S(1)} %pack.1), channel_id=1, source_target_pairs={{0,1},{1,0},{2,3},{3,2},{4,5},{5,4},{6,7},{7,6},{8,9},{9,8},{10,11... | collective-permute-start | bytes 1769480 | tf_op jit(solution)/shard_map/ppermute | solution.py:434
  198.5 1.6 collective-permute-done.11.rec
  200.1 0.6 merge.1
  200.7 1.6 collective-permute-start.12
  202.4 8.2 %collective-permute-done.12.rec = bf16[144,1024]{1,0:T(8,128)(2,1)S(1)} collective-permute-done((bf16[144,1024]{1,0:T(8,128)(2,1)S(1)}, bf16[144,1024]{1,0:T(8,128)(2,1)S(1)}, u32[]{:S(2)}, u32[]{:S(2)}) %collective-permute-start.12) | collective-permute-done | bytes 294944 | tf_op jit(solution)/shard_map/ppermute | solution.py:436
  210.5 1.5 finish.1
  (38 shorter events, 0.2 us)
Async XLA Ops:
  0.0 16.0 %copy-start = (bf16[256,16,128]{2,1,0:T(8,128)(2,1)S(1)}, bf16[256,16,128]{2,1,0:T(8,128)(2,1)}, u32[]{:S(2)}) copy-start(bf16[256,16,128]{2,1,0:T(8,128)(2,1)} %param.7) | copy-start | bytes 3145732
  0.0 1.0 copy-start.1
  1.0 0.7 copy-start.3
  2.7 35.0 %collective-permute-start = (bf16[144,1024]{1,0:T(8,128)(2,1)S(1)}, bf16[144,1024]{1,0:T(8,128)(2,1)S(1)}, u32[]{:S(2)}, u32[]{:S(2)}) collective-permute-start(bf16[144,1024]{1,0:T(8,128)(2,1)S(1)} %queries.1), channel_id=1, source_target_pairs={{0,16},{16,0},{1,17},{17,1},{2,18},{18,2},{3,19},{19,3},{4,20},{20... | collective-permute-start | bytes 884744 | tf_op jit(solution)/shard_map/ppermute | solution.py:403
  6.5 61.8 %collective-permute-start.1 = (bf16[144,1024]{1,0:T(8,128)(2,1)S(1)}, bf16[144,1024]{1,0:T(8,128)(2,1)S(1)}, u32[]{:S(2)}, u32[]{:S(2)}) collective-permute-start(bf16[144,1024]{1,0:T(8,128)(2,1)S(1)} %queries.1), channel_id=1, source_target_pairs={{0,1},{1,0},{2,3},{3,2},{4,5},{5,4},{6,7},{7,6},{8,9},{9,8},{10,11... | collective-permute-start | bytes 884744 | tf_op jit(solution)/shard_map/ppermute | solution.py:404
  9.2 0.9 copy-start.2
  11.9 11.6 %all-to-all-start = ((bf16[8,2,64,128]{3,2,1,0:T(8,128)(2,1)}), bf16[8,2,64,128]{3,2,1,0:T(8,128)(2,1)S(1)}, u32[]{:S(2)}, u32[]{:S(2)}) async-start(bf16[8,2,64,128]{3,2,1,0:T(8,128)(2,1)} %documents.1), calls=%async_computation | async-start | bytes 524288 | tf_op jit(solution)/shard_map/all_to_all | solution.py:400
  23.5 11.5 %collective-permute-start.3 = (bf16[8,2,64,128]{3,2,1,0:T(8,128)(2,1)S(1)}, bf16[8,2,64,128]{3,2,1,0:T(8,128)(2,1)S(1)}, u32[]{:S(2)}, u32[]{:S(2)}) collective-permute-start(bf16[8,2,64,128]{3,2,1,0:T(8,128)(2,1)S(1)} %all-to-all-done.refs_2_), channel_id=1, source_target_pairs={{0,32},{32,64},{64,96},{96,128},{128,160},{160,192},{192,224},{224... | collective-permute-start | bytes 786440 | tf_op jit(solution)/shard_map/ppermute | solution.py:417
  25.1 9.8 %collective-permute-start.4 = (bf16[8,2,64,128]{3,2,1,0:T(8,128)(2,1)S(1)}, bf16[8,2,64,128]{3,2,1,0:T(8,128)(2,1)S(1)}, u32[]{:S(2)}, u32[]{:S(2)}) collective-permute-start(bf16[8,2,64,128]{3,2,1,0:T(8,128)(2,1)S(1)} %all-to-all-done.refs_2_), channel_id=1, source_target_pairs={{0,224},{32,0},{64,32},{96,64},{128,96},{160,128},{192,160},{224,1... | collective-permute-start | bytes 786440 | tf_op jit(solution)/shard_map/ppermute | solution.py:418
  34.9 7.6 %collective-permute-start.5 = (bf16[8,2,64,128]{3,2,1,0:T(8,128)(2,1)S(1)}, bf16[8,2,64,128]{3,2,1,0:T(8,128)(2,1)S(1)}, u32[]{:S(2)}, u32[]{:S(2)}) collective-permute-start(bf16[8,2,64,128]{3,2,1,0:T(8,128)(2,1)S(1)} %collective-permute-done.3.refs_4_), channel_id=1, source_target_pairs={{0,32},{32,64},{64,96},{96,128},{128,160},{160,192},{192,224},{224... | collective-permute-start | bytes 786440 | tf_op jit(solution)/shard_map/ppermute | solution.py:422
  34.9 7.6 %collective-permute-start.6 = (bf16[8,2,64,128]{3,2,1,0:T(8,128)(2,1)S(1)}, bf16[8,2,64,128]{3,2,1,0:T(8,128)(2,1)S(1)}, u32[]{:S(2)}, u32[]{:S(2)}) collective-permute-start(bf16[8,2,64,128]{3,2,1,0:T(8,128)(2,1)S(1)} %collective-permute-done.4.refs_5_), channel_id=1, source_target_pairs={{0,224},{32,0},{64,32},{96,64},{128,96},{160,128},{192,160},{224,1... | collective-permute-start | bytes 786440 | tf_op jit(solution)/shard_map/ppermute | solution.py:423
  37.7 30.7 %collective-permute-start.2 = (bf16[144,1024]{1,0:T(8,128)(2,1)S(1)}, bf16[144,1024]{1,0:T(8,128)(2,1)S(1)}, u32[]{:S(2)}, u32[]{:S(2)}) collective-permute-start(bf16[144,1024]{1,0:T(8,128)(2,1)S(1)} %collective-permute-done), channel_id=1, source_target_pairs={{0,1},{1,0},{2,3},{3,2},{4,5},{5,4},{6,7},{7,6},{8,9},{9,8},{10,11... | collective-permute-start | bytes 884744 | tf_op jit(solution)/shard_map/ppermute | solution.py:405
  42.5 25.5 %collective-permute-start.7 = (bf16[8,2,64,128]{3,2,1,0:T(8,128)(2,1)S(1)}, bf16[8,2,64,128]{3,2,1,0:T(8,128)(2,1)S(1)}, u32[]{:S(2)}, u32[]{:S(2)}) collective-permute-start(bf16[8,2,64,128]{3,2,1,0:T(8,128)(2,1)S(1)} %collective-permute-done.5.refs_4_), channel_id=1, source_target_pairs={{0,32},{32,64},{64,96},{96,128},{128,160},{160,192},{192,224},{224... | collective-permute-start | bytes 786440 | tf_op jit(solution)/shard_map/ppermute | solution.py:425
  42.5 23.5 %collective-permute-start.8 = (bf16[8,2,64,128]{3,2,1,0:T(8,128)(2,1)S(1)}, bf16[8,2,64,128]{3,2,1,0:T(8,128)(2,1)S(1)}, u32[]{:S(2)}, u32[]{:S(2)}) collective-permute-start(bf16[8,2,64,128]{3,2,1,0:T(8,128)(2,1)S(1)} %collective-permute-done.6.refs_5_), channel_id=1, source_target_pairs={{0,224},{32,0},{64,32},{96,64},{128,96},{160,128},{192,160},{224,1... | collective-permute-start | bytes 786440 | tf_op jit(solution)/shard_map/ppermute | solution.py:426
  66.1 104.9 %collective-permute-start.10 = (bf16[4,2,64,128]{3,2,1,0:T(8,128)(2,1)S(1)}, bf16[4,2,64,128]{3,2,1,0:T(8,128)(2,1)S(1)}, u32[]{:S(2)}, u32[]{:S(2)}) collective-permute-start(bf16[4,2,64,128]{3,2,1,0:T(8,128)(2,1)S(1)} %slice.90), channel_id=1, source_target_pairs={{0,224},{32,0},{64,32},{96,64},{128,96},{160,128},{192,160},{224,1... | collective-permute-start | bytes 393224 | tf_op jit(solution)/shard_map/ppermute | solution.py:429
  68.1 102.9 %collective-permute-start.9 = (bf16[4,2,64,128]{3,2,1,0:T(8,128)(2,1)S(1)}, bf16[4,2,64,128]{3,2,1,0:T(8,128)(2,1)S(1)}, u32[]{:S(2)}, u32[]{:S(2)}) collective-permute-start(bf16[4,2,64,128]{3,2,1,0:T(8,128)(2,1)S(1)} %slice.89), channel_id=1, source_target_pairs={{0,32},{32,64},{64,96},{96,128},{128,160},{160,192},{192,224},{224... | collective-permute-start | bytes 393224 | tf_op jit(solution)/shard_map/ppermute | solution.py:428
  189.9 10.2 %collective-permute-start.11 = (bf16[144,2048]{1,0:T(8,128)(2,1)S(1)}, bf16[144,2048]{1,0:T(8,128)(2,1)S(1)}, u32[]{:S(2)}, u32[]{:S(2)}) collective-permute-start(bf16[144,2048]{1,0:T(8,128)(2,1)S(1)} %pack.1), channel_id=1, source_target_pairs={{0,1},{1,0},{2,3},{3,2},{4,5},{5,4},{6,7},{7,6},{8,9},{9,8},{10,11... | collective-permute-start | bytes 1769480 | tf_op jit(solution)/shard_map/ppermute | solution.py:434
  200.7 9.8 %collective-permute-start.12 = (bf16[144,1024]{1,0:T(8,128)(2,1)S(1)}, bf16[144,1024]{1,0:T(8,128)(2,1)S(1)}, u32[]{:S(2)}, u32[]{:S(2)}) collective-permute-start(bf16[144,1024]{1,0:T(8,128)(2,1)S(1)} %get-tuple-element.48), channel_id=1, source_target_pairs={{0,16},{16,0},{1,17},{17,1},{2,18},{18,2},{3,19},{19,3},{4,20},{20... | collective-permute-start | bytes 884744 | tf_op jit(solution)/shard_map/ppermute | solution.py:436

commit v2 on v1

v2 whole, which is shorter than its diff:
```python
import functools
import math

import jax
import jax.numpy as jnp
from jax import lax
from jax.experimental import pallas as pl
from jax.experimental.pallas import tpu as pltpu
from jax.sharding import Mesh
from jax.sharding import PartitionSpec as P

F32 = jnp.float32
BF16 = jnp.bfloat16
KVH = 8
HD = 128
TILE = 256
RING = 8
SEND = 64
ROWS = 1024
BLOCKS = 4
AUX = 16
ASKED = 128
LED = 32
CACHE_ROWS = 2 * (ASKED + LED)
UNROLL = 2
SUB = 512
MASKED = -1e30
HEADROOM = 100.0
LOG2E = math.log2(math.e)
SCALE2 = LOG2E / math.sqrt(HD)
VMEM_LIMIT = 24 * 2**20


def shift(count, step):
    return [(i, (i + step) % count) for i in range(count)]


def params():
    return pltpu.CompilerParams(vmem_limit_bytes=VMEM_LIMIT)


def whole(shape):
    return pl.BlockSpec(shape, lambda *_: (0,) * len(shape))


def after(x, *others):
    return lax.optimization_barrier((x, *others))[0]


def split3(x):
    hi = x.astype(BF16)
    rest = x - hi.astype(F32)
    mid = rest.astype(BF16)
    low = (rest - mid.astype(F32)).astype(BF16)
    return hi, mid, low


def join3(rows):
    r = rows.astype(F32)
    return r[0:1] + r[1:2] + r[2:3]


def aux_rows(x):
    hi, mid, low = split3(x)
    pad = jnp.zeros((AUX - 3, x.shape[1]), F32)
    parts = [hi.astype(F32), mid.astype(F32), low.astype(F32), pad]
    return jnp.concatenate(parts, axis=0).astype(BF16)


def prepare_queries(soft_ref, q_ref, out_ref):
    tokens, heads, _ = q_ref.shape
    for h in range(heads):
        cols = slice(h * tokens, (h + 1) * tokens)
        out_ref[:HD, cols] = q_ref[:, h, :].astype(F32).T.astype(BF16)
        factor = jnp.full((1, tokens), 1.0, F32) / soft_ref[h] * SCALE2
        out_ref[HD:, cols] = aux_rows(factor)


def query_block(asker_vectors, softening_factor):
    tokens, heads, _ = asker_vectors.shape
    return pl.pallas_call(
        prepare_queries,
        in_specs=[pl.BlockSpec(memory_space=pltpu.SMEM), pl.BlockSpec(memory_space=pltpu.VMEM)],
        out_shape=jax.ShapeDtypeStruct((HD + AUX, tokens * heads), BF16),
        compiler_params=params(),
        name="queries",
    )(softening_factor, asker_vectors)


def live_counts(extent_ref, zpos):
    base = (2 * zpos + lax.axis_index("yh")) * 4
    start = lax.axis_index("c") * SEND
    return [extent_ref[base + j // 2] - (j % 2) * 128 - start for j in range(KVH)]


def prepare_documents(extent_ref, doc_ref, out_ref):
    rows = doc_ref.shape[0]
    own = lax.axis_index("yl") * 4 + lax.axis_index("x")
    live = jnp.int32(0)
    for j, count in enumerate(live_counts(extent_ref, lax.axis_index("z"))):
        live = jnp.where(own == j, count, live)
    keep = lax.broadcasted_iota(jnp.int32, (rows, HD), 0) < live
    for g in range(KVH):
        for s in range(2):
            out_ref[g, s] = jnp.where(keep, doc_ref[:, 2 * g + s, :].astype(F32), 0.0).astype(BF16)


def document_blocks(document_memory_pairs, extent):
    rows = document_memory_pairs.shape[0]
    return pl.pallas_call(
        prepare_documents,
        in_specs=[pl.BlockSpec(memory_space=pltpu.SMEM), pl.BlockSpec(memory_space=pltpu.VMEM)],
        out_shape=jax.ShapeDtypeStruct((KVH, 2, rows, HD), BF16),
        compiler_params=params(),
        name="documents",
    )(extent, document_memory_pairs)


def prepare_caches(asker_ref, lead_ref, out_ref):
    own = lax.axis_index("yl") * 4 + lax.axis_index("x")
    c = lax.axis_index("c")
    half, lead = asker_ref.shape[0] // 2, lead_ref.shape[0] // 2
    mine = pl.ds(pl.multiple_of(c * half, half), half)
    led = pl.ds(pl.multiple_of(c * lead, lead), lead)
    for g in range(KVH):

        @pl.when(own == g)
        def _():
            for s in range(2):
                out_ref[s * half : (s + 1) * half, :] = asker_ref[mine, 2 * g + s, :]
                at = 2 * half + s * lead
                out_ref[at : at + lead, :] = lead_ref[led, 2 * g + s, :]


def cache_block(asker_memory_pairs, leading_memory_pairs):
    return pl.pallas_call(
        prepare_caches,
        out_shape=jax.ShapeDtypeStruct((CACHE_ROWS, HD), BF16),
        compiler_params=params(),
        name="caches",
    )(asker_memory_pairs, leading_memory_pairs)


def attend_kernel(shards, first, *refs):
    refs = list(refs)
    extent_ref, q_ref = refs[:2]
    refs = refs[2:]
    if first:
        m0, l0, acc0 = refs[-3:]
        refs = refs[:-3]
    else:
        m0, l0, acc0 = refs[:3]
        refs = refs[3:]
    pay = refs[: len(shards)]
    m_out, l_out, acc_out, k_ref, v_ref = refs[len(shards) :]
    width = q_ref.shape[1]
    count = len(shards)
    zpos, ypos, cpos = lax.axis_index("z"), lax.axis_index("yh"), lax.axis_index("c")
    span = KVH * SEND
    asked_at = count * span
    led_at = asked_at + count * ASKED

    values, asked, led, alive, asked_alive = [], [], [], [], []
    for n, (ref, away) in enumerate(zip(pay, shards)):
        counts = live_counts(extent_ref, (zpos + away) % RING)
        lane = lax.broadcasted_iota(jnp.int32, (AUX, span), 1)
        bound = jnp.zeros((AUX, span), jnp.int32)
        for j in range(KVH):
            bound = jnp.where(lane // SEND == j, counts[j], bound)
            at = n * span + j * SEND
            k_ref[at : at + SEND, :] = ref[2 * j * SEND : (2 * j + 1) * SEND, :]
            values.append(ref[(2 * j + 1) * SEND : (2 * j + 2) * SEND, :])
        alive.append(jnp.where(lane % SEND < bound, 1.0, 0.0))
        at = 2 * span
        keys = ref[at : at + ASKED, :]
        vals = ref[at + ASKED : at + 2 * ASKED, :]
        if away == 0:
            asked_alive.append(jnp.ones((AUX, ASKED), F32))
        else:
            seen = (zpos + away >= 0) if away < 0 else (zpos + away >= RING)
            flag = jnp.where(seen, 1.0, 0.0).astype(F32)
            keys = (keys.astype(F32) * flag).astype(BF16)
            vals = (vals.astype(F32) * flag).astype(BF16)
            asked_alive.append(jnp.full((AUX, ASKED), 1.0, F32) * flag)
        k_ref[asked_at + n * ASKED : asked_at + (n + 1) * ASKED, :] = keys
        asked.append(vals)
        at += 2 * ASKED
        k_ref[led_at + n * LED : led_at + (n + 1) * LED, :] = ref[at : at + LED, :]
        led.append(ref[at + LED : at + 2 * LED, :])
    stacked = jnp.concatenate(values + asked + led, axis=0).astype(F32)
    v_ref[:HD, :] = stacked.T.astype(BF16)
    ones = [jnp.ones((AUX, count * LED), F32)]
    v_ref[HD:, :] = jnp.concatenate(alive + asked_alive + ones, axis=1).astype(BF16)

    if first:
        for i in range(width // SUB):
            cols = slice(i * SUB, (i + 1) * SUB)
            s = jnp.dot(k_ref[led_at:, :], q_ref[:HD, cols], preferred_element_type=F32) * SCALE2
            m0[:, cols] = jnp.max(s, axis=0, keepdims=True)
        l0[...] = jnp.zeros_like(l0)
        acc0[...] = jnp.zeros_like(acc0)

    def scores(cols, start, size):
        s = jnp.dot(k_ref[...], q_ref[:HD, cols], preferred_element_type=F32)
        factor = join3(q_ref[HD : HD + 3, cols])
        rest = s[asked_at:] * SCALE2
        if first:
            token = (lax.broadcasted_iota(jnp.int32, (1, size), 1) + start) % TILE
            block = start // ROWS
            yrow = jnp.where(block % 2 == 0, ypos, 1 - ypos)
            query = yrow * TILE + token
            key = ypos * TILE + cpos * ASKED + lax.broadcasted_iota(jnp.int32, (ASKED, 1), 0)
            near = jnp.where(key <= query, rest[:ASKED], MASKED)
            rest = jnp.concatenate([near, rest[ASKED:]], axis=0)
        return jnp.concatenate([s[:asked_at] * factor, rest], axis=0)

    def lazy(i, excess):
        start = pl.multiple_of(i * SUB, SUB)
        cols = pl.ds(start, SUB)
        s = scores(cols, start, SUB)
        base = m0[:, cols]
        excess = jnp.maximum(excess, jnp.max(s, axis=0, keepdims=True) - base)
        p = jnp.exp2(s - base).astype(BF16)
        o = jnp.dot(v_ref[...], p, preferred_element_type=F32)
        m_out[:, cols] = base
        l_out[:, cols] = l0[:, cols] + o[HD : HD + 1]
        acc_out[:, cols] = acc0[:, cols] + o[:HD]
        return excess

    excess = lax.fori_loop(0, width // SUB, lazy, jnp.full((1, SUB), MASKED, F32), unroll=UNROLL)

    @pl.when(jnp.max(excess) > HEADROOM)
    def _():
        total = k_ref.shape[0]
        living = jnp.broadcast_to(v_ref[HD : HD + 1, :].astype(F32), (128, total)).T

        def exact(i, carry):
            start = pl.multiple_of(i * 128, 128)
            cols = pl.ds(start, 128)
            s = jnp.where(living > 0.5, scores(cols, start, 128), MASKED)
            base = m0[:, cols]
            peak = jnp.maximum(base, jnp.max(s, axis=0, keepdims=True))
            shrink = jnp.exp2(base - peak)
            p = jnp.exp2(s - peak).astype(BF16)
            o = jnp.dot(v_ref[...], p, preferred_element_type=F32)
            m_out[:, cols] = peak
            l_out[:, cols] = l0[:, cols] * shrink + o[HD : HD + 1]
            acc_out[:, cols] = acc0[:, cols] * shrink + o[:HD]
            return carry

        lax.fori_loop(0, width // 128, exact, 0)


def state_shapes(width):
    return [
        jax.ShapeDtypeStruct((1, width), F32),
        jax.ShapeDtypeStruct((1, width), F32),
        jax.ShapeDtypeStruct((HD, width), F32),
    ]


def row_spec(height):
    return pl.BlockSpec((height, ROWS), lambda i: (0, i))


def attend(extent, queries, state, pays, shards):
    first = state is None
    width = queries.shape[1]
    keys = len(shards) * (KVH * SEND + ASKED + LED)
    scratch = [pltpu.VMEM((keys, HD), BF16), pltpu.VMEM((HD + AUX, keys), BF16)]
    args = [extent, queries]
    if first:
        scratch += [pltpu.VMEM((1, width), F32), pltpu.VMEM((1, width), F32), pltpu.VMEM((HD, width), F32)]
    else:
        args += list(state)
    args += list(pays)
    vmem = pl.BlockSpec(memory_space=pltpu.VMEM)
    return pl.pallas_call(
        functools.partial(attend_kernel, shards, first),
        in_specs=[pl.BlockSpec(memory_space=pltpu.SMEM)] + [vmem] * (len(args) - 1),
        out_specs=[vmem] * 3,
        out_shape=state_shapes(width),
        scratch_shapes=scratch,
        compiler_params=params(),
        name="attend",
    )(*args)


def pack(m, l, acc):
    total = m + jnp.log2(l)
    return jnp.concatenate([(acc / l).astype(BF16), aux_rows(total)], axis=0)


def pack_kernel(m, l, acc, out_ref):
    out_ref[...] = pack(m[...], l[...], acc[...])


def pack_blocks(state, low, high):
    width = (high - low) * ROWS

    def spec(height):
        return pl.BlockSpec((height, ROWS), lambda i: (0, i + low))

    return pl.pallas_call(
        pack_kernel,
        grid=(high - low,),
        in_specs=[spec(1), spec(1), spec(HD)],
        out_specs=row_spec(HD + AUX),
        out_shape=jax.ShapeDtypeStruct((HD + AUX, width), BF16),
        compiler_params=params(),
        name="pack",
    )(*state)


def fold(m, l, acc, received):
    other = join3(received[HD : HD + 3])
    peak = jnp.maximum(m, other)
    mine = jnp.exp2(m - peak)
    theirs = jnp.exp2(other - peak)
    return peak, l * mine + theirs, acc * mine + received[:HD].astype(F32) * theirs


def merge_kernel(m, l, acc, rec, m_out, l_out, acc_out, send_ref):
    total = m[...] + jnp.log2(l[...])
    m1, l1, acc1 = fold(total, jnp.ones_like(total), acc[...] / l[...], rec[...])

    @pl.when(pl.program_id(0) == 0)
    def _():
        send_ref[...] = pack(m1, l1, acc1)

    @pl.when(pl.program_id(0) == 1)
    def _():
        m_out[...] = m1
        l_out[...] = l1
        acc_out[...] = acc1


def merge_cores(state, received):
    def spec(height):
        return pl.BlockSpec((height, ROWS), lambda i: (0, 1 - i))

    def fixed(height):
        return pl.BlockSpec((height, ROWS), lambda i: (0, 0))

    return pl.pallas_call(
        merge_kernel,
        grid=(2,),
        in_specs=[spec(1), spec(1), spec(HD), spec(HD + AUX)],
        out_specs=[fixed(1), fixed(1), fixed(HD), fixed(HD + AUX)],
        out_shape=state_shapes(ROWS) + [jax.ShapeDtypeStruct((HD + AUX, ROWS), BF16)],
        compiler_params=params(),
        name="merge",
    )(*state, received)


def finish_kernel(m, l, acc, rec, out_ref):
    _, l1, acc1 = fold(m[...], l[...], acc[...], rec[...])
    result = acc1 / l1
    tokens, heads, _ = out_ref.shape
    for h in range(heads):
        out_ref[:, h, :] = result[:, h * tokens : (h + 1) * tokens].T.astype(BF16)


def finish(state, received, shape):
    return pl.pallas_call(
        finish_kernel,
        out_shape=jax.ShapeDtypeStruct(shape, BF16),
        compiler_params=params(),
        name="finish",
    )(*state, received)


def body(
    asker_vectors,
    asker_memory_pairs,
    leading_memory_pairs,
    document_memory_pairs,
    document_valid_extent,
    softening_factor,
):
    extent = document_valid_extent
    sending = document_blocks(document_memory_pairs, extent)
    q0 = query_block(after(asker_vectors, sending), softening_factor)
    q1 = lax.ppermute(q0, "yh", shift(2, 1))
    q2 = lax.ppermute(q0, "c", shift(2, 1))
    cache = cache_block(asker_memory_pairs, leading_memory_pairs)
    moved = lax.all_to_all(sending, ("yl", "x"), 0, 0, tiled=True)
    own = jnp.concatenate([moved.reshape(-1, HD), cache], axis=0)

    up, down = shift(RING, 1), shift(RING, -1)
    f1 = lax.ppermute(own, "z", up)
    b1 = lax.ppermute(own, "z", down)
    q3 = lax.ppermute(q1, "c", shift(2, 1))
    queries = jnp.concatenate([q0, q1, q2, q3], axis=1)
    state = attend(extent, queries, None, [own], [0])
    f2 = lax.ppermute(after(f1, state[0]), "z", up)
    b2 = lax.ppermute(after(b1, state[0]), "z", down)
    state = attend(extent, queries, state, [f1, b1], [-1, 1])
    f3 = lax.ppermute(after(f2, state[0]), "z", up)
    b3 = lax.ppermute(after(b2, state[0]), "z", down)
    state = attend(extent, queries, state, [f2, b2], [-2, 2])
    f4 = lax.ppermute(after(f3, state[0]), "z", up)
    state = attend(extent, queries, state, [f3, b3], [-3, 3])
    state = attend(extent, queries, state, [f4], [-4])

    received = lax.ppermute(pack_blocks(state, 2, 4), "c", shift(2, 1))
    *kept, send = merge_cores(state, received)
    last = lax.ppermute(send, "yh", shift(2, 1))
    return finish(kept, last, asker_vectors.shape)


def solution(mesh):
    fine = Mesh(mesh.devices.reshape(8, 2, 2, 4, 2), ("z", "yh", "yl", "x", "c"))
    ctx, head = ("z", "yh"), ("yl", "x", "c")
    return jax.shard_map(
        body,
        mesh=fine,
        in_specs=(
            P(ctx, head, None),
            P(ctx, None, None),
            P(ctx, None, None),
            P(ctx + head, None, None),
            P(),
            P(head),
        ),
        out_specs=P(ctx, head, None),
        check_vma=False,
    )
```

time: 212 us -> 182 us (0.86)
  blocking collectives: 20.8 us -> 0 us
  waiting for transfers between devices: 24.5 us -> 11.5 us
  Pallas kernels: 126 us -> 137 us
  starting transfers between devices: 34.4 us -> 28.3 us
    all_gather x1 -> x0, blocking collectives: 20.8 us -> none  [body(): cache = lax.all_gather(cache_own, 'z', axis=0, tiled=False)]
    pallas_call x6, Pallas kernels: 121 us -> 132 us  [the longest x5 132 us: attend(): pl.pallas_call(functools.partial(attend_kernel, shards, first), in_specs=...]
    ppermute x1, waiting for transfers between devices: 5.86 us -> 0.01 us  [body(): f1 = lax.ppermute(own, 'z', up)]
    ppermute x1, starting transfers between devices: 8.61 us -> 3.52 us  [body(): received = lax.ppermute(pack_blocks(state, 2, 4), 'c', shift(2, 1))]
    all_to_all x1, waiting for transfers between devices: 6.07 us -> 1.45 us  [body(): moved = lax.all_to_all(sending, ('yl', 'x'), 0, 0, tiled=True)]
    ppermute x6 -> x5, waiting for transfers between devices: 2.78 us -> 0.01 us  [the longest x1 0.01 us: body(): b3 = lax.ppermute(after(b2, state[0]), 'z', down)]
    ppermute x6 -> x5, starting transfers between devices: 7.6 us -> 5.56 us  [the longest x1 2.66 us: body(): b3 = lax.ppermute(after(b2, state[0]), 'z', down)]
    unnamed x10 -> x14, local copies, waits for them, and re-layouts: 2.66 us -> 4.25 us
  transfers between devices with their start and end apart: 14 -> 13, of which waited for: 5 -> 4; matrix products, arithmetic and copies ran while one was open for 2% -> 0% of each run, Pallas kernels for 49% -> 61%
where the time goes in v2:
time: 182 us
  Pallas kernels  137 us (75%)
  starting transfers between devices  28.3 us (16%)
  waiting for transfers between devices  11.5 us (6%)
  local copies, waits for them, and re-layouts  4.25 us (2%)
    pallas_call x5, Pallas kernels, attend(): pl.pallas_call(functools.partial(attend_kernel, shards, first), in_specs=...  132 us
    ppermute x1, waiting for transfers between devices, body(): last = lax.ppermute(send, 'yh', shift(2, 1))  8.17 us
    all_to_all x1, starting transfers between devices, body(): moved = lax.all_to_all(sending, ('yl', 'x'), 0, 0, tiled=True)  4.27 us
    unnamed x14, local copies, waits for them, and re-layouts  4.25 us
    ppermute x1, starting transfers between devices, body(): b1 = lax.ppermute(own, 'z', down)  4.03 us
    ppermute x1, starting transfers between devices, body(): q1 = lax.ppermute(q0, 'yh', shift(2, 1))  3.83 us
  transfers between devices with their start and end apart: 13, of which 4 were waited for; matrix products, arithmetic and copies ran while one was open for 0% of the time, Pallas kernels for 61%

profile of v2, /device:TPU:1, one launch (start us, length us, event | category | flops | bytes accessed | tf_op | source)
XLA Modules:
  0.0 181.7 jit_solution(7539183964992204681)
XLA Ops:
  0.0 0.0 copy-start
  0.0 0.0 copy-start.1
  0.0 1.0 copy-done.1
  1.0 0.0 copy-start.4
  1.0 0.7 copy-done.4
  1.7 1.7 documents.1
  3.4 0.9 copy-done.2
  4.3 0.7 copy-done.6
  5.0 1.0 queries.1
  6.0 3.8 %collective-permute-start = (bf16[144,1024]{1,0:T(8,128)(2,1)S(1)}, bf16[144,1024]{1,0:T(8,128)(2,1)S(1)}, u32[]{:S(2)}, u32[]{:S(2)}) collective-permute-start(bf16[144,1024]{1,0:T(8,128)(2,1)S(1)} %queries.1), channel_id=1, source_target_pairs={{0,16},{16,0},{1,17},{17,1},{2,18},{18,2},{3,19},{19,3},{4,20},{20... | collective-permute-start | bytes 884744 | tf_op jit(solution)/shard_map/ppermute | solution.py:384
  9.8 4.3 %all-to-all-start = ((bf16[8,2,64,128]{3,2,1,0:T(8,128)(2,1)}), bf16[8,2,64,128]{3,2,1,0:T(8,128)(2,1)S(1)}, u32[]{:S(2)}, u32[]{:S(2)}) async-start(bf16[8,2,64,128]{3,2,1,0:T(8,128)(2,1)} %documents.1), calls=%async_computation | async-start | bytes 524288 | tf_op jit(solution)/shard_map/all_to_all | solution.py:387
  14.1 1.2 collective-permute-start.1
  15.3 0.2 collective-permute-done
  15.5 2.5 %collective-permute-start.2 = (bf16[144,1024]{1,0:T(8,128)(2,1)S(1)}, bf16[144,1024]{1,0:T(8,128)(2,1)S(1)}, u32[]{:S(2)}, u32[]{:S(2)}) collective-permute-start(bf16[144,1024]{1,0:T(8,128)(2,1)S(1)} %collective-permute-done), channel_id=1, source_target_pairs={{0,1},{1,0},{2,3},{3,2},{4,5},{5,4},{6,7},{7,6},{8,9},{9,8},{10,11... | collective-permute-start | bytes 884744 | tf_op jit(solution)/shard_map/ppermute | solution.py:393
  18.0 0.0 copy-done
  18.0 0.9 copy-done.3
  18.9 0.2 caches.1
  19.1 1.5 all-to-all-done
  20.6 1.7 collective-permute-start.3
  22.3 4.0 %collective-permute-start.4 = (bf16[1344,128]{1,0:T(8,128)(2,1)S(1)}, bf16[1344,128]{1,0:T(8,128)(2,1)S(1)}, u32[]{:S(2)}, u32[]{:S(2)}) collective-permute-start(bf16[1344,128]{1,0:T(8,128)(2,1)S(1)} %pad_maximum_fusion.1.refs_2_), channel_id=1, source_target_pairs={{0,224},{32,0},{64,32},{96,64},{128,96},{160,128},{192,160},{224,1... | collective-permute-start | bytes 1032200 | tf_op jit(solution)/shard_map/ppermute | solution.py:392
  26.3 0.0 collective-permute-done.1
  26.3 0.0 collective-permute-done.2
  26.3 0.1 pad_maximum_fusion.refs_1_
  26.4 0.0 copy-done.5
  26.4 21.6 %attend.5 = (f32[1,4096]{1,0:T(1,128)S(1)}, f32[1,4096]{1,0:T(1,128)S(1)}, f32[128,4096]{1,0:T(8,128)S(1)}) custom-call(s32[64]{0:T(128)S(1)} %copy-done.5, bf16[144,4096]{1,0:T(8,128)(2,1)S(1)} %pad_maximum_fusion.refs_1_, bf16[1344,128]{1,0:T(8,128)(2,1)S(1)} %pad_maximum_fusion.1.refs_2_), custom_call_target="tpu_custom_call" | custom-call | tf_op jit(solution)/shard_map/attend/pallas_call | solution.py:278
  48.1 0.0 collective-permute-done.3.refs_5_
  48.1 0.1 collective-permute-start.5
  48.2 0.0 collective-permute-done.4.refs_6_
  48.2 2.7 %collective-permute-start.6 = (bf16[1344,128]{1,0:T(8,128)(2,1)S(1)}, bf16[1344,128]{1,0:T(8,128)(2,1)S(1)}, u32[]{:S(2)}, u32[]{:S(2)}) collective-permute-start(bf16[1344,128]{1,0:T(8,128)(2,1)S(1)} %collective-permute-done.4.refs_6_), channel_id=1, source_target_pairs={{0,224},{32,0},{64,32},{96,64},{128,96},{160,128},{192,160},{224,1... | collective-permute-start | bytes 1032200 | tf_op jit(solution)/shard_map/ppermute | solution.py:397
  50.8 29.9 %attend.6 = (f32[1,4096]{1,0:T(1,128)S(1)}, f32[1,4096]{1,0:T(1,128)S(1)}, f32[128,4096]{1,0:T(8,128)S(1)}) custom-call(s32[64]{0:T(128)S(1)} %copy-done.5, bf16[144,4096]{1,0:T(8,128)(2,1)S(1)} %pad_maximum_fusion.refs_1_, f32[1,4096]{1,0:T(1,128)S(1)} %get-tuple-element.31.refs_2_, f32[1,4096]{1,0:T(1,128)S(1)} %get-tuple-element.32.refs_3_, ...), custom_call_target="tpu_custom_call" | custom-call | tf_op jit(solution)/shard_map/attend/pallas_call | solution.py:278
  80.8 0.0 collective-permute-done.5.refs_5_
  80.8 0.1 collective-permute-start.7
  80.9 0.0 collective-permute-done.6.refs_6_
  80.9 2.7 %collective-permute-start.8 = (bf16[1344,128]{1,0:T(8,128)(2,1)S(1)}, bf16[1344,128]{1,0:T(8,128)(2,1)S(1)}, u32[]{:S(2)}, u32[]{:S(2)}) collective-permute-start(bf16[1344,128]{1,0:T(8,128)(2,1)S(1)} %collective-permute-done.6.refs_6_), channel_id=1, source_target_pairs={{0,224},{32,0},{64,32},{96,64},{128,96},{160,128},{192,160},{224,1... | collective-permute-start | bytes 1032200 | tf_op jit(solution)/shard_map/ppermute | solution.py:400
  83.5 29.9 %attend.7 = (f32[1,4096]{1,0:T(1,128)S(1)}, f32[1,4096]{1,0:T(1,128)S(1)}, f32[128,4096]{1,0:T(8,128)S(1)}) custom-call(s32[64]{0:T(128)S(1)} %copy-done.5, bf16[144,4096]{1,0:T(8,128)(2,1)S(1)} %pad_maximum_fusion.refs_1_, f32[1,4096]{1,0:T(1,128)S(1)} %get-tuple-element.34.refs_2_, f32[1,4096]{1,0:T(1,128)S(1)} %get-tuple-element.35.refs_3_, ...), custom_call_target="tpu_custom_call" | custom-call | tf_op jit(solution)/shard_map/attend/pallas_call | solution.py:278
  113.4 0.0 collective-permute-done.7.refs_5_
  113.4 0.1 collective-permute-start.9
  113.5 0.0 collective-permute-done.8.refs_6_
  113.5 29.9 %attend.8 = (f32[1,4096]{1,0:T(1,128)S(1)}, f32[1,4096]{1,0:T(1,128)S(1)}, f32[128,4096]{1,0:T(8,128)S(1)}) custom-call(s32[64]{0:T(128)S(1)} %copy-done.5, bf16[144,4096]{1,0:T(8,128)(2,1)S(1)} %pad_maximum_fusion.refs_1_, f32[1,4096]{1,0:T(1,128)S(1)} %get-tuple-element.39.refs_2_, f32[1,4096]{1,0:T(1,128)S(1)} %get-tuple-element.40.refs_3_, ...), custom_call_target="tpu_custom_call" | custom-call | tf_op jit(solution)/shard_map/attend/pallas_call | solution.py:278
  143.4 0.0 collective-permute-done.9.refs_5_
  143.5 20.8 %attend.9 = (f32[1,4096]{1,0:T(1,128)S(1)}, f32[1,4096]{1,0:T(1,128)S(1)}, f32[128,4096]{1,0:T(8,128)S(1)}) custom-call(s32[64]{0:T(128)S(1)} %copy-done.5, bf16[144,4096]{1,0:T(8,128)(2,1)S(1)} %pad_maximum_fusion.refs_1_, f32[1,4096]{1,0:T(1,128)S(1)} %get-tuple-element.44.refs_2_, f32[1,4096]{1,0:T(1,128)S(1)} %get-tuple-element.45.refs_3_, ...), custom_call_target="tpu_custom_call" | custom-call | tf_op jit(solution)/shard_map/attend/pallas_call | solution.py:278
  164.3 0.3 pack.1
  164.6 3.5 %collective-permute-start.10 = (bf16[144,2048]{1,0:T(8,128)(2,1)S(1)}, bf16[144,2048]{1,0:T(8,128)(2,1)S(1)}, u32[]{:S(2)}, u32[]{:S(2)}) collective-permute-start(bf16[144,2048]{1,0:T(8,128)(2,1)S(1)} %pack.1), channel_id=1, source_target_pairs={{0,1},{1,0},{2,3},{3,2},{4,5},{5,4},{6,7},{7,6},{8,9},{9,8},{10,11... | collective-permute-start | bytes 1769480 | tf_op jit(solution)/shard_map/ppermute | solution.py:406
  168.1 1.6 collective-permute-done.10.rec
  169.7 0.6 merge.1
  170.4 1.6 collective-permute-start.11
  172.0 8.2 %collective-permute-done.11.rec = bf16[144,1024]{1,0:T(8,128)(2,1)S(1)} collective-permute-done((bf16[144,1024]{1,0:T(8,128)(2,1)S(1)}, bf16[144,1024]{1,0:T(8,128)(2,1)S(1)}, u32[]{:S(2)}, u32[]{:S(2)}) %collective-permute-start.11) | collective-permute-done | bytes 294944 | tf_op jit(solution)/shard_map/ppermute | solution.py:408
  180.2 1.5 finish.1
  (5 shorter events, 0.0 us)
Async XLA Ops:
  0.0 18.0 %copy-start = (bf16[256,16,128]{2,1,0:T(8,128)(2,1)S(1)}, bf16[256,16,128]{2,1,0:T(8,128)(2,1)}, u32[]{:S(2)}) copy-start(bf16[256,16,128]{2,1,0:T(8,128)(2,1)} %asker_ref.1) | copy-start | bytes 3145732
  0.0 1.0 copy-start.1
  1.0 0.7 copy-start.4
  3.4 0.9 copy-start.2
  4.3 0.7 copy-start.6
  6.0 9.5 %collective-permute-start = (bf16[144,1024]{1,0:T(8,128)(2,1)S(1)}, bf16[144,1024]{1,0:T(8,128)(2,1)S(1)}, u32[]{:S(2)}, u32[]{:S(2)}) collective-permute-start(bf16[144,1024]{1,0:T(8,128)(2,1)S(1)} %queries.1), channel_id=1, source_target_pairs={{0,16},{16,0},{1,17},{17,1},{2,18},{18,2},{3,19},{19,3},{4,20},{20... | collective-permute-start | bytes 884744 | tf_op jit(solution)/shard_map/ppermute | solution.py:384
  9.8 16.6 %copy-start.5 = (s32[64]{0:T(128)S(1)}, s32[64]{0:T(128)}, u32[]{:S(2)}) copy-start(s32[64]{0:T(128)} %refs_0_.9) | copy-start | bytes 772
  9.8 10.8 %all-to-all-start = ((bf16[8,2,64,128]{3,2,1,0:T(8,128)(2,1)}), bf16[8,2,64,128]{3,2,1,0:T(8,128)(2,1)S(1)}, u32[]{:S(2)}, u32[]{:S(2)}) async-start(bf16[8,2,64,128]{3,2,1,0:T(8,128)(2,1)} %documents.1), calls=%async_computation | async-start | bytes 524288 | tf_op jit(solution)/shard_map/all_to_all | solution.py:387
  14.1 12.3 %collective-permute-start.1 = (bf16[144,1024]{1,0:T(8,128)(2,1)S(1)}, bf16[144,1024]{1,0:T(8,128)(2,1)S(1)}, u32[]{:S(2)}, u32[]{:S(2)}) collective-permute-start(bf16[144,1024]{1,0:T(8,128)(2,1)S(1)} %queries.1), channel_id=1, source_target_pairs={{0,1},{1,0},{2,3},{3,2},{4,5},{5,4},{6,7},{7,6},{8,9},{9,8},{10,11... | collective-permute-start | bytes 884744 | tf_op jit(solution)/shard_map/ppermute | solution.py:385
  15.5 10.9 %collective-permute-start.2 = (bf16[144,1024]{1,0:T(8,128)(2,1)S(1)}, bf16[144,1024]{1,0:T(8,128)(2,1)S(1)}, u32[]{:S(2)}, u32[]{:S(2)}) collective-permute-start(bf16[144,1024]{1,0:T(8,128)(2,1)S(1)} %collective-permute-done), channel_id=1, source_target_pairs={{0,1},{1,0},{2,3},{3,2},{4,5},{5,4},{6,7},{7,6},{8,9},{9,8},{10,11... | collective-permute-start | bytes 884744 | tf_op jit(solution)/shard_map/ppermute | solution.py:393
  18.0 1.0 copy-start.3
  20.6 27.5 %collective-permute-start.3 = (bf16[1344,128]{1,0:T(8,128)(2,1)S(1)}, bf16[1344,128]{1,0:T(8,128)(2,1)S(1)}, u32[]{:S(2)}, u32[]{:S(2)}) collective-permute-start(bf16[1344,128]{1,0:T(8,128)(2,1)S(1)} %pad_maximum_fusion.1.refs_2_), channel_id=1, source_target_pairs={{0,32},{32,64},{64,96},{96,128},{128,160},{160,192},{192,224},{224... | collective-permute-start | bytes 1032200 | tf_op jit(solution)/shard_map/ppermute | solution.py:391
  22.3 25.9 %collective-permute-start.4 = (bf16[1344,128]{1,0:T(8,128)(2,1)S(1)}, bf16[1344,128]{1,0:T(8,128)(2,1)S(1)}, u32[]{:S(2)}, u32[]{:S(2)}) collective-permute-start(bf16[1344,128]{1,0:T(8,128)(2,1)S(1)} %pad_maximum_fusion.1.refs_2_), channel_id=1, source_target_pairs={{0,224},{32,0},{64,32},{96,64},{128,96},{160,128},{192,160},{224,1... | collective-permute-start | bytes 1032200 | tf_op jit(solution)/shard_map/ppermute | solution.py:392
  48.1 32.7 %collective-permute-start.5 = (bf16[1344,128]{1,0:T(8,128)(2,1)S(1)}, bf16[1344,128]{1,0:T(8,128)(2,1)S(1)}, u32[]{:S(2)}, u32[]{:S(2)}) collective-permute-start(bf16[1344,128]{1,0:T(8,128)(2,1)S(1)} %collective-permute-done.3.refs_5_), channel_id=1, source_target_pairs={{0,32},{32,64},{64,96},{96,128},{128,160},{160,192},{192,224},{224... | collective-permute-start | bytes 1032200 | tf_op jit(solution)/shard_map/ppermute | solution.py:396
  48.2 32.7 %collective-permute-start.6 = (bf16[1344,128]{1,0:T(8,128)(2,1)S(1)}, bf16[1344,128]{1,0:T(8,128)(2,1)S(1)}, u32[]{:S(2)}, u32[]{:S(2)}) collective-permute-start(bf16[1344,128]{1,0:T(8,128)(2,1)S(1)} %collective-permute-done.4.refs_6_), channel_id=1, source_target_pairs={{0,224},{32,0},{64,32},{96,64},{128,96},{160,128},{192,160},{224,1... | collective-permute-start | bytes 1032200 | tf_op jit(solution)/shard_map/ppermute | solution.py:397
  80.8 32.7 %collective-permute-start.7 = (bf16[1344,128]{1,0:T(8,128)(2,1)S(1)}, bf16[1344,128]{1,0:T(8,128)(2,1)S(1)}, u32[]{:S(2)}, u32[]{:S(2)}) collective-permute-start(bf16[1344,128]{1,0:T(8,128)(2,1)S(1)} %collective-permute-done.5.refs_5_), channel_id=1, source_target_pairs={{0,32},{32,64},{64,96},{96,128},{128,160},{160,192},{192,224},{224... | collective-permute-start | bytes 1032200 | tf_op jit(solution)/shard_map/ppermute | solution.py:399
  80.9 32.7 %collective-permute-start.8 = (bf16[1344,128]{1,0:T(8,128)(2,1)S(1)}, bf16[1344,128]{1,0:T(8,128)(2,1)S(1)}, u32[]{:S(2)}, u32[]{:S(2)}) collective-permute-start(bf16[1344,128]{1,0:T(8,128)(2,1)S(1)} %collective-permute-done.6.refs_6_), channel_id=1, source_target_pairs={{0,224},{32,0},{64,32},{96,64},{128,96},{160,128},{192,160},{224,1... | collective-permute-start | bytes 1032200 | tf_op jit(solution)/shard_map/ppermute | solution.py:400
  113.4 30.0 %collective-permute-start.9 = (bf16[1344,128]{1,0:T(8,128)(2,1)S(1)}, bf16[1344,128]{1,0:T(8,128)(2,1)S(1)}, u32[]{:S(2)}, u32[]{:S(2)}) collective-permute-start(bf16[1344,128]{1,0:T(8,128)(2,1)S(1)} %collective-permute-done.7.refs_5_), channel_id=1, source_target_pairs={{0,32},{32,64},{64,96},{96,128},{128,160},{160,192},{192,224},{224... | collective-permute-start | bytes 1032200 | tf_op jit(solution)/shard_map/ppermute | solution.py:402
  164.6 5.2 %collective-permute-start.10 = (bf16[144,2048]{1,0:T(8,128)(2,1)S(1)}, bf16[144,2048]{1,0:T(8,128)(2,1)S(1)}, u32[]{:S(2)}, u32[]{:S(2)}) collective-permute-start(bf16[144,2048]{1,0:T(8,128)(2,1)S(1)} %pack.1), channel_id=1, source_target_pairs={{0,1},{1,0},{2,3},{3,2},{4,5},{5,4},{6,7},{7,6},{8,9},{9,8},{10,11... | collective-permute-start | bytes 1769480 | tf_op jit(solution)/shard_map/ppermute | solution.py:406
  170.4 9.8 %collective-permute-start.11 = (bf16[144,1024]{1,0:T(8,128)(2,1)S(1)}, bf16[144,1024]{1,0:T(8,128)(2,1)S(1)}, u32[]{:S(2)}, u32[]{:S(2)}) collective-permute-start(bf16[144,1024]{1,0:T(8,128)(2,1)S(1)} %get-tuple-element.54), channel_id=1, source_target_pairs={{0,16},{16,0},{1,17},{17,1},{2,18},{18,2},{3,19},{19,3},{4,20},{20... | collective-permute-start | bytes 884744 | tf_op jit(solution)/shard_map/ppermute | solution.py:408

commit v3 on v2

v3 whole, which is shorter than its diff:
```python
import functools
import math

import jax
import jax.numpy as jnp
from jax import lax
from jax.experimental import pallas as pl
from jax.experimental.pallas import tpu as pltpu
from jax.sharding import Mesh
from jax.sharding import PartitionSpec as P

F32 = jnp.float32
BF16 = jnp.bfloat16
KVH = 8
HD = 128
TILE = 256
RING = 8
SEND = 64
ROWS = 1024
BLOCKS = 4
AUX = 16
ASKED = 128
LED = 32
CACHE_ROWS = 2 * (ASKED + LED)
UNROLL = 2
SUB = 1024
MASKED = -1e30
HEADROOM = 100.0
LOG2E = math.log2(math.e)
SCALE2 = LOG2E / math.sqrt(HD)
VMEM_LIMIT = 24 * 2**20


def shift(count, step):
    return [(i, (i + step) % count) for i in range(count)]


def params():
    return pltpu.CompilerParams(vmem_limit_bytes=VMEM_LIMIT)


def whole(shape):
    return pl.BlockSpec(shape, lambda *_: (0,) * len(shape))


def after(x, *others):
    return lax.optimization_barrier((x, *others))[0]


def split3(x):
    hi = x.astype(BF16)
    rest = x - hi.astype(F32)
    mid = rest.astype(BF16)
    low = (rest - mid.astype(F32)).astype(BF16)
    return hi, mid, low


def join3(rows):
    r = rows.astype(F32)
    return r[0:1] + r[1:2] + r[2:3]


def aux_rows(x):
    hi, mid, low = split3(x)
    pad = jnp.zeros((AUX - 3, x.shape[1]), F32)
    parts = [hi.astype(F32), mid.astype(F32), low.astype(F32), pad]
    return jnp.concatenate(parts, axis=0).astype(BF16)


def live_counts(extent_ref, zpos, cpos):
    base = (2 * zpos + lax.axis_index("yh")) * 4
    start = cpos * SEND
    return [extent_ref[base + j // 2] - (j % 2) * 128 - start for j in range(KVH)]


def prepare(extent_hbm, soft_hbm, doc_hbm, q_hbm, doc_out, q_out, extent_ref, soft_ref, doc_ref, q_ref, sems):
    pairs = ((extent_hbm, extent_ref), (doc_hbm, doc_ref), (soft_hbm, soft_ref), (q_hbm, q_ref))
    copies = [pltpu.make_async_copy(src, dst, sems.at[i]) for i, (src, dst) in enumerate(pairs)]
    for copy in copies:
        copy.start()
    copies[0].wait()
    copies[1].wait()
    rows = doc_ref.shape[0]
    own = lax.axis_index("yl") * 4 + lax.axis_index("x")
    live = jnp.int32(0)
    for j, count in enumerate(live_counts(extent_ref, lax.axis_index("z"), lax.axis_index("c"))):
        live = jnp.where(own == j, count, live)
    keep = lax.broadcasted_iota(jnp.int32, (rows, HD), 0) < live
    for g in range(KVH):
        for s in range(2):
            doc_out[g, s] = jnp.where(keep, doc_ref[:, 2 * g + s, :].astype(F32), 0.0).astype(BF16)
    copies[2].wait()
    copies[3].wait()
    tokens, heads, _ = q_ref.shape
    for h in range(heads):
        cols = slice(h * tokens, (h + 1) * tokens)
        q_out[:HD, cols] = q_ref[:, h, :].astype(F32).T.astype(BF16)
        factor = jnp.full((1, tokens), 1.0, F32) / soft_ref[h] * SCALE2
        q_out[HD:, cols] = aux_rows(factor)


def prepared(extent, softening_factor, document_memory_pairs, asker_vectors):
    rows = document_memory_pairs.shape[0]
    tokens, heads, _ = asker_vectors.shape
    vmem = pl.BlockSpec(memory_space=pltpu.VMEM)
    return pl.pallas_call(
        prepare,
        in_specs=[pl.BlockSpec(memory_space=pltpu.HBM)] * 4,
        out_specs=[vmem, vmem],
        out_shape=[
            jax.ShapeDtypeStruct((KVH, 2, rows, HD), BF16),
            jax.ShapeDtypeStruct((HD + AUX, tokens * heads), BF16),
        ],
        scratch_shapes=[
            pltpu.SMEM(extent.shape, jnp.int32),
            pltpu.SMEM(softening_factor.shape, F32),
            pltpu.VMEM(document_memory_pairs.shape, BF16),
            pltpu.VMEM(asker_vectors.shape, BF16),
            pltpu.SemaphoreType.DMA((4,)),
        ],
        compiler_params=params(),
        name="prepare",
    )(*[pltpu.with_memory_space_constraint(x, pltpu.HBM) for x in (extent, softening_factor, document_memory_pairs, asker_vectors)])


def prepare_caches(asker_ref, lead_ref, out_ref):
    own = lax.axis_index("yl") * 4 + lax.axis_index("x")
    c = lax.axis_index("c")
    half, lead = asker_ref.shape[0] // 2, lead_ref.shape[0] // 2
    mine = pl.ds(pl.multiple_of(c * half, half), half)
    led = pl.ds(pl.multiple_of(c * lead, lead), lead)
    for g in range(KVH):

        @pl.when(own == g)
        def _():
            for s in range(2):
                out_ref[s * half : (s + 1) * half, :] = asker_ref[mine, 2 * g + s, :]
                at = 2 * half + s * lead
                out_ref[at : at + lead, :] = lead_ref[led, 2 * g + s, :]


def cache_block(asker_memory_pairs, leading_memory_pairs):
    return pl.pallas_call(
        prepare_caches,
        out_shape=jax.ShapeDtypeStruct((CACHE_ROWS, HD), BF16),
        compiler_params=params(),
        name="caches",
    )(asker_memory_pairs, leading_memory_pairs)


def attend_kernel(shards, mode, q_low, *refs):
    refs = list(refs)
    extent_ref = refs.pop(0)
    first = mode == "first"
    count = len(shards)
    if first:
        parts = refs[:BLOCKS]
        pay = refs[BLOCKS : BLOCKS + count]
        m_out, l_out, acc_out, q_ref, k_ref, v_ref, m0, l0, acc0 = refs[BLOCKS + count :]
        for n, part in enumerate(parts):
            q_ref[:, n * ROWS : (n + 1) * ROWS] = part[...]
    else:
        q_ref, m0, l0, acc0 = refs[:4]
        pay = refs[4 : 4 + count]
        refs = refs[4 + count :]
        if mode in ("middle", "part"):
            m_out, l_out, acc_out, k_ref, v_ref = refs
        elif mode == "pack":
            m_out, l_out, acc_out, packed_ref, k_ref, v_ref = refs
        else:
            rec_ref, m_end, l_end, acc_end, k_ref, v_ref, m_out, l_out, acc_out = refs
    width = m_out.shape[1]
    zpos, ypos, cpos = lax.axis_index("z"), lax.axis_index("yh"), lax.axis_index("c")
    span = KVH * SEND
    asked_at = count * span
    led_at = asked_at + count * ASKED

    values, asked, led, alive, asked_alive = [], [], [], [], []
    for n, (ref, (away, swapped)) in enumerate(zip(pay, shards)):
        counts = live_counts(extent_ref, (zpos + away) % RING, 1 - cpos if swapped else cpos)
        lane = lax.broadcasted_iota(jnp.int32, (AUX, span), 1)
        bound = jnp.zeros((AUX, span), jnp.int32)
        for j in range(KVH):
            bound = jnp.where(lane // SEND == j, counts[j], bound)
            at = n * span + j * SEND
            k_ref[at : at + SEND, :] = ref[2 * j * SEND : (2 * j + 1) * SEND, :]
            values.append(ref[(2 * j + 1) * SEND : (2 * j + 2) * SEND, :])
        alive.append(jnp.where(lane % SEND < bound, 1.0, 0.0))
        at = 2 * span
        keys = ref[at : at + ASKED, :]
        vals = ref[at + ASKED : at + 2 * ASKED, :]
        if away == 0:
            asked_alive.append(jnp.ones((AUX, ASKED), F32))
        else:
            seen = (zpos + away >= 0) if away < 0 else (zpos + away >= RING)
            flag = jnp.where(seen, 1.0, 0.0).astype(F32)
            keys = (keys.astype(F32) * flag).astype(BF16)
            vals = (vals.astype(F32) * flag).astype(BF16)
            asked_alive.append(jnp.full((AUX, ASKED), 1.0, F32) * flag)
        k_ref[asked_at + n * ASKED : asked_at + (n + 1) * ASKED, :] = keys
        asked.append(vals)
        at += 2 * ASKED
        k_ref[led_at + n * LED : led_at + (n + 1) * LED, :] = ref[at : at + LED, :]
        led.append(ref[at + LED : at + 2 * LED, :])
    stacked = jnp.concatenate(values + asked + led, axis=0).astype(F32)
    v_ref[:HD, :] = stacked.T.astype(BF16)
    ones = [jnp.ones((AUX, count * LED), F32)]
    v_ref[HD:, :] = jnp.concatenate(alive + asked_alive + ones, axis=1).astype(BF16)

    if first:
        for i in range(width // SUB):
            cols = slice(i * SUB, (i + 1) * SUB)
            s = jnp.dot(k_ref[led_at:, :], q_ref[:HD, q_low + i * SUB : q_low + (i + 1) * SUB], preferred_element_type=F32) * SCALE2
            m0[:, cols] = jnp.max(s, axis=0, keepdims=True)
        l0[...] = jnp.zeros_like(l0)
        acc0[...] = jnp.zeros_like(acc0)

    def scores(start, size):
        cols = pl.ds(pl.multiple_of(start + q_low, 128), size)
        s = jnp.dot(k_ref[...], q_ref[:HD, cols], preferred_element_type=F32)
        factor = join3(q_ref[HD : HD + 3, cols])
        rest = s[asked_at:] * SCALE2
        if first:
            token = (lax.broadcasted_iota(jnp.int32, (1, size), 1) + start) % TILE
            yrow = jnp.where(start + q_low < 2 * ROWS, ypos, 1 - ypos)
            query = yrow * TILE + token
            key = ypos * TILE + cpos * ASKED + lax.broadcasted_iota(jnp.int32, (ASKED, 1), 0)
            near = jnp.where(key <= query, rest[:ASKED], MASKED)
            rest = jnp.concatenate([near, rest[ASKED:]], axis=0)
        return jnp.concatenate([s[:asked_at] * factor, rest], axis=0)

    def lazy(i, excess):
        start = pl.multiple_of(i * SUB, SUB)
        cols = pl.ds(start, SUB)
        old = pl.ds(pl.multiple_of(start + q_low, 128), SUB)
        s = scores(start, SUB)
        base = m0[:, old]
        excess = jnp.maximum(excess, jnp.max(s, axis=0, keepdims=True) - base)
        p = jnp.exp2(s - base).astype(BF16)
        o = jnp.dot(v_ref[...], p, preferred_element_type=F32)
        m_out[:, cols] = base
        l_out[:, cols] = l0[:, old] + o[HD : HD + 1]
        acc_out[:, cols] = acc0[:, old] + o[:HD]
        return excess

    excess = lax.fori_loop(0, width // SUB, lazy, jnp.full((1, SUB), MASKED, F32), unroll=min(UNROLL, width // SUB))

    @pl.when(jnp.max(excess) > HEADROOM)
    def _():
        total = k_ref.shape[0]
        living = jnp.broadcast_to(v_ref[HD : HD + 1, :].astype(F32), (128, total)).T

        def exact(i, carry):
            start = pl.multiple_of(i * 128, 128)
            cols = pl.ds(start, 128)
            old = pl.ds(pl.multiple_of(start + q_low, 128), 128)
            s = jnp.where(living > 0.5, scores(start, 128), MASKED)
            base = m0[:, old]
            peak = jnp.maximum(base, jnp.max(s, axis=0, keepdims=True))
            shrink = jnp.exp2(base - peak)
            p = jnp.exp2(s - peak).astype(BF16)
            o = jnp.dot(v_ref[...], p, preferred_element_type=F32)
            m_out[:, cols] = peak
            l_out[:, cols] = l0[:, old] * shrink + o[HD : HD + 1]
            acc_out[:, cols] = acc0[:, old] * shrink + o[:HD]
            return carry

        lax.fori_loop(0, width // 128, exact, 0)

    if mode == "pack":
        for n in range(2):
            cols = slice((2 * n + 1) * ROWS, (2 * n + 2) * ROWS)
            packed_ref[:, n * ROWS : (n + 1) * ROWS] = pack(m_out[:, cols], l_out[:, cols], acc_out[:, cols])
    if mode == "keep":
        m_end[...], l_end[...], acc_end[...] = fold(*normal(m_out[...], l_out[...], acc_out[...]), rec_ref[:, :ROWS])


def state_shapes(width):
    return [
        jax.ShapeDtypeStruct((1, width), F32),
        jax.ShapeDtypeStruct((1, width), F32),
        jax.ShapeDtypeStruct((HD, width), F32),
    ]


def attend(extent, queries, state, pays, shards, mode, received=None, q_low=0):
    keys = len(shards) * (KVH * SEND + ASKED + LED)
    width = ROWS if mode in ("part", "keep") else BLOCKS * ROWS
    scratch = [pltpu.VMEM((keys, HD), BF16), pltpu.VMEM((HD + AUX, keys), BF16)]
    floats = [pltpu.VMEM((1, width), F32), pltpu.VMEM((1, width), F32), pltpu.VMEM((HD, width), F32)]
    shapes = state_shapes(width)
    if mode == "first":
        args = [extent, *queries, *pays]
        shapes.append(jax.ShapeDtypeStruct((HD + AUX, width), BF16))
        scratch += floats
    else:
        args = [extent, queries, *state, *pays]
    if mode == "pack":
        shapes.append(jax.ShapeDtypeStruct((HD + AUX, 2 * ROWS), BF16))
    if mode == "keep":
        args.append(received)
        scratch += floats
    vmem = pl.BlockSpec(memory_space=pltpu.VMEM)
    return pl.pallas_call(
        functools.partial(attend_kernel, shards, mode, q_low),
        in_specs=[pl.BlockSpec(memory_space=pltpu.SMEM)] + [vmem] * (len(args) - 1),
        out_specs=[vmem] * len(shapes),
        out_shape=shapes,
        scratch_shapes=scratch,
        compiler_params=params(),
        name="attend",
    )(*args)


def pack(m, l, acc):
    total = m + jnp.log2(l)
    return jnp.concatenate([(acc / l).astype(BF16), aux_rows(total)], axis=0)


def fold(m, l, acc, received):
    other = join3(received[HD : HD + 3])
    peak = jnp.maximum(m, other)
    mine = jnp.exp2(m - peak)
    theirs = jnp.exp2(other - peak)
    return peak, l * mine + theirs, acc * mine + received[:HD].astype(F32) * theirs


def normal(m, l, acc):
    total = m + jnp.log2(l)
    return total, jnp.ones_like(total), acc / l


def merge_kernel(m, l, acc, rec, send_ref):
    send_ref[...] = pack(*fold(*normal(m[...], l[...], acc[...]), rec[:, ROWS:]))


def merge_cores(state, received):
    return pl.pallas_call(
        merge_kernel,
        out_shape=jax.ShapeDtypeStruct((HD + AUX, ROWS), BF16),
        compiler_params=params(),
        name="merge",
    )(*state, received)


def finish_kernel(m, l, acc, far, out_ref):
    _, total, summed = fold(m[...], l[...], acc[...], far[...])
    result = summed / total
    tokens, heads, _ = out_ref.shape
    for h in range(heads):
        out_ref[:, h, :] = result[:, h * tokens : (h + 1) * tokens].T.astype(BF16)


def finish(state, far, shape):
    return pl.pallas_call(
        finish_kernel,
        out_shape=jax.ShapeDtypeStruct(shape, BF16),
        compiler_params=params(),
        name="finish",
    )(*state, far)


def body(
    asker_vectors,
    asker_memory_pairs,
    leading_memory_pairs,
    document_memory_pairs,
    document_valid_extent,
    softening_factor,
):
    extent = document_valid_extent
    sending, q0 = prepared(extent, softening_factor, document_memory_pairs, asker_vectors)
    q1 = lax.ppermute(q0, "yh", shift(2, 1))
    q2 = lax.ppermute(q0, "c", shift(2, 1))
    moved = lax.all_to_all(sending, ("yl", "x"), 0, 0, tiled=True)
    cache = cache_block(after(asker_memory_pairs, q0), leading_memory_pairs)
    q3 = lax.ppermute(q1, "c", shift(2, 1))
    own = jnp.concatenate([moved.reshape(-1, HD), cache], axis=0)

    up, down = shift(RING, 1), shift(RING, -1)
    f1 = lax.ppermute(own, "z", up)
    b1 = lax.ppermute(own, "z", down)
    q0, q2, q1, q3 = lax.optimization_barrier((q0, q2, q1, q3))
    *state, queries = attend(extent, [q0, q2, q1, q3], None, [own], [(0, False)], "first")
    f2 = lax.ppermute(after(f1, state[0]), "z", up)
    b2 = lax.ppermute(after(b1, state[0]), "z", down)
    state = attend(extent, queries, state, [f1, b1], [(-1, False), (1, False)], "middle")
    f3 = lax.ppermute(after(f2, state[0]), "z", up)
    b3 = lax.ppermute(after(b2, state[0]), "z", down)
    state = attend(extent, queries, state, [f2, b2], [(-2, False), (2, False)], "middle")
    f4 = lax.ppermute(after(f3, state[0]), "z", up)
    cross = [(2 * z + c, 2 * ((z - 1) % RING) + 1 - c) for z in range(RING) for c in range(2)]
    b4 = lax.ppermute(after(b3, state[0]), ("z", "c"), cross)
    *state, packed = attend(extent, queries, state, [f3, b3], [(-3, False), (3, False)], "pack")
    received = lax.ppermute(after(packed, f4, b4), "c", shift(2, 1))
    rest = [(-4, False), (-4, True)]
    apart = attend(extent, queries, state, [f4, b4], rest, "part", None, 2 * ROWS)
    send = merge_cores(apart, received)
    far = lax.ppermute(send, "yh", shift(2, 1))
    kept = attend(extent, queries, state, [after(f4, send), b4], rest, "keep", received, 0)
    return finish(kept, far, asker_vectors.shape)


def solution(mesh):
    fine = Mesh(mesh.devices.reshape(8, 2, 2, 4, 2), ("z", "yh", "yl", "x", "c"))
    ctx, head = ("z", "yh"), ("yl", "x", "c")
    return jax.shard_map(
        body,
        mesh=fine,
        in_specs=(
            P(ctx, head, None),
            P(ctx, None, None),
            P(ctx, None, None),
            P(ctx + head, None, None),
            P(),
            P(head),
        ),
        out_specs=P(ctx, head, None),
        check_vma=False,
    )
```

time: 182 us -> 166 us (0.912)
  waiting for transfers between devices: 11.5 us -> 3.12 us
  Pallas kernels: 137 us -> 130 us
  local copies, waits for them, and re-layouts: 4.25 us -> 2.18 us
    ppermute x2 -> x3, waiting for transfers between devices: 9.8 us -> 0.01 us  [the longest x1 0.01 us: body(): b4 = lax.ppermute(after(b3, state[0]), ('z', 'c'), cross)]
    pallas_call x9 -> x8, Pallas kernels: 136 us -> 129 us  [the longest x6 126 us: attend(): pl.pallas_call(functools.partial(attend_kernel, shards, mode, q_low), in_...]
    ppermute x1, starting transfers between devices: 2.51 us -> 0.01 us  [body(): q3 = lax.ppermute(q1, 'c', shift(2, 1))]
    unnamed x14 -> x6, local copies, waits for them, and re-layouts: 4.25 us -> 2.18 us
    ppermute x2 -> x3, starting transfers between devices: 5.16 us -> 6.15 us  [the longest x1 4.03 us: body(): b4 = lax.ppermute(after(b3, state[0]), ('z', 'c'), cross)]
  transfers between devices with their start and end apart: 13 -> 14, of which waited for: 4 -> 3; matrix products, arithmetic and copies ran while one was open for 0% -> 0% of each run, Pallas kernels for 61% -> 76%
where the time goes in v3:
time: 166 us
  Pallas kernels  130 us (78%)
  starting transfers between devices  29.9 us (18%)
  waiting for transfers between devices  3.12 us (2%)
  local copies, waits for them, and re-layouts  2.18 us (1%)
    pallas_call x6, Pallas kernels, attend(): pl.pallas_call(functools.partial(attend_kernel, shards, mode, q_low), in_...  126 us
    all_to_all x1, starting transfers between devices, body(): moved = lax.all_to_all(sending, ('yl', 'x'), 0, 0, tiled=True)  5.87 us
    ppermute x1, starting transfers between devices, body(): b2 = lax.ppermute(after(b1, state[0]), 'z', down)  4.04 us
    ppermute x1, starting transfers between devices, body(): b4 = lax.ppermute(after(b3, state[0]), ('z', 'c'), cross)  4.03 us
    ppermute x1, starting transfers between devices, body(): b1 = lax.ppermute(own, 'z', down)  4.03 us
  transfers between devices with their start and end apart: 14, of which 3 were waited for; matrix products, arithmetic and copies ran while one was open for 0% of the time, Pallas kernels for 76%

profile of v3, /device:TPU:1, one launch (start us, length us, event | category | flops | bytes accessed | tf_op | source)
XLA Modules:
  0.0 165.6 jit_solution(13152575310957885499)
XLA Ops:
  0.0 0.0 copy-start.2
  0.0 2.0 %prepare.1 = (bf16[8,2,64,128]{3,2,1,0:T(8,128)(2,1)}, bf16[144,1024]{1,0:T(8,128)(2,1)S(1)}) custom-call(s32[64]{0:T(128)} %refs_0_.11, f32[4]{0:T(128)} %soft_hbm.1, bf16[64,16,128]{2,1,0:T(8,128)(2,1)} %doc_hbm.1, bf16[256,4,128]{2,1,0:T(4,128)(2,1)} %q_hbm.1), custom_call_target="tpu_custom_call" | custom-call | tf_op jit(solution)/shard_map/prepare/pallas_call | solution.py:106
  2.1 5.9 %all-to-all-start = ((bf16[8,2,64,128]{3,2,1,0:T(8,128)(2,1)}), bf16[8,2,64,128]{3,2,1,0:T(8,128)(2,1)S(1)}, u32[]{:S(2)}, u32[]{:S(2)}) async-start(bf16[8,2,64,128]{3,2,1,0:T(8,128)(2,1)} %get-tuple-element.45), calls=%async_computation | async-start | bytes 524288 | tf_op jit(solution)/shard_map/all_to_all | solution.py:375
  7.9 2.6 %collective-permute-start.1 = (bf16[144,1024]{1,0:T(8,128)(2,1)S(1)}, bf16[144,1024]{1,0:T(8,128)(2,1)S(1)}, u32[]{:S(2)}, u32[]{:S(2)}) collective-permute-start(bf16[144,1024]{1,0:T(8,128)(2,1)S(1)} %get-tuple-element.41.refs_1_), channel_id=1, source_target_pairs={{0,16},{16,0},{1,17},{17,1},{2,18},{18,2},{3,19},{19,3},{4,20},{20... | collective-permute-start | bytes 884744 | tf_op jit(solution)/shard_map/ppermute | solution.py:373
  10.6 0.0 copy-start
  10.6 1.2 copy-done
  11.8 0.0 copy-start.1
  11.8 0.9 copy-done.1
  12.7 0.2 caches.1
  12.9 1.5 all-to-all-done
  14.4 1.7 %collective-permute-start.3 = (bf16[1344,128]{1,0:T(8,128)(2,1)S(1)}, bf16[1344,128]{1,0:T(8,128)(2,1)S(1)}, u32[]{:S(2)}, u32[]{:S(2)}) collective-permute-start(bf16[1344,128]{1,0:T(8,128)(2,1)S(1)} %pad_maximum_fusion.refs_5_), channel_id=1, source_target_pairs={{0,32},{32,64},{64,96},{96,128},{128,160},{160,192},{192,224},{224... | collective-permute-start | bytes 1032200 | tf_op jit(solution)/shard_map/ppermute | solution.py:381
  16.1 4.0 %collective-permute-start.4 = (bf16[1344,128]{1,0:T(8,128)(2,1)S(1)}, bf16[1344,128]{1,0:T(8,128)(2,1)S(1)}, u32[]{:S(2)}, u32[]{:S(2)}) collective-permute-start(bf16[1344,128]{1,0:T(8,128)(2,1)S(1)} %pad_maximum_fusion.refs_5_), channel_id=1, source_target_pairs={{0,224},{32,0},{64,32},{96,64},{128,96},{160,128},{192,160},{224,1... | collective-permute-start | bytes 1032200 | tf_op jit(solution)/shard_map/ppermute | solution.py:382
  20.1 2.2 %collective-permute-start = (bf16[144,1024]{1,0:T(8,128)(2,1)S(1)}, bf16[144,1024]{1,0:T(8,128)(2,1)S(1)}, u32[]{:S(2)}, u32[]{:S(2)}) collective-permute-start(bf16[144,1024]{1,0:T(8,128)(2,1)S(1)} %get-tuple-element.41.refs_1_), channel_id=1, source_target_pairs={{0,1},{1,0},{2,3},{3,2},{4,5},{5,4},{6,7},{7,6},{8,9},{9,8},{10,11... | collective-permute-start | bytes 884744 | tf_op jit(solution)/shard_map/ppermute | solution.py:374
  22.3 0.0 collective-permute-done.1.refs_3_
  22.3 0.0 collective-permute-start.2
  22.3 1.2 collective-permute-done.refs_2_
  23.5 0.4 collective-permute-done.2.refs_4_
  23.9 0.0 copy-done.2
  23.9 20.9 %attend.6 = (f32[1,4096]{1,0:T(1,128)S(1)}, f32[1,4096]{1,0:T(1,128)S(1)}, f32[128,4096]{1,0:T(8,128)S(1)}, bf16[144,4096]{1,0:T(8,128)(2,1)S(1)}) custom-call(s32[64]{0:T(128)S(1)} %copy-done.2, bf16[144,1024]{1,0:T(8,128)(2,1)S(1)} %get-tuple-element.41.refs_1_, bf16[144,1024]{1,0:T(8,128)(2,1)S(1)} %collective-permute-done.refs_2_, ...), custom_call_target="tpu_custom_call" | custom-call | tf_op jit(solution)/shard_map/attend/pallas_call | solution.py:304
  44.8 0.0 collective-permute-done.3.refs_5_
  44.8 0.5 collective-permute-start.5
  45.3 0.0 collective-permute-done.4.refs_6_
  45.3 4.0 %collective-permute-start.6 = (bf16[1344,128]{1,0:T(8,128)(2,1)S(1)}, bf16[1344,128]{1,0:T(8,128)(2,1)S(1)}, u32[]{:S(2)}, u32[]{:S(2)}) collective-permute-start(bf16[1344,128]{1,0:T(8,128)(2,1)S(1)} %collective-permute-done.4.refs_6_), channel_id=1, source_target_pairs={{0,224},{32,0},{64,32},{96,64},{128,96},{160,128},{192,160},{224,1... | collective-permute-start | bytes 1032200 | tf_op jit(solution)/shard_map/ppermute | solution.py:386
  49.4 29.8 %attend.7 = (f32[1,4096]{1,0:T(1,128)S(1)}, f32[1,4096]{1,0:T(1,128)S(1)}, f32[128,4096]{1,0:T(8,128)S(1)}) custom-call(s32[64]{0:T(128)S(1)} %copy-done.2, bf16[144,4096]{1,0:T(8,128)(2,1)S(1)} %get-tuple-element.47.refs_1_, f32[1,4096]{1,0:T(1,128)S(1)} %get-tuple-element.48.refs_2_, f32[1,4096]{1,0:T(1,128)S(1)} %get-tuple-element.49.refs_3_, ...), custom_call_target="tpu_custom_call" | custom-call | tf_op jit(solution)/shard_map/attend/pallas_call | solution.py:304
  79.1 0.0 collective-permute-done.5.refs_5_
  79.2 0.1 collective-permute-start.7
  79.2 0.0 collective-permute-done.6.refs_6_
  79.3 2.7 %collective-permute-start.8 = (bf16[1344,128]{1,0:T(8,128)(2,1)S(1)}, bf16[1344,128]{1,0:T(8,128)(2,1)S(1)}, u32[]{:S(2)}, u32[]{:S(2)}) collective-permute-start(bf16[1344,128]{1,0:T(8,128)(2,1)S(1)} %collective-permute-done.6.refs_6_), channel_id=1, source_target_pairs={{0,224},{32,0},{64,32},{96,64},{128,96},{160,128},{192,160},{224,1... | collective-permute-start | bytes 1032200 | tf_op jit(solution)/shard_map/ppermute | solution.py:389
  81.9 29.6 %attend.8 = (f32[1,4096]{1,0:T(1,128)S(1)}, f32[1,4096]{1,0:T(1,128)S(1)}, f32[128,4096]{1,0:T(8,128)S(1)}) custom-call(s32[64]{0:T(128)S(1)} %copy-done.2, bf16[144,4096]{1,0:T(8,128)(2,1)S(1)} %get-tuple-element.47.refs_1_, f32[1,4096]{1,0:T(1,128)S(1)} %get-tuple-element.51.refs_2_, f32[1,4096]{1,0:T(1,128)S(1)} %get-tuple-element.52.refs_3_, ...), custom_call_target="tpu_custom_call" | custom-call | tf_op jit(solution)/shard_map/attend/pallas_call | solution.py:304
  111.5 0.0 collective-permute-done.7.refs_5_
  111.5 0.1 collective-permute-start.9
  111.6 0.0 collective-permute-done.8.refs_6_
  111.6 4.0 %collective-permute-start.10 = (bf16[1344,128]{1,0:T(8,128)(2,1)S(1)}, bf16[1344,128]{1,0:T(8,128)(2,1)S(1)}, u32[]{:S(2)}, u32[]{:S(2)}) collective-permute-start(bf16[1344,128]{1,0:T(8,128)(2,1)S(1)} %collective-permute-done.8.refs_6_), channel_id=1, source_target_pairs={{0,225},{1,224},{32,1},{33,0},{64,33},{65,32},{96,65},{97,64},{128... | collective-permute-start | bytes 1032200 | tf_op jit(solution)/shard_map/ppermute | solution.py:393
  115.6 29.7 %attend.9 = (f32[1,4096]{1,0:T(1,128)S(1)}, f32[1,4096]{1,0:T(1,128)S(1)}, f32[128,4096]{1,0:T(8,128)S(1)}, bf16[144,2048]{1,0:T(8,128)(2,1)S(1)}) custom-call(s32[64]{0:T(128)S(1)} %copy-done.2, bf16[144,4096]{1,0:T(8,128)(2,1)S(1)} %get-tuple-element.47.refs_1_, f32[1,4096]{1,0:T(1,128)S(1)} %get-tuple-element.56.refs_2_, ...), custom_call_target="tpu_custom_call" | custom-call | tf_op jit(solution)/shard_map/attend/pallas_call | solution.py:304
  145.3 0.0 collective-permute-done.9.refs_5_
  145.3 0.0 collective-permute-done.10.refs_6_
  145.3 0.3 collective-permute-start.11
  145.6 8.2 %attend.10 = (f32[1,1024]{1,0:T(1,128)S(1)}, f32[1,1024]{1,0:T(1,128)S(1)}, f32[128,1024]{1,0:T(8,128)S(1)}) custom-call(s32[64]{0:T(128)S(1)} %copy-done.2, bf16[144,4096]{1,0:T(8,128)(2,1)S(1)} %get-tuple-element.47.refs_1_, f32[1,4096]{1,0:T(1,128)S(1)} %get-tuple-element.61.refs_2_, f32[1,4096]{1,0:T(1,128)S(1)} %get-tuple-element.62.refs_3_, ...), custom_call_target="tpu_custom_call" | custom-call | tf_op jit(solution)/shard_map/attend/pallas_call | solution.py:304
  153.8 0.0 collective-permute-done.11.rec.refs_7_
  153.8 0.2 merge.1
  154.0 1.8 %collective-permute-start.12 = (bf16[144,1024]{1,0:T(8,128)(2,1)S(1)}, bf16[144,1024]{1,0:T(8,128)(2,1)S(1)}, u32[]{:S(2)}, u32[]{:S(2)}) collective-permute-start(bf16[144,1024]{1,0:T(8,128)(2,1)S(1)} %merge.1), channel_id=1, source_target_pairs={{0,16},{16,0},{1,17},{17,1},{2,18},{18,2},{3,19},{19,3},{4,20},{20... | collective-permute-start | bytes 884744 | tf_op jit(solution)/shard_map/ppermute | solution.py:399
  155.8 8.3 %attend.11 = (f32[1,1024]{1,0:T(1,128)S(1)}, f32[1,1024]{1,0:T(1,128)S(1)}, f32[128,1024]{1,0:T(8,128)S(1)}) custom-call(s32[64]{0:T(128)S(1)} %copy-done.2, bf16[144,4096]{1,0:T(8,128)(2,1)S(1)} %get-tuple-element.47.refs_1_, f32[1,4096]{1,0:T(1,128)S(1)} %get-tuple-element.61.refs_2_, f32[1,4096]{1,0:T(1,128)S(1)} %get-tuple-element.62.refs_3_, ...), custom_call_target="tpu_custom_call" | custom-call | tf_op jit(solution)/shard_map/attend/pallas_call | solution.py:304
  164.1 0.0 collective-permute-done.12.far
  164.1 1.5 finish.1
  (1 shorter events, 0.0 us)
Async XLA Ops:
  0.0 23.9 %copy-start.2 = (s32[64]{0:T(128)S(1)}, s32[64]{0:T(128)}, u32[]{:S(2)}) copy-start(s32[64]{0:T(128)} %refs_0_.11) | copy-start | bytes 772
  2.1 12.3 %all-to-all-start = ((bf16[8,2,64,128]{3,2,1,0:T(8,128)(2,1)}), bf16[8,2,64,128]{3,2,1,0:T(8,128)(2,1)S(1)}, u32[]{:S(2)}, u32[]{:S(2)}) async-start(bf16[8,2,64,128]{3,2,1,0:T(8,128)(2,1)} %get-tuple-element.45), calls=%async_computation | async-start | bytes 524288 | tf_op jit(solution)/shard_map/all_to_all | solution.py:375
  7.9 14.4 %collective-permute-start.1 = (bf16[144,1024]{1,0:T(8,128)(2,1)S(1)}, bf16[144,1024]{1,0:T(8,128)(2,1)S(1)}, u32[]{:S(2)}, u32[]{:S(2)}) collective-permute-start(bf16[144,1024]{1,0:T(8,128)(2,1)S(1)} %get-tuple-element.41.refs_1_), channel_id=1, source_target_pairs={{0,16},{16,0},{1,17},{17,1},{2,18},{18,2},{3,19},{19,3},{4,20},{20... | collective-permute-start | bytes 884744 | tf_op jit(solution)/shard_map/ppermute | solution.py:373
  10.6 1.2 copy-start
  11.8 0.9 copy-start.1
  14.4 30.4 %collective-permute-start.3 = (bf16[1344,128]{1,0:T(8,128)(2,1)S(1)}, bf16[1344,128]{1,0:T(8,128)(2,1)S(1)}, u32[]{:S(2)}, u32[]{:S(2)}) collective-permute-start(bf16[1344,128]{1,0:T(8,128)(2,1)S(1)} %pad_maximum_fusion.refs_5_), channel_id=1, source_target_pairs={{0,32},{32,64},{64,96},{96,128},{128,160},{160,192},{192,224},{224... | collective-permute-start | bytes 1032200 | tf_op jit(solution)/shard_map/ppermute | solution.py:381
  16.1 29.2 %collective-permute-start.4 = (bf16[1344,128]{1,0:T(8,128)(2,1)S(1)}, bf16[1344,128]{1,0:T(8,128)(2,1)S(1)}, u32[]{:S(2)}, u32[]{:S(2)}) collective-permute-start(bf16[1344,128]{1,0:T(8,128)(2,1)S(1)} %pad_maximum_fusion.refs_5_), channel_id=1, source_target_pairs={{0,224},{32,0},{64,32},{96,64},{128,96},{160,128},{192,160},{224,1... | collective-permute-start | bytes 1032200 | tf_op jit(solution)/shard_map/ppermute | solution.py:382
  20.1 3.4 %collective-permute-start = (bf16[144,1024]{1,0:T(8,128)(2,1)S(1)}, bf16[144,1024]{1,0:T(8,128)(2,1)S(1)}, u32[]{:S(2)}, u32[]{:S(2)}) collective-permute-start(bf16[144,1024]{1,0:T(8,128)(2,1)S(1)} %get-tuple-element.41.refs_1_), channel_id=1, source_target_pairs={{0,1},{1,0},{2,3},{3,2},{4,5},{5,4},{6,7},{7,6},{8,9},{9,8},{10,11... | collective-permute-start | bytes 884744 | tf_op jit(solution)/shard_map/ppermute | solution.py:374
  22.3 1.6 collective-permute-start.2
  44.8 34.3 %collective-permute-start.5 = (bf16[1344,128]{1,0:T(8,128)(2,1)S(1)}, bf16[1344,128]{1,0:T(8,128)(2,1)S(1)}, u32[]{:S(2)}, u32[]{:S(2)}) collective-permute-start(bf16[1344,128]{1,0:T(8,128)(2,1)S(1)} %collective-permute-done.3.refs_5_), channel_id=1, source_target_pairs={{0,32},{32,64},{64,96},{96,128},{128,160},{160,192},{192,224},{224... | collective-permute-start | bytes 1032200 | tf_op jit(solution)/shard_map/ppermute | solution.py:385
  45.3 33.9 %collective-permute-start.6 = (bf16[1344,128]{1,0:T(8,128)(2,1)S(1)}, bf16[1344,128]{1,0:T(8,128)(2,1)S(1)}, u32[]{:S(2)}, u32[]{:S(2)}) collective-permute-start(bf16[1344,128]{1,0:T(8,128)(2,1)S(1)} %collective-permute-done.4.refs_6_), channel_id=1, source_target_pairs={{0,224},{32,0},{64,32},{96,64},{128,96},{160,128},{192,160},{224,1... | collective-permute-start | bytes 1032200 | tf_op jit(solution)/shard_map/ppermute | solution.py:386
  79.2 32.3 %collective-permute-start.7 = (bf16[1344,128]{1,0:T(8,128)(2,1)S(1)}, bf16[1344,128]{1,0:T(8,128)(2,1)S(1)}, u32[]{:S(2)}, u32[]{:S(2)}) collective-permute-start(bf16[1344,128]{1,0:T(8,128)(2,1)S(1)} %collective-permute-done.5.refs_5_), channel_id=1, source_target_pairs={{0,32},{32,64},{64,96},{96,128},{128,160},{160,192},{192,224},{224... | collective-permute-start | bytes 1032200 | tf_op jit(solution)/shard_map/ppermute | solution.py:388
  79.3 32.3 %collective-permute-start.8 = (bf16[1344,128]{1,0:T(8,128)(2,1)S(1)}, bf16[1344,128]{1,0:T(8,128)(2,1)S(1)}, u32[]{:S(2)}, u32[]{:S(2)}) collective-permute-start(bf16[1344,128]{1,0:T(8,128)(2,1)S(1)} %collective-permute-done.6.refs_6_), channel_id=1, source_target_pairs={{0,224},{32,0},{64,32},{96,64},{128,96},{160,128},{192,160},{224,1... | collective-permute-start | bytes 1032200 | tf_op jit(solution)/shard_map/ppermute | solution.py:389
  111.5 33.8 %collective-permute-start.9 = (bf16[1344,128]{1,0:T(8,128)(2,1)S(1)}, bf16[1344,128]{1,0:T(8,128)(2,1)S(1)}, u32[]{:S(2)}, u32[]{:S(2)}) collective-permute-start(bf16[1344,128]{1,0:T(8,128)(2,1)S(1)} %collective-permute-done.7.refs_5_), channel_id=1, source_target_pairs={{0,32},{32,64},{64,96},{96,128},{128,160},{160,192},{192,224},{224... | collective-permute-start | bytes 1032200 | tf_op jit(solution)/shard_map/ppermute | solution.py:391
  111.6 33.7 %collective-permute-start.10 = (bf16[1344,128]{1,0:T(8,128)(2,1)S(1)}, bf16[1344,128]{1,0:T(8,128)(2,1)S(1)}, u32[]{:S(2)}, u32[]{:S(2)}) collective-permute-start(bf16[1344,128]{1,0:T(8,128)(2,1)S(1)} %collective-permute-done.8.refs_6_), channel_id=1, source_target_pairs={{0,225},{1,224},{32,1},{33,0},{64,33},{65,32},{96,65},{97,64},{128... | collective-permute-start | bytes 1032200 | tf_op jit(solution)/shard_map/ppermute | solution.py:393
  145.3 8.5 %collective-permute-start.11 = (bf16[144,2048]{1,0:T(8,128)(2,1)S(1)}, bf16[144,2048]{1,0:T(8,128)(2,1)S(1)}, u32[]{:S(2)}, u32[]{:S(2)}) collective-permute-start(bf16[144,2048]{1,0:T(8,128)(2,1)S(1)} %get-tuple-element.70), channel_id=1, source_target_pairs={{0,1},{1,0},{2,3},{3,2},{4,5},{5,4},{6,7},{7,6},{8,9},{9,8},{10,11... | collective-permute-start | bytes 1769480 | tf_op jit(solution)/shard_map/ppermute | solution.py:395
  154.0 10.1 %collective-permute-start.12 = (bf16[144,1024]{1,0:T(8,128)(2,1)S(1)}, bf16[144,1024]{1,0:T(8,128)(2,1)S(1)}, u32[]{:S(2)}, u32[]{:S(2)}) collective-permute-start(bf16[144,1024]{1,0:T(8,128)(2,1)S(1)} %merge.1), channel_id=1, source_target_pairs={{0,16},{16,0},{1,17},{17,1},{2,18},{18,2},{3,19},{19,3},{4,20},{20... | collective-permute-start | bytes 884744 | tf_op jit(solution)/shard_map/ppermute | solution.py:399

commit v4 on v3

--- a/solution.py
+++ b/solution.py
@@ -25,7 +25,7 @@
 UNROLL = 2
 SUB = 1024
 MASKED = -1e30
-HEADROOM = 100.0
+LIMIT = 2.0**110
 LOG2E = math.log2(math.e)
 SCALE2 = LOG2E / math.sqrt(HD)
 VMEM_LIMIT = 24 * 2**20
@@ -202,8 +202,7 @@
         at += 2 * ASKED
         k_ref[led_at + n * LED : led_at + (n + 1) * LED, :] = ref[at : at + LED, :]
         led.append(ref[at + LED : at + 2 * LED, :])
-    stacked = jnp.concatenate(values + asked + led, axis=0).astype(F32)
-    v_ref[:HD, :] = stacked.T.astype(BF16)
+    v_ref[:HD, :] = jnp.concatenate(values + asked + led, axis=0).T
     ones = [jnp.ones((AUX, count * LED), F32)]
     v_ref[HD:, :] = jnp.concatenate(alive + asked_alive + ones, axis=1).astype(BF16)
 
@@ -235,17 +234,16 @@
         old = pl.ds(pl.multiple_of(start + q_low, 128), SUB)
         s = scores(start, SUB)
         base = m0[:, old]
-        excess = jnp.maximum(excess, jnp.max(s, axis=0, keepdims=True) - base)
         p = jnp.exp2(s - base).astype(BF16)
         o = jnp.dot(v_ref[...], p, preferred_element_type=F32)
         m_out[:, cols] = base
         l_out[:, cols] = l0[:, old] + o[HD : HD + 1]
         acc_out[:, cols] = acc0[:, old] + o[:HD]
-        return excess
-
-    excess = lax.fori_loop(0, width // SUB, lazy, jnp.full((1, SUB), MASKED, F32), unroll=min(UNROLL, width // SUB))
-
-    @pl.when(jnp.max(excess) > HEADROOM)
+        return jnp.where(o[HD : HD + 1] <= LIMIT, excess, 1.0)
+
+    excess = lax.fori_loop(0, width // SUB, lazy, jnp.zeros((1, SUB), F32), unroll=min(UNROLL, width // SUB))
+
+    @pl.when(jnp.max(excess) > 0.5)
     def _():
         total = k_ref.shape[0]
         living = jnp.broadcast_to(v_ref[HD : HD + 1, :].astype(F32), (128, total)).T
@@ -375,7 +373,7 @@
     moved = lax.all_to_all(sending, ("yl", "x"), 0, 0, tiled=True)
     cache = cache_block(after(asker_memory_pairs, q0), leading_memory_pairs)
     q3 = lax.ppermute(q1, "c", shift(2, 1))
-    own = jnp.concatenate([moved.reshape(-1, HD), cache], axis=0)
+    own = jnp.concatenate([after(moved, q1, q2).reshape(-1, HD), cache], axis=0)
 
     up, down = shift(RING, 1), shift(RING, -1)
     f1 = lax.ppermute(own, "z", up)

time: 166 us -> 164 us (0.988)
  waiting for transfers between devices: 3.12 us -> 5.9 us
  starting transfers between devices: 29.9 us -> 27.5 us
  Pallas kernels: 130 us -> 128 us
    all_to_all x1, waiting for transfers between devices: 1.47 us -> 4.66 us  [body(): moved = lax.all_to_all(sending, ('yl', 'x'), 0, 0, tiled=True)]
    pallas_call x6, Pallas kernels: 126 us -> 124 us  [attend(): pl.pallas_call(functools.partial(attend_kernel, shards, mode, q_low), in_...]
    all_to_all x1, starting transfers between devices: 5.87 us -> 4.13 us  [body(): moved = lax.all_to_all(sending, ('yl', 'x'), 0, 0, tiled=True)]
  transfers between devices with their start and end apart: 14 -> 14, of which waited for: 3 -> 2; matrix products, arithmetic and copies ran while one was open for 0% -> 0% of each run, Pallas kernels for 76% -> 76%
where the time goes in v4:
time: 164 us
  Pallas kernels  128 us (78%)
  starting transfers between devices  27.5 us (17%)
  waiting for transfers between devices  5.9 us (4%)
  local copies, waits for them, and re-layouts  2.17 us (1%)
    pallas_call x6, Pallas kernels, attend(): pl.pallas_call(functools.partial(attend_kernel, shards, mode, q_low), in_...  124 us
    all_to_all x1, waiting for transfers between devices, body(): moved = lax.all_to_all(sending, ('yl', 'x'), 0, 0, tiled=True)  4.66 us
    ppermute x1, starting transfers between devices, body(): b4 = lax.ppermute(after(b3, state[0]), ('z', 'c'), cross)  4.31 us
    all_to_all x1, starting transfers between devices, body(): moved = lax.all_to_all(sending, ('yl', 'x'), 0, 0, tiled=True)  4.13 us
    ppermute x1, starting transfers between devices, body(): b1 = lax.ppermute(own, 'z', down)  4.03 us
    ppermute x1, starting transfers between devices, body(): q2 = lax.ppermute(q0, 'c', shift(2, 1))  3.33 us
  transfers between devices with their start and end apart: 14, of which 2 were waited for; matrix products, arithmetic and copies ran while one was open for 0% of the time, Pallas kernels for 76%

profile of v4, /device:TPU:1, one launch (start us, length us, event | category | flops | bytes accessed | tf_op | source)
XLA Modules:
  0.0 163.6 jit_solution(350640617899841836)
XLA Ops:
  0.0 0.0 copy-start.2
  0.0 2.0 %prepare.1 = (bf16[8,2,64,128]{3,2,1,0:T(8,128)(2,1)}, bf16[144,1024]{1,0:T(8,128)(2,1)S(1)}) custom-call(s32[64]{0:T(128)} %refs_0_.11, f32[4]{0:T(128)} %soft_hbm.1, bf16[64,16,128]{2,1,0:T(8,128)(2,1)} %doc_hbm.1, bf16[256,4,128]{2,1,0:T(4,128)(2,1)} %q_hbm.1), custom_call_target="tpu_custom_call" | custom-call | tf_op jit(solution)/shard_map/prepare/pallas_call | solution.py:106
  2.1 3.3 %collective-permute-start = (bf16[144,1024]{1,0:T(8,128)(2,1)S(1)}, bf16[144,1024]{1,0:T(8,128)(2,1)S(1)}, u32[]{:S(2)}, u32[]{:S(2)}) collective-permute-start(bf16[144,1024]{1,0:T(8,128)(2,1)S(1)} %get-tuple-element.42.refs_1_), channel_id=1, source_target_pairs={{0,1},{1,0},{2,3},{3,2},{4,5},{5,4},{6,7},{7,6},{8,9},{9,8},{10,11... | collective-permute-start | bytes 884744 | tf_op jit(solution)/shard_map/ppermute | solution.py:372
  5.4 1.2 collective-permute-start.1
  6.6 4.1 %all-to-all-start = ((bf16[8,2,64,128]{3,2,1,0:T(8,128)(2,1)}), bf16[8,2,64,128]{3,2,1,0:T(8,128)(2,1)S(1)}, u32[]{:S(2)}, u32[]{:S(2)}) async-start(bf16[8,2,64,128]{3,2,1,0:T(8,128)(2,1)} %get-tuple-element.46), calls=%async_computation | async-start | bytes 524288 | tf_op jit(solution)/shard_map/all_to_all | solution.py:373
  10.7 0.0 copy-start
  10.7 1.2 copy-done
  11.9 0.0 copy-start.1
  11.9 0.9 copy-done.1
  12.9 0.2 caches.1
  13.1 4.7 %all-to-all-done = bf16[8,2,64,128]{3,2,1,0:T(8,128)(2,1)S(1)} async-done(((bf16[8,2,64,128]{3,2,1,0:T(8,128)(2,1)}), bf16[8,2,64,128]{3,2,1,0:T(8,128)(2,1)S(1)}, u32[]{:S(2)}, u32[]{:S(2)}) %all-to-all-start) | async-done | bytes 262176 | tf_op jit(solution)/shard_map/all_to_all | solution.py:373
  17.7 0.0 collective-permute-done.refs_2_
  17.7 0.0 collective-permute-done.1.refs_3_
  17.8 1.7 %collective-permute-start.3 = (bf16[1344,128]{1,0:T(8,128)(2,1)S(1)}, bf16[1344,128]{1,0:T(8,128)(2,1)S(1)}, u32[]{:S(2)}, u32[]{:S(2)}) collective-permute-start(bf16[1344,128]{1,0:T(8,128)(2,1)S(1)} %pad_maximum_fusion.refs_5_), channel_id=1, source_target_pairs={{0,32},{32,64},{64,96},{96,128},{128,160},{160,192},{192,224},{224... | collective-permute-start | bytes 1032200 | tf_op jit(solution)/shard_map/ppermute | solution.py:379
  19.5 4.0 %collective-permute-start.4 = (bf16[1344,128]{1,0:T(8,128)(2,1)S(1)}, bf16[1344,128]{1,0:T(8,128)(2,1)S(1)}, u32[]{:S(2)}, u32[]{:S(2)}) collective-permute-start(bf16[1344,128]{1,0:T(8,128)(2,1)S(1)} %pad_maximum_fusion.refs_5_), channel_id=1, source_target_pairs={{0,224},{32,0},{64,32},{96,64},{128,96},{160,128},{192,160},{224,1... | collective-permute-start | bytes 1032200 | tf_op jit(solution)/shard_map/ppermute | solution.py:380
  23.5 1.5 collective-permute-start.2
  25.0 1.2 collective-permute-done.2.refs_4_
  26.2 0.0 copy-done.2
  26.2 20.3 %attend.6 = (f32[1,4096]{1,0:T(1,128)S(1)}, f32[1,4096]{1,0:T(1,128)S(1)}, f32[128,4096]{1,0:T(8,128)S(1)}, bf16[144,4096]{1,0:T(8,128)(2,1)S(1)}) custom-call(s32[64]{0:T(128)S(1)} %copy-done.2, bf16[144,1024]{1,0:T(8,128)(2,1)S(1)} %get-tuple-element.42.refs_1_, bf16[144,1024]{1,0:T(8,128)(2,1)S(1)} %collective-permute-done.refs_2_, ...), custom_call_target="tpu_custom_call" | custom-call | tf_op jit(solution)/shard_map/attend/pallas_call | solution.py:302
  46.6 0.0 collective-permute-done.3.refs_5_
  46.6 0.1 collective-permute-start.5
  46.7 0.0 collective-permute-done.4.refs_6_
  46.7 2.7 %collective-permute-start.6 = (bf16[1344,128]{1,0:T(8,128)(2,1)S(1)}, bf16[1344,128]{1,0:T(8,128)(2,1)S(1)}, u32[]{:S(2)}, u32[]{:S(2)}) collective-permute-start(bf16[1344,128]{1,0:T(8,128)(2,1)S(1)} %collective-permute-done.4.refs_6_), channel_id=1, source_target_pairs={{0,224},{32,0},{64,32},{96,64},{128,96},{160,128},{192,160},{224,1... | collective-permute-start | bytes 1032200 | tf_op jit(solution)/shard_map/ppermute | solution.py:384
  49.3 29.2 %attend.7 = (f32[1,4096]{1,0:T(1,128)S(1)}, f32[1,4096]{1,0:T(1,128)S(1)}, f32[128,4096]{1,0:T(8,128)S(1)}) custom-call(s32[64]{0:T(128)S(1)} %copy-done.2, bf16[144,4096]{1,0:T(8,128)(2,1)S(1)} %get-tuple-element.49.refs_1_, f32[1,4096]{1,0:T(1,128)S(1)} %get-tuple-element.50.refs_2_, f32[1,4096]{1,0:T(1,128)S(1)} %get-tuple-element.51.refs_3_, ...), custom_call_target="tpu_custom_call" | custom-call | tf_op jit(solution)/shard_map/attend/pallas_call | solution.py:302
  78.5 0.0 collective-permute-done.5.refs_5_
  78.5 0.1 collective-permute-start.7
  78.6 0.0 collective-permute-done.6.refs_6_
  78.6 2.7 %collective-permute-start.8 = (bf16[1344,128]{1,0:T(8,128)(2,1)S(1)}, bf16[1344,128]{1,0:T(8,128)(2,1)S(1)}, u32[]{:S(2)}, u32[]{:S(2)}) collective-permute-start(bf16[1344,128]{1,0:T(8,128)(2,1)S(1)} %collective-permute-done.6.refs_6_), channel_id=1, source_target_pairs={{0,224},{32,0},{64,32},{96,64},{128,96},{160,128},{192,160},{224,1... | collective-permute-start | bytes 1032200 | tf_op jit(solution)/shard_map/ppermute | solution.py:387
  81.3 29.0 %attend.8 = (f32[1,4096]{1,0:T(1,128)S(1)}, f32[1,4096]{1,0:T(1,128)S(1)}, f32[128,4096]{1,0:T(8,128)S(1)}) custom-call(s32[64]{0:T(128)S(1)} %copy-done.2, bf16[144,4096]{1,0:T(8,128)(2,1)S(1)} %get-tuple-element.49.refs_1_, f32[1,4096]{1,0:T(1,128)S(1)} %get-tuple-element.53.refs_2_, f32[1,4096]{1,0:T(1,128)S(1)} %get-tuple-element.54.refs_3_, ...), custom_call_target="tpu_custom_call" | custom-call | tf_op jit(solution)/shard_map/attend/pallas_call | solution.py:302
  110.2 0.0 collective-permute-done.7.refs_5_
  110.2 0.1 collective-permute-start.9
  110.3 0.0 collective-permute-done.8.refs_6_
  110.3 4.3 %collective-permute-start.10 = (bf16[1344,128]{1,0:T(8,128)(2,1)S(1)}, bf16[1344,128]{1,0:T(8,128)(2,1)S(1)}, u32[]{:S(2)}, u32[]{:S(2)}) collective-permute-start(bf16[1344,128]{1,0:T(8,128)(2,1)S(1)} %collective-permute-done.8.refs_6_), channel_id=1, source_target_pairs={{0,225},{1,224},{32,1},{33,0},{64,33},{65,32},{96,65},{97,64},{128... | collective-permute-start | bytes 1032200 | tf_op jit(solution)/shard_map/ppermute | solution.py:391
  114.7 29.2 %attend.9 = (f32[1,4096]{1,0:T(1,128)S(1)}, f32[1,4096]{1,0:T(1,128)S(1)}, f32[128,4096]{1,0:T(8,128)S(1)}, bf16[144,2048]{1,0:T(8,128)(2,1)S(1)}) custom-call(s32[64]{0:T(128)S(1)} %copy-done.2, bf16[144,4096]{1,0:T(8,128)(2,1)S(1)} %get-tuple-element.49.refs_1_, f32[1,4096]{1,0:T(1,128)S(1)} %get-tuple-element.58.refs_2_, ...), custom_call_target="tpu_custom_call" | custom-call | tf_op jit(solution)/shard_map/attend/pallas_call | solution.py:302
  143.8 0.0 collective-permute-done.9.refs_5_
  143.8 0.0 collective-permute-done.10.refs_6_
  143.8 0.1 collective-permute-start.11
  143.9 8.2 %attend.10 = (f32[1,1024]{1,0:T(1,128)S(1)}, f32[1,1024]{1,0:T(1,128)S(1)}, f32[128,1024]{1,0:T(8,128)S(1)}) custom-call(s32[64]{0:T(128)S(1)} %copy-done.2, bf16[144,4096]{1,0:T(8,128)(2,1)S(1)} %get-tuple-element.49.refs_1_, f32[1,4096]{1,0:T(1,128)S(1)} %get-tuple-element.63.refs_2_, f32[1,4096]{1,0:T(1,128)S(1)} %get-tuple-element.64.refs_3_, ...), custom_call_target="tpu_custom_call" | custom-call | tf_op jit(solution)/shard_map/attend/pallas_call | solution.py:302
  152.2 0.0 collective-permute-done.11.rec.refs_7_
  152.2 0.2 merge.1
  152.4 1.6 %collective-permute-start.12 = (bf16[144,1024]{1,0:T(8,128)(2,1)S(1)}, bf16[144,1024]{1,0:T(8,128)(2,1)S(1)}, u32[]{:S(2)}, u32[]{:S(2)}) collective-permute-start(bf16[144,1024]{1,0:T(8,128)(2,1)S(1)} %merge.1), channel_id=1, source_target_pairs={{0,16},{16,0},{1,17},{17,1},{2,18},{18,2},{3,19},{19,3},{4,20},{20... | collective-permute-start | bytes 884744 | tf_op jit(solution)/shard_map/ppermute | solution.py:397
  154.0 8.1 %attend.11 = (f32[1,1024]{1,0:T(1,128)S(1)}, f32[1,1024]{1,0:T(1,128)S(1)}, f32[128,1024]{1,0:T(8,128)S(1)}) custom-call(s32[64]{0:T(128)S(1)} %copy-done.2, bf16[144,4096]{1,0:T(8,128)(2,1)S(1)} %get-tuple-element.49.refs_1_, f32[1,4096]{1,0:T(1,128)S(1)} %get-tuple-element.63.refs_2_, f32[1,4096]{1,0:T(1,128)S(1)} %get-tuple-element.64.refs_3_, ...), custom_call_target="tpu_custom_call" | custom-call | tf_op jit(solution)/shard_map/attend/pallas_call | solution.py:302
  162.1 0.0 collective-permute-done.12.far
  162.2 1.5 finish.1
  (1 shorter events, 0.0 us)
Async XLA Ops:
  0.0 26.2 %copy-start.2 = (s32[64]{0:T(128)S(1)}, s32[64]{0:T(128)}, u32[]{:S(2)}) copy-start(s32[64]{0:T(128)} %refs_0_.11) | copy-start | bytes 772
  2.1 15.7 %collective-permute-start = (bf16[144,1024]{1,0:T(8,128)(2,1)S(1)}, bf16[144,1024]{1,0:T(8,128)(2,1)S(1)}, u32[]{:S(2)}, u32[]{:S(2)}) collective-permute-start(bf16[144,1024]{1,0:T(8,128)(2,1)S(1)} %get-tuple-element.42.refs_1_), channel_id=1, source_target_pairs={{0,1},{1,0},{2,3},{3,2},{4,5},{5,4},{6,7},{7,6},{8,9},{9,8},{10,11... | collective-permute-start | bytes 884744 | tf_op jit(solution)/shard_map/ppermute | solution.py:372
  5.4 12.3 %collective-permute-start.1 = (bf16[144,1024]{1,0:T(8,128)(2,1)S(1)}, bf16[144,1024]{1,0:T(8,128)(2,1)S(1)}, u32[]{:S(2)}, u32[]{:S(2)}) collective-permute-start(bf16[144,1024]{1,0:T(8,128)(2,1)S(1)} %get-tuple-element.42.refs_1_), channel_id=1, source_target_pairs={{0,16},{16,0},{1,17},{17,1},{2,18},{18,2},{3,19},{19,3},{4,20},{20... | collective-permute-start | bytes 884744 | tf_op jit(solution)/shard_map/ppermute | solution.py:371
  6.6 11.1 %all-to-all-start = ((bf16[8,2,64,128]{3,2,1,0:T(8,128)(2,1)}), bf16[8,2,64,128]{3,2,1,0:T(8,128)(2,1)S(1)}, u32[]{:S(2)}, u32[]{:S(2)}) async-start(bf16[8,2,64,128]{3,2,1,0:T(8,128)(2,1)} %get-tuple-element.46), calls=%async_computation | async-start | bytes 524288 | tf_op jit(solution)/shard_map/all_to_all | solution.py:373
  10.7 1.2 copy-start
  11.9 0.9 copy-start.1
  17.8 28.8 %collective-permute-start.3 = (bf16[1344,128]{1,0:T(8,128)(2,1)S(1)}, bf16[1344,128]{1,0:T(8,128)(2,1)S(1)}, u32[]{:S(2)}, u32[]{:S(2)}) collective-permute-start(bf16[1344,128]{1,0:T(8,128)(2,1)S(1)} %pad_maximum_fusion.refs_5_), channel_id=1, source_target_pairs={{0,32},{32,64},{64,96},{96,128},{128,160},{160,192},{192,224},{224... | collective-permute-start | bytes 1032200 | tf_op jit(solution)/shard_map/ppermute | solution.py:379
  19.5 27.2 %collective-permute-start.4 = (bf16[1344,128]{1,0:T(8,128)(2,1)S(1)}, bf16[1344,128]{1,0:T(8,128)(2,1)S(1)}, u32[]{:S(2)}, u32[]{:S(2)}) collective-permute-start(bf16[1344,128]{1,0:T(8,128)(2,1)S(1)} %pad_maximum_fusion.refs_5_), channel_id=1, source_target_pairs={{0,224},{32,0},{64,32},{96,64},{128,96},{160,128},{192,160},{224,1... | collective-permute-start | bytes 1032200 | tf_op jit(solution)/shard_map/ppermute | solution.py:380
  23.5 2.7 %collective-permute-start.2 = (bf16[144,1024]{1,0:T(8,128)(2,1)S(1)}, bf16[144,1024]{1,0:T(8,128)(2,1)S(1)}, u32[]{:S(2)}, u32[]{:S(2)}) collective-permute-start(bf16[144,1024]{1,0:T(8,128)(2,1)S(1)} %collective-permute-done.1.refs_3_), channel_id=1, source_target_pairs={{0,1},{1,0},{2,3},{3,2},{4,5},{5,4},{6,7},{7,6},{8,9},{9,8},{10,11... | collective-permute-start | bytes 884744 | tf_op jit(solution)/shard_map/ppermute | solution.py:375
  46.6 31.9 %collective-permute-start.5 = (bf16[1344,128]{1,0:T(8,128)(2,1)S(1)}, bf16[1344,128]{1,0:T(8,128)(2,1)S(1)}, u32[]{:S(2)}, u32[]{:S(2)}) collective-permute-start(bf16[1344,128]{1,0:T(8,128)(2,1)S(1)} %collective-permute-done.3.refs_5_), channel_id=1, source_target_pairs={{0,32},{32,64},{64,96},{96,128},{128,160},{160,192},{192,224},{224... | collective-permute-start | bytes 1032200 | tf_op jit(solution)/shard_map/ppermute | solution.py:383
  46.7 31.9 %collective-permute-start.6 = (bf16[1344,128]{1,0:T(8,128)(2,1)S(1)}, bf16[1344,128]{1,0:T(8,128)(2,1)S(1)}, u32[]{:S(2)}, u32[]{:S(2)}) collective-permute-start(bf16[1344,128]{1,0:T(8,128)(2,1)S(1)} %collective-permute-done.4.refs_6_), channel_id=1, source_target_pairs={{0,224},{32,0},{64,32},{96,64},{128,96},{160,128},{192,160},{224,1... | collective-permute-start | bytes 1032200 | tf_op jit(solution)/shard_map/ppermute | solution.py:384
  78.5 31.7 %collective-permute-start.7 = (bf16[1344,128]{1,0:T(8,128)(2,1)S(1)}, bf16[1344,128]{1,0:T(8,128)(2,1)S(1)}, u32[]{:S(2)}, u32[]{:S(2)}) collective-permute-start(bf16[1344,128]{1,0:T(8,128)(2,1)S(1)} %collective-permute-done.5.refs_5_), channel_id=1, source_target_pairs={{0,32},{32,64},{64,96},{96,128},{128,160},{160,192},{192,224},{224... | collective-permute-start | bytes 1032200 | tf_op jit(solution)/shard_map/ppermute | solution.py:386
  78.6 31.7 %collective-permute-start.8 = (bf16[1344,128]{1,0:T(8,128)(2,1)S(1)}, bf16[1344,128]{1,0:T(8,128)(2,1)S(1)}, u32[]{:S(2)}, u32[]{:S(2)}) collective-permute-start(bf16[1344,128]{1,0:T(8,128)(2,1)S(1)} %collective-permute-done.6.refs_6_), channel_id=1, source_target_pairs={{0,224},{32,0},{64,32},{96,64},{128,96},{160,128},{192,160},{224,1... | collective-permute-start | bytes 1032200 | tf_op jit(solution)/shard_map/ppermute | solution.py:387
  110.2 33.6 %collective-permute-start.9 = (bf16[1344,128]{1,0:T(8,128)(2,1)S(1)}, bf16[1344,128]{1,0:T(8,128)(2,1)S(1)}, u32[]{:S(2)}, u32[]{:S(2)}) collective-permute-start(bf16[1344,128]{1,0:T(8,128)(2,1)S(1)} %collective-permute-done.7.refs_5_), channel_id=1, source_target_pairs={{0,32},{32,64},{64,96},{96,128},{128,160},{160,192},{192,224},{224... | collective-permute-start | bytes 1032200 | tf_op jit(solution)/shard_map/ppermute | solution.py:389
  110.3 33.5 %collective-permute-start.10 = (bf16[1344,128]{1,0:T(8,128)(2,1)S(1)}, bf16[1344,128]{1,0:T(8,128)(2,1)S(1)}, u32[]{:S(2)}, u32[]{:S(2)}) collective-permute-start(bf16[1344,128]{1,0:T(8,128)(2,1)S(1)} %collective-permute-done.8.refs_6_), channel_id=1, source_target_pairs={{0,225},{1,224},{32,1},{33,0},{64,33},{65,32},{96,65},{97,64},{128... | collective-permute-start | bytes 1032200 | tf_op jit(solution)/shard_map/ppermute | solution.py:391
  143.8 8.3 %collective-permute-start.11 = (bf16[144,2048]{1,0:T(8,128)(2,1)S(1)}, bf16[144,2048]{1,0:T(8,128)(2,1)S(1)}, u32[]{:S(2)}, u32[]{:S(2)}) collective-permute-start(bf16[144,2048]{1,0:T(8,128)(2,1)S(1)} %get-tuple-element.72), channel_id=1, source_target_pairs={{0,1},{1,0},{2,3},{3,2},{4,5},{5,4},{6,7},{7,6},{8,9},{9,8},{10,11... | collective-permute-start | bytes 1769480 | tf_op jit(solution)/shard_map/ppermute | solution.py:393
  152.4 9.8 %collective-permute-start.12 = (bf16[144,1024]{1,0:T(8,128)(2,1)S(1)}, bf16[144,1024]{1,0:T(8,128)(2,1)S(1)}, u32[]{:S(2)}, u32[]{:S(2)}) collective-permute-start(bf16[144,1024]{1,0:T(8,128)(2,1)S(1)} %merge.1), channel_id=1, source_target_pairs={{0,16},{16,0},{1,17},{17,1},{2,18},{18,2},{3,19},{19,3},{4,20},{20... | collective-permute-start | bytes 884744 | tf_op jit(solution)/shard_map/ppermute | solution.py:397

commit v5 on v4

--- a/solution.py
+++ b/solution.py
@@ -67,8 +67,8 @@
     return jnp.concatenate(parts, axis=0).astype(BF16)
 
 
-def live_counts(extent_ref, zpos, cpos):
-    base = (2 * zpos + lax.axis_index("yh")) * 4
+def live_counts(extent_ref, zpos, ypos, cpos):
+    base = (2 * zpos + ypos) * 4
     start = cpos * SEND
     return [extent_ref[base + j // 2] - (j % 2) * 128 - start for j in range(KVH)]
 
@@ -83,7 +83,7 @@
     rows = doc_ref.shape[0]
     own = lax.axis_index("yl") * 4 + lax.axis_index("x")
     live = jnp.int32(0)
-    for j, count in enumerate(live_counts(extent_ref, lax.axis_index("z"), lax.axis_index("c"))):
+    for j, count in enumerate(live_counts(extent_ref, lax.axis_index("z"), lax.axis_index("yh"), lax.axis_index("c"))):
         live = jnp.where(own == j, count, live)
     keep = lax.broadcasted_iota(jnp.int32, (rows, HD), 0) < live
     for g in range(KVH):
@@ -163,12 +163,12 @@
         q_ref, m0, l0, acc0 = refs[:4]
         pay = refs[4 : 4 + count]
         refs = refs[4 + count :]
-        if mode in ("middle", "part"):
+        if mode == "pack":
+            m_out, l_out, acc_out, packed_ref, k_ref, v_ref = refs
+        elif mode == "only":
+            packed_ref, k_ref, v_ref, m_out, l_out, acc_out = refs
+        else:
             m_out, l_out, acc_out, k_ref, v_ref = refs
-        elif mode == "pack":
-            m_out, l_out, acc_out, packed_ref, k_ref, v_ref = refs
-        else:
-            rec_ref, m_end, l_end, acc_end, k_ref, v_ref, m_out, l_out, acc_out = refs
     width = m_out.shape[1]
     zpos, ypos, cpos = lax.axis_index("z"), lax.axis_index("yh"), lax.axis_index("c")
     span = KVH * SEND
@@ -177,7 +177,7 @@
 
     values, asked, led, alive, asked_alive = [], [], [], [], []
     for n, (ref, (away, swapped)) in enumerate(zip(pay, shards)):
-        counts = live_counts(extent_ref, (zpos + away) % RING, 1 - cpos if swapped else cpos)
+        counts = live_counts(extent_ref, (zpos + away) % RING, 1 - ypos if swapped else ypos, cpos)
         lane = lax.broadcasted_iota(jnp.int32, (AUX, span), 1)
         bound = jnp.zeros((AUX, span), jnp.int32)
         for j in range(KVH):
@@ -217,7 +217,7 @@
     def scores(start, size):
         cols = pl.ds(pl.multiple_of(start + q_low, 128), size)
         s = jnp.dot(k_ref[...], q_ref[:HD, cols], preferred_element_type=F32)
-        factor = join3(q_ref[HD : HD + 3, cols])
+        factor = join3(q_ref[HD:, cols])
         rest = s[asked_at:] * SCALE2
         if first:
             token = (lax.broadcasted_iota(jnp.int32, (1, size), 1) + start) % TILE
@@ -246,7 +246,7 @@
     @pl.when(jnp.max(excess) > 0.5)
     def _():
         total = k_ref.shape[0]
-        living = jnp.broadcast_to(v_ref[HD : HD + 1, :].astype(F32), (128, total)).T
+        living = jnp.broadcast_to(v_ref[HD:, :].astype(F32)[:1], (128, total)).T
 
         def exact(i, carry):
             start = pl.multiple_of(i * 128, 128)
@@ -265,12 +265,9 @@
 
         lax.fori_loop(0, width // 128, exact, 0)
 
-    if mode == "pack":
-        for n in range(2):
-            cols = slice((2 * n + 1) * ROWS, (2 * n + 2) * ROWS)
-            packed_ref[:, n * ROWS : (n + 1) * ROWS] = pack(m_out[:, cols], l_out[:, cols], acc_out[:, cols])
-    if mode == "keep":
-        m_end[...], l_end[...], acc_end[...] = fold(*normal(m_out[...], l_out[...], acc_out[...]), rec_ref[:, :ROWS])
+    if mode in ("pack", "only"):
+        cols = slice(width - ROWS, width)
+        packed_ref[...] = pack(m_out[:, cols], l_out[:, cols], acc_out[:, cols])
 
 
 def state_shapes(width):
@@ -281,23 +278,21 @@
     ]
 
 
-def attend(extent, queries, state, pays, shards, mode, received=None, q_low=0):
+def attend(extent, queries, state, pays, shards, mode, q_low=0, width=BLOCKS * ROWS):
     keys = len(shards) * (KVH * SEND + ASKED + LED)
-    width = ROWS if mode in ("part", "keep") else BLOCKS * ROWS
     scratch = [pltpu.VMEM((keys, HD), BF16), pltpu.VMEM((HD + AUX, keys), BF16)]
-    floats = [pltpu.VMEM((1, width), F32), pltpu.VMEM((1, width), F32), pltpu.VMEM((HD, width), F32)]
     shapes = state_shapes(width)
     if mode == "first":
         args = [extent, *queries, *pays]
         shapes.append(jax.ShapeDtypeStruct((HD + AUX, width), BF16))
-        scratch += floats
+        scratch += [pltpu.VMEM((1, width), F32), pltpu.VMEM((1, width), F32), pltpu.VMEM((HD, width), F32)]
     else:
         args = [extent, queries, *state, *pays]
-    if mode == "pack":
-        shapes.append(jax.ShapeDtypeStruct((HD + AUX, 2 * ROWS), BF16))
-    if mode == "keep":
-        args.append(received)
-        scratch += floats
+    if mode == "only":
+        shapes = []
+        scratch += [pltpu.VMEM((1, width), F32), pltpu.VMEM((1, width), F32), pltpu.VMEM((HD, width), F32)]
+    if mode in ("pack", "only"):
+        shapes.append(jax.ShapeDtypeStruct((HD + AUX, ROWS), BF16))
     vmem = pl.BlockSpec(memory_space=pltpu.VMEM)
     return pl.pallas_call(
         functools.partial(attend_kernel, shards, mode, q_low),
@@ -312,7 +307,7 @@
 
 def pack(m, l, acc):
     total = m + jnp.log2(l)
-    return jnp.concatenate([(acc / l).astype(BF16), aux_rows(total)], axis=0)
+    return jnp.concatenate([(acc * (1.0 / l)).astype(BF16), aux_rows(total)], axis=0)
 
 
 def fold(m, l, acc, received):
@@ -325,11 +320,11 @@
 
 def normal(m, l, acc):
     total = m + jnp.log2(l)
-    return total, jnp.ones_like(total), acc / l
+    return total, jnp.ones_like(total), acc * (1.0 / l)
 
 
 def merge_kernel(m, l, acc, rec, send_ref):
-    send_ref[...] = pack(*fold(*normal(m[...], l[...], acc[...]), rec[:, ROWS:]))
+    send_ref[...] = pack(*fold(*normal(m[:, :ROWS], l[:, :ROWS], acc[:, :ROWS]), rec[...]))
 
 
 def merge_cores(state, received):
@@ -341,21 +336,22 @@
     )(*state, received)
 
 
-def finish_kernel(m, l, acc, far, out_ref):
-    _, total, summed = fold(m[...], l[...], acc[...], far[...])
-    result = summed / total
+def finish_kernel(m, l, acc, rec, far, out_ref):
+    near = fold(*normal(m[...], l[...], acc[...]), rec[...])
+    _, total, summed = fold(*near, far[...])
+    result = (summed * (1.0 / total)).astype(BF16)
     tokens, heads, _ = out_ref.shape
-    for h in range(heads):
-        out_ref[:, h, :] = result[:, h * tokens : (h + 1) * tokens].T.astype(BF16)
-
-
-def finish(state, far, shape):
+    parts = [result[:, h * tokens : (h + 1) * tokens].T for h in range(heads)]
+    out_ref[...] = jnp.stack(parts, axis=1)
+
+
+def finish(state, received, far, shape):
     return pl.pallas_call(
         finish_kernel,
         out_shape=jax.ShapeDtypeStruct(shape, BF16),
         compiler_params=params(),
         name="finish",
-    )(*state, far)
+    )(*state, received, far)
 
 
 def body(
@@ -387,16 +383,20 @@
     b3 = lax.ppermute(after(b2, state[0]), "z", down)
     state = attend(extent, queries, state, [f2, b2], [(-2, False), (2, False)], "middle")
     f4 = lax.ppermute(after(f3, state[0]), "z", up)
-    cross = [(2 * z + c, 2 * ((z - 1) % RING) + 1 - c) for z in range(RING) for c in range(2)]
-    b4 = lax.ppermute(after(b3, state[0]), ("z", "c"), cross)
-    *state, packed = attend(extent, queries, state, [f3, b3], [(-3, False), (3, False)], "pack")
-    received = lax.ppermute(after(packed, f4, b4), "c", shift(2, 1))
-    rest = [(-4, False), (-4, True)]
-    apart = attend(extent, queries, state, [f4, b4], rest, "part", None, 2 * ROWS)
+    cross = [(2 * z + y, 2 * ((z - 1) % RING) + 1 - y) for z in range(RING) for y in range(2)]
+    b4 = lax.ppermute(after(b3, state[0]), ("z", "yh"), cross)
+    half = 2 * ROWS
+    last = [(-3, False), (3, False)]
+    *apart, packed = attend(extent, queries, state, [f3, b3], last, "pack", half, half)
+    received = lax.ppermute(packed, "c", shift(2, 1))
     send = merge_cores(apart, received)
     far = lax.ppermute(send, "yh", shift(2, 1))
-    kept = attend(extent, queries, state, [after(f4, send), b4], rest, "keep", received, 0)
-    return finish(kept, far, asker_vectors.shape)
+    state = attend(extent, queries, state, [after(f3, send), b3], last, "middle", 0, half)
+    rest = [(-4, False), (-4, True)]
+    (packed,) = attend(extent, queries, state, [f4, b4], rest, "only", ROWS, ROWS)
+    received = lax.ppermute(packed, "c", shift(2, 1))
+    kept = attend(extent, queries, state, [after(f4, packed), b4], rest, "middle", 0, ROWS)
+    return finish(kept, received, far, asker_vectors.shape)
 
 
 def solution(mesh):

time: 164 us -> 168 us (1.024)
  starting transfers between devices: 27.5 us -> 30 us
    ppermute x2 -> x3, starting transfers between devices: 4.4 us -> 6.79 us  [the longest x1 3.93 us: body(): b4 = lax.ppermute(after(b3, state[0]), ('z', 'yh'), cross)]
    pallas_call x6 -> x7, Pallas kernels: 124 us -> 125 us  [attend(): pl.pallas_call(functools.partial(attend_kernel, shards, mode, q_low), in_...]
  transfers between devices with their start and end apart: 14 -> 15, of which waited for: 2 -> 3; matrix products, arithmetic and copies ran while one was open for 0% -> 0% of each run, Pallas kernels for 76% -> 74%
where the time goes in v5:
time: 168 us
  Pallas kernels  129 us (77%)
  starting transfers between devices  30 us (18%)
  waiting for transfers between devices  7.11 us (4%)
  local copies, waits for them, and re-layouts  2.17 us (1%)
    pallas_call x7, Pallas kernels, attend(): pl.pallas_call(functools.partial(attend_kernel, shards, mode, q_low), in_...  125 us
    all_to_all x1, waiting for transfers between devices, body(): moved = lax.all_to_all(sending, ('yl', 'x'), 0, 0, tiled=True)  4.66 us
    all_to_all x1, starting transfers between devices, body(): moved = lax.all_to_all(sending, ('yl', 'x'), 0, 0, tiled=True)  4.13 us
    ppermute x1, starting transfers between devices, body(): b1 = lax.ppermute(own, 'z', down)  4.03 us
    ppermute x1, starting transfers between devices, body(): b4 = lax.ppermute(after(b3, state[0]), ('z', 'yh'), cross)  3.93 us
  transfers between devices with their start and end apart: 15, of which 3 were waited for; matrix products, arithmetic and copies ran while one was open for 0% of the time, Pallas kernels for 74%

profile of v5, /device:TPU:1, one launch (start us, length us, event | category | flops | bytes accessed | tf_op | source)
XLA Modules:
  0.0 168.0 jit_solution(1749198342445571579)
XLA Ops:
  0.0 0.0 copy-start.2
  0.0 2.1 %prepare.1 = (bf16[8,2,64,128]{3,2,1,0:T(8,128)(2,1)}, bf16[144,1024]{1,0:T(8,128)(2,1)S(1)}) custom-call(s32[64]{0:T(128)} %refs_0_.13, f32[4]{0:T(128)} %soft_hbm.1, bf16[64,16,128]{2,1,0:T(8,128)(2,1)} %doc_hbm.1, bf16[256,4,128]{2,1,0:T(4,128)(2,1)} %q_hbm.1), custom_call_target="tpu_custom_call" | custom-call | tf_op jit(solution)/shard_map/prepare/pallas_call | solution.py:106
  2.1 3.3 %collective-permute-start = (bf16[144,1024]{1,0:T(8,128)(2,1)S(1)}, bf16[144,1024]{1,0:T(8,128)(2,1)S(1)}, u32[]{:S(2)}, u32[]{:S(2)}) collective-permute-start(bf16[144,1024]{1,0:T(8,128)(2,1)S(1)} %get-tuple-element.42.refs_1_), channel_id=1, source_target_pairs={{0,1},{1,0},{2,3},{3,2},{4,5},{5,4},{6,7},{7,6},{8,9},{9,8},{10,11... | collective-permute-start | bytes 884744 | tf_op jit(solution)/shard_map/ppermute | solution.py:368
  5.4 1.2 collective-permute-start.1
  6.6 4.1 %all-to-all-start = ((bf16[8,2,64,128]{3,2,1,0:T(8,128)(2,1)}), bf16[8,2,64,128]{3,2,1,0:T(8,128)(2,1)S(1)}, u32[]{:S(2)}, u32[]{:S(2)}) async-start(bf16[8,2,64,128]{3,2,1,0:T(8,128)(2,1)} %get-tuple-element.46), calls=%async_computation | async-start | bytes 524288 | tf_op jit(solution)/shard_map/all_to_all | solution.py:369
  10.7 0.0 copy-start
  10.7 1.2 copy-done
  11.9 0.0 copy-start.1
  11.9 0.9 copy-done.1
  12.9 0.2 caches.1
  13.1 4.7 %all-to-all-done = bf16[8,2,64,128]{3,2,1,0:T(8,128)(2,1)S(1)} async-done(((bf16[8,2,64,128]{3,2,1,0:T(8,128)(2,1)}), bf16[8,2,64,128]{3,2,1,0:T(8,128)(2,1)S(1)}, u32[]{:S(2)}, u32[]{:S(2)}) %all-to-all-start) | async-done | bytes 262176 | tf_op jit(solution)/shard_map/all_to_all | solution.py:369
  17.7 0.0 collective-permute-done.refs_2_
  17.7 0.0 collective-permute-done.1.refs_3_
  17.8 1.7 %collective-permute-start.3 = (bf16[1344,128]{1,0:T(8,128)(2,1)S(1)}, bf16[1344,128]{1,0:T(8,128)(2,1)S(1)}, u32[]{:S(2)}, u32[]{:S(2)}) collective-permute-start(bf16[1344,128]{1,0:T(8,128)(2,1)S(1)} %pad_maximum_fusion.refs_5_), channel_id=1, source_target_pairs={{0,32},{32,64},{64,96},{96,128},{128,160},{160,192},{192,224},{224... | collective-permute-start | bytes 1032200 | tf_op jit(solution)/shard_map/ppermute | solution.py:375
  19.5 4.0 %collective-permute-start.4 = (bf16[1344,128]{1,0:T(8,128)(2,1)S(1)}, bf16[1344,128]{1,0:T(8,128)(2,1)S(1)}, u32[]{:S(2)}, u32[]{:S(2)}) collective-permute-start(bf16[1344,128]{1,0:T(8,128)(2,1)S(1)} %pad_maximum_fusion.refs_5_), channel_id=1, source_target_pairs={{0,224},{32,0},{64,32},{96,64},{128,96},{160,128},{192,160},{224,1... | collective-permute-start | bytes 1032200 | tf_op jit(solution)/shard_map/ppermute | solution.py:376
  23.5 1.5 collective-permute-start.2
  25.0 1.2 collective-permute-done.2.refs_4_
  26.2 0.0 copy-done.2
  26.2 20.4 %attend.7 = (f32[1,4096]{1,0:T(1,128)S(1)}, f32[1,4096]{1,0:T(1,128)S(1)}, f32[128,4096]{1,0:T(8,128)S(1)}, bf16[144,4096]{1,0:T(8,128)(2,1)S(1)}) custom-call(s32[64]{0:T(128)S(1)} %copy-done.2, bf16[144,1024]{1,0:T(8,128)(2,1)S(1)} %get-tuple-element.42.refs_1_, bf16[144,1024]{1,0:T(8,128)(2,1)S(1)} %collective-permute-done.refs_2_, ...), custom_call_target="tpu_custom_call" | custom-call | tf_op jit(solution)/shard_map/attend/pallas_call | solution.py:297
  46.6 0.0 collective-permute-done.3.refs_5_
  46.6 0.1 collective-permute-start.5
  46.7 0.0 collective-permute-done.4.refs_6_
  46.7 2.7 %collective-permute-start.6 = (bf16[1344,128]{1,0:T(8,128)(2,1)S(1)}, bf16[1344,128]{1,0:T(8,128)(2,1)S(1)}, u32[]{:S(2)}, u32[]{:S(2)}) collective-permute-start(bf16[1344,128]{1,0:T(8,128)(2,1)S(1)} %collective-permute-done.4.refs_6_), channel_id=1, source_target_pairs={{0,224},{32,0},{64,32},{96,64},{128,96},{160,128},{192,160},{224,1... | collective-permute-start | bytes 1032200 | tf_op jit(solution)/shard_map/ppermute | solution.py:380
  49.3 29.1 %attend.8 = (f32[1,4096]{1,0:T(1,128)S(1)}, f32[1,4096]{1,0:T(1,128)S(1)}, f32[128,4096]{1,0:T(8,128)S(1)}) custom-call(s32[64]{0:T(128)S(1)} %copy-done.2, bf16[144,4096]{1,0:T(8,128)(2,1)S(1)} %get-tuple-element.49.refs_1_, f32[1,4096]{1,0:T(1,128)S(1)} %get-tuple-element.50.refs_2_, f32[1,4096]{1,0:T(1,128)S(1)} %get-tuple-element.51.refs_3_, ...), custom_call_target="tpu_custom_call" | custom-call | tf_op jit(solution)/shard_map/attend/pallas_call | solution.py:297
  78.5 0.0 collective-permute-done.5.refs_5_
  78.5 0.1 collective-permute-start.7
  78.6 0.0 collective-permute-done.6.refs_6_
  78.6 2.7 %collective-permute-start.8 = (bf16[1344,128]{1,0:T(8,128)(2,1)S(1)}, bf16[1344,128]{1,0:T(8,128)(2,1)S(1)}, u32[]{:S(2)}, u32[]{:S(2)}) collective-permute-start(bf16[1344,128]{1,0:T(8,128)(2,1)S(1)} %collective-permute-done.6.refs_6_), channel_id=1, source_target_pairs={{0,224},{32,0},{64,32},{96,64},{128,96},{160,128},{192,160},{224,1... | collective-permute-start | bytes 1032200 | tf_op jit(solution)/shard_map/ppermute | solution.py:383
  81.3 29.0 %attend.9 = (f32[1,4096]{1,0:T(1,128)S(1)}, f32[1,4096]{1,0:T(1,128)S(1)}, f32[128,4096]{1,0:T(8,128)S(1)}) custom-call(s32[64]{0:T(128)S(1)} %copy-done.2, bf16[144,4096]{1,0:T(8,128)(2,1)S(1)} %get-tuple-element.49.refs_1_, f32[1,4096]{1,0:T(1,128)S(1)} %get-tuple-element.53.refs_2_, f32[1,4096]{1,0:T(1,128)S(1)} %get-tuple-element.54.refs_3_, ...), custom_call_target="tpu_custom_call" | custom-call | tf_op jit(solution)/shard_map/attend/pallas_call | solution.py:297
  110.3 0.0 collective-permute-done.7.refs_5_
  110.3 0.1 collective-permute-start.10
  110.4 0.0 collective-permute-done.8.refs_6_
  110.4 3.9 %collective-permute-start.11 = (bf16[1344,128]{1,0:T(8,128)(2,1)S(1)}, bf16[1344,128]{1,0:T(8,128)(2,1)S(1)}, u32[]{:S(2)}, u32[]{:S(2)}) collective-permute-start(bf16[1344,128]{1,0:T(8,128)(2,1)S(1)} %collective-permute-done.8.refs_6_), channel_id=1, source_target_pairs={{0,240},{16,224},{32,16},{48,0},{64,48},{80,32},{96,80},{112,64},{... | collective-permute-start | bytes 1032200 | tf_op jit(solution)/shard_map/ppermute | solution.py:387
  114.3 15.1 %attend.10 = (f32[1,2048]{1,0:T(1,128)S(1)}, f32[1,2048]{1,0:T(1,128)S(1)}, f32[128,2048]{1,0:T(8,128)S(1)}, bf16[144,1024]{1,0:T(8,128)(2,1)S(1)}) custom-call(s32[64]{0:T(128)S(1)} %copy-done.2, bf16[144,4096]{1,0:T(8,128)(2,1)S(1)} %get-tuple-element.49.refs_1_, f32[1,4096]{1,0:T(1,128)S(1)} %get-tuple-element.58.refs_2_, ...), custom_call_target="tpu_custom_call" | custom-call | tf_op jit(solution)/shard_map/attend/pallas_call | solution.py:297
  129.4 2.1 %collective-permute-start.9 = (bf16[144,1024]{1,0:T(8,128)(2,1)S(1)}, bf16[144,1024]{1,0:T(8,128)(2,1)S(1)}, u32[]{:S(2)}, u32[]{:S(2)}) collective-permute-start(bf16[144,1024]{1,0:T(8,128)(2,1)S(1)} %get-tuple-element.66), channel_id=1, source_target_pairs={{0,1},{1,0},{2,3},{3,2},{4,5},{5,4},{6,7},{7,6},{8,9},{9,8},{10,11... | collective-permute-start | bytes 884744 | tf_op jit(solution)/shard_map/ppermute | solution.py:391
  131.5 1.2 collective-permute-done.9.rec
  132.7 0.2 merge.1
  132.9 1.7 %collective-permute-start.13 = (bf16[144,1024]{1,0:T(8,128)(2,1)S(1)}, bf16[144,1024]{1,0:T(8,128)(2,1)S(1)}, u32[]{:S(2)}, u32[]{:S(2)}) collective-permute-start(bf16[144,1024]{1,0:T(8,128)(2,1)S(1)} %merge.1), channel_id=1, source_target_pairs={{0,16},{16,0},{1,17},{17,1},{2,18},{18,2},{3,19},{19,3},{4,20},{20... | collective-permute-start | bytes 884744 | tf_op jit(solution)/shard_map/ppermute | solution.py:393
  134.6 15.0 %attend.11 = (f32[1,2048]{1,0:T(1,128)S(1)}, f32[1,2048]{1,0:T(1,128)S(1)}, f32[128,2048]{1,0:T(8,128)S(1)}) custom-call(s32[64]{0:T(128)S(1)} %copy-done.2, bf16[144,4096]{1,0:T(8,128)(2,1)S(1)} %get-tuple-element.49.refs_1_, f32[1,4096]{1,0:T(1,128)S(1)} %get-tuple-element.58.refs_2_, f32[1,4096]{1,0:T(1,128)S(1)} %get-tuple-element.59.refs_3_, ...), custom_call_target="tpu_custom_call" | custom-call | tf_op jit(solution)/shard_map/attend/pallas_call | solution.py:297
  149.6 0.0 collective-permute-done.10.refs_5_
  149.6 0.0 collective-permute-done.11.refs_6_
  149.6 8.1 %attend.12 = bf16[144,1024]{1,0:T(8,128)(2,1)S(1)} custom-call(s32[64]{0:T(128)S(1)} %copy-done.2, bf16[144,4096]{1,0:T(8,128)(2,1)S(1)} %get-tuple-element.49.refs_1_, f32[1,2048]{1,0:T(1,128)S(1)} %get-tuple-element.68.refs_2_, f32[1,2048]{1,0:T(1,128)S(1)} %get-tuple-element.69.refs_3_, f32[128,2048]{1,0:T(8,128)S(1)} %get-tuple-element.70.refs_4_, ...), custom_call_target="tpu_custom_call" | custom-call | tf_op jit(solution)/shard_map/attend/pallas_call | solution.py:297
  157.7 0.7 collective-permute-start.12
  158.4 8.0 %attend.13 = (f32[1,1024]{1,0:T(1,128)S(1)}, f32[1,1024]{1,0:T(1,128)S(1)}, f32[128,1024]{1,0:T(8,128)S(1)}) custom-call(s32[64]{0:T(128)S(1)} %copy-done.2, bf16[144,4096]{1,0:T(8,128)(2,1)S(1)} %get-tuple-element.49.refs_1_, f32[1,2048]{1,0:T(1,128)S(1)} %get-tuple-element.68.refs_2_, f32[1,2048]{1,0:T(1,128)S(1)} %get-tuple-element.69.refs_3_, ...), custom_call_target="tpu_custom_call" | custom-call | tf_op jit(solution)/shard_map/attend/pallas_call | solution.py:297
  166.4 0.0 collective-permute-done.13.far
  166.4 0.0 collective-permute-done.12.rec
  166.4 1.5 finish.1
  (1 shorter events, 0.0 us)
Async XLA Ops:
  0.0 26.2 %copy-start.2 = (s32[64]{0:T(128)S(1)}, s32[64]{0:T(128)}, u32[]{:S(2)}) copy-start(s32[64]{0:T(128)} %refs_0_.13) | copy-start | bytes 772
  2.1 15.7 %collective-permute-start = (bf16[144,1024]{1,0:T(8,128)(2,1)S(1)}, bf16[144,1024]{1,0:T(8,128)(2,1)S(1)}, u32[]{:S(2)}, u32[]{:S(2)}) collective-permute-start(bf16[144,1024]{1,0:T(8,128)(2,1)S(1)} %get-tuple-element.42.refs_1_), channel_id=1, source_target_pairs={{0,1},{1,0},{2,3},{3,2},{4,5},{5,4},{6,7},{7,6},{8,9},{9,8},{10,11... | collective-permute-start | bytes 884744 | tf_op jit(solution)/shard_map/ppermute | solution.py:368
  5.4 12.3 %collective-permute-start.1 = (bf16[144,1024]{1,0:T(8,128)(2,1)S(1)}, bf16[144,1024]{1,0:T(8,128)(2,1)S(1)}, u32[]{:S(2)}, u32[]{:S(2)}) collective-permute-start(bf16[144,1024]{1,0:T(8,128)(2,1)S(1)} %get-tuple-element.42.refs_1_), channel_id=1, source_target_pairs={{0,16},{16,0},{1,17},{17,1},{2,18},{18,2},{3,19},{19,3},{4,20},{20... | collective-permute-start | bytes 884744 | tf_op jit(solution)/shard_map/ppermute | solution.py:367
  6.6 11.1 %all-to-all-start = ((bf16[8,2,64,128]{3,2,1,0:T(8,128)(2,1)}), bf16[8,2,64,128]{3,2,1,0:T(8,128)(2,1)S(1)}, u32[]{:S(2)}, u32[]{:S(2)}) async-start(bf16[8,2,64,128]{3,2,1,0:T(8,128)(2,1)} %get-tuple-element.46), calls=%async_computation | async-start | bytes 524288 | tf_op jit(solution)/shard_map/all_to_all | solution.py:369
  10.7 1.2 copy-start
  11.9 0.9 copy-start.1
  17.8 28.8 %collective-permute-start.3 = (bf16[1344,128]{1,0:T(8,128)(2,1)S(1)}, bf16[1344,128]{1,0:T(8,128)(2,1)S(1)}, u32[]{:S(2)}, u32[]{:S(2)}) collective-permute-start(bf16[1344,128]{1,0:T(8,128)(2,1)S(1)} %pad_maximum_fusion.refs_5_), channel_id=1, source_target_pairs={{0,32},{32,64},{64,96},{96,128},{128,160},{160,192},{192,224},{224... | collective-permute-start | bytes 1032200 | tf_op jit(solution)/shard_map/ppermute | solution.py:375
  19.5 27.2 %collective-permute-start.4 = (bf16[1344,128]{1,0:T(8,128)(2,1)S(1)}, bf16[1344,128]{1,0:T(8,128)(2,1)S(1)}, u32[]{:S(2)}, u32[]{:S(2)}) collective-permute-start(bf16[1344,128]{1,0:T(8,128)(2,1)S(1)} %pad_maximum_fusion.refs_5_), channel_id=1, source_target_pairs={{0,224},{32,0},{64,32},{96,64},{128,96},{160,128},{192,160},{224,1... | collective-permute-start | bytes 1032200 | tf_op jit(solution)/shard_map/ppermute | solution.py:376
  23.5 2.7 %collective-permute-start.2 = (bf16[144,1024]{1,0:T(8,128)(2,1)S(1)}, bf16[144,1024]{1,0:T(8,128)(2,1)S(1)}, u32[]{:S(2)}, u32[]{:S(2)}) collective-permute-start(bf16[144,1024]{1,0:T(8,128)(2,1)S(1)} %collective-permute-done.1.refs_3_), channel_id=1, source_target_pairs={{0,1},{1,0},{2,3},{3,2},{4,5},{5,4},{6,7},{7,6},{8,9},{9,8},{10,11... | collective-permute-start | bytes 884744 | tf_op jit(solution)/shard_map/ppermute | solution.py:371
  46.6 31.9 %collective-permute-start.5 = (bf16[1344,128]{1,0:T(8,128)(2,1)S(1)}, bf16[1344,128]{1,0:T(8,128)(2,1)S(1)}, u32[]{:S(2)}, u32[]{:S(2)}) collective-permute-start(bf16[1344,128]{1,0:T(8,128)(2,1)S(1)} %collective-permute-done.3.refs_5_), channel_id=1, source_target_pairs={{0,32},{32,64},{64,96},{96,128},{128,160},{160,192},{192,224},{224... | collective-permute-start | bytes 1032200 | tf_op jit(solution)/shard_map/ppermute | solution.py:379
  46.7 31.9 %collective-permute-start.6 = (bf16[1344,128]{1,0:T(8,128)(2,1)S(1)}, bf16[1344,128]{1,0:T(8,128)(2,1)S(1)}, u32[]{:S(2)}, u32[]{:S(2)}) collective-permute-start(bf16[1344,128]{1,0:T(8,128)(2,1)S(1)} %collective-permute-done.4.refs_6_), channel_id=1, source_target_pairs={{0,224},{32,0},{64,32},{96,64},{128,96},{160,128},{192,160},{224,1... | collective-permute-start | bytes 1032200 | tf_op jit(solution)/shard_map/ppermute | solution.py:380
  78.5 31.7 %collective-permute-start.7 = (bf16[1344,128]{1,0:T(8,128)(2,1)S(1)}, bf16[1344,128]{1,0:T(8,128)(2,1)S(1)}, u32[]{:S(2)}, u32[]{:S(2)}) collective-permute-start(bf16[1344,128]{1,0:T(8,128)(2,1)S(1)} %collective-permute-done.5.refs_5_), channel_id=1, source_target_pairs={{0,32},{32,64},{64,96},{96,128},{128,160},{160,192},{192,224},{224... | collective-permute-start | bytes 1032200 | tf_op jit(solution)/shard_map/ppermute | solution.py:382
  78.6 31.7 %collective-permute-start.8 = (bf16[1344,128]{1,0:T(8,128)(2,1)S(1)}, bf16[1344,128]{1,0:T(8,128)(2,1)S(1)}, u32[]{:S(2)}, u32[]{:S(2)}) collective-permute-start(bf16[1344,128]{1,0:T(8,128)(2,1)S(1)} %collective-permute-done.6.refs_6_), channel_id=1, source_target_pairs={{0,224},{32,0},{64,32},{96,64},{128,96},{160,128},{192,160},{224,1... | collective-permute-start | bytes 1032200 | tf_op jit(solution)/shard_map/ppermute | solution.py:383
  110.3 39.3 %collective-permute-start.10 = (bf16[1344,128]{1,0:T(8,128)(2,1)S(1)}, bf16[1344,128]{1,0:T(8,128)(2,1)S(1)}, u32[]{:S(2)}, u32[]{:S(2)}) collective-permute-start(bf16[1344,128]{1,0:T(8,128)(2,1)S(1)} %collective-permute-done.7.refs_5_), channel_id=1, source_target_pairs={{0,32},{32,64},{64,96},{96,128},{128,160},{160,192},{192,224},{224... | collective-permute-start | bytes 1032200 | tf_op jit(solution)/shard_map/ppermute | solution.py:385
  110.4 39.2 %collective-permute-start.11 = (bf16[1344,128]{1,0:T(8,128)(2,1)S(1)}, bf16[1344,128]{1,0:T(8,128)(2,1)S(1)}, u32[]{:S(2)}, u32[]{:S(2)}) collective-permute-start(bf16[1344,128]{1,0:T(8,128)(2,1)S(1)} %collective-permute-done.8.refs_6_), channel_id=1, source_target_pairs={{0,240},{16,224},{32,16},{48,0},{64,48},{80,32},{96,80},{112,64},{... | collective-permute-start | bytes 1032200 | tf_op jit(solution)/shard_map/ppermute | solution.py:387
  129.4 3.3 %collective-permute-start.9 = (bf16[144,1024]{1,0:T(8,128)(2,1)S(1)}, bf16[144,1024]{1,0:T(8,128)(2,1)S(1)}, u32[]{:S(2)}, u32[]{:S(2)}) collective-permute-start(bf16[144,1024]{1,0:T(8,128)(2,1)S(1)} %get-tuple-element.66), channel_id=1, source_target_pairs={{0,1},{1,0},{2,3},{3,2},{4,5},{5,4},{6,7},{7,6},{8,9},{9,8},{10,11... | collective-permute-start | bytes 884744 | tf_op jit(solution)/shard_map/ppermute | solution.py:391
  132.9 33.6 %collective-permute-start.13 = (bf16[144,1024]{1,0:T(8,128)(2,1)S(1)}, bf16[144,1024]{1,0:T(8,128)(2,1)S(1)}, u32[]{:S(2)}, u32[]{:S(2)}) collective-permute-start(bf16[144,1024]{1,0:T(8,128)(2,1)S(1)} %merge.1), channel_id=1, source_target_pairs={{0,16},{16,0},{1,17},{17,1},{2,18},{18,2},{3,19},{19,3},{4,20},{20... | collective-permute-start | bytes 884744 | tf_op jit(solution)/shard_map/ppermute | solution.py:393
  157.7 8.8 %collective-permute-start.12 = (bf16[144,1024]{1,0:T(8,128)(2,1)S(1)}, bf16[144,1024]{1,0:T(8,128)(2,1)S(1)}, u32[]{:S(2)}, u32[]{:S(2)}) collective-permute-start(bf16[144,1024]{1,0:T(8,128)(2,1)S(1)} %attend.12), channel_id=1, source_target_pairs={{0,1},{1,0},{2,3},{3,2},{4,5},{5,4},{6,7},{7,6},{8,9},{9,8},{10,11... | collective-permute-start | bytes 884744 | tf_op jit(solution)/shard_map/ppermute | solution.py:397

commit v6 on v5

--- a/solution.py
+++ b/solution.py
@@ -73,7 +73,7 @@
     return [extent_ref[base + j // 2] - (j % 2) * 128 - start for j in range(KVH)]
 
 
-def prepare(extent_hbm, soft_hbm, doc_hbm, q_hbm, doc_out, q_out, extent_ref, soft_ref, doc_ref, q_ref, sems):
+def prepare(extent_hbm, soft_hbm, doc_hbm, q_hbm, doc_out, q_out, bare_out, extent_ref, soft_ref, doc_ref, q_ref, sems):
     pairs = ((extent_hbm, extent_ref), (doc_hbm, doc_ref), (soft_hbm, soft_ref), (q_hbm, q_ref))
     copies = [pltpu.make_async_copy(src, dst, sems.at[i]) for i, (src, dst) in enumerate(pairs)]
     for copy in copies:
@@ -94,7 +94,9 @@
     tokens, heads, _ = q_ref.shape
     for h in range(heads):
         cols = slice(h * tokens, (h + 1) * tokens)
-        q_out[:HD, cols] = q_ref[:, h, :].astype(F32).T.astype(BF16)
+        turned = q_ref[:, h, :].astype(F32).T.astype(BF16)
+        q_out[:HD, cols] = turned
+        bare_out[:, cols] = turned
         factor = jnp.full((1, tokens), 1.0, F32) / soft_ref[h] * SCALE2
         q_out[HD:, cols] = aux_rows(factor)
 
@@ -106,10 +108,11 @@
     return pl.pallas_call(
         prepare,
         in_specs=[pl.BlockSpec(memory_space=pltpu.HBM)] * 4,
-        out_specs=[vmem, vmem],
+        out_specs=[vmem, vmem, vmem],
         out_shape=[
             jax.ShapeDtypeStruct((KVH, 2, rows, HD), BF16),
             jax.ShapeDtypeStruct((HD + AUX, tokens * heads), BF16),
+            jax.ShapeDtypeStruct((HD, tokens * heads), BF16),
         ],
         scratch_shapes=[
             pltpu.SMEM(extent.shape, jnp.int32),
@@ -158,7 +161,8 @@
         pay = refs[BLOCKS : BLOCKS + count]
         m_out, l_out, acc_out, q_ref, k_ref, v_ref, m0, l0, acc0 = refs[BLOCKS + count :]
         for n, part in enumerate(parts):
-            q_ref[:, n * ROWS : (n + 1) * ROWS] = part[...]
+            q_ref[:HD, n * ROWS : (n + 1) * ROWS] = part[:HD, :]
+            q_ref[HD:, n * ROWS : (n + 1) * ROWS] = parts[n % 2][HD:, :]
     else:
         q_ref, m0, l0, acc0 = refs[:4]
         pay = refs[4 : 4 + count]
@@ -363,8 +367,8 @@
     softening_factor,
 ):
     extent = document_valid_extent
-    sending, q0 = prepared(extent, softening_factor, document_memory_pairs, asker_vectors)
-    q1 = lax.ppermute(q0, "yh", shift(2, 1))
+    sending, q0, bare = prepared(extent, softening_factor, document_memory_pairs, asker_vectors)
+    q1 = lax.ppermute(bare, "yh", shift(2, 1))
     q2 = lax.ppermute(q0, "c", shift(2, 1))
     moved = lax.all_to_all(sending, ("yl", "x"), 0, 0, tiled=True)
     cache = cache_block(after(asker_memory_pairs, q0), leading_memory_pairs)

time: 168 us -> 168 us (level)
  no operation moved by 1% of the time
where the time goes in v6:
time: 168 us
  Pallas kernels  129 us (77%)
  starting transfers between devices  30 us (18%)
  waiting for transfers between devices  7.07 us (4%)
  local copies, waits for them, and re-layouts  2.17 us (1%)
    pallas_call x7, Pallas kernels, attend(): pl.pallas_call(functools.partial(attend_kernel, shards, mode, q_low), in_...  125 us
    all_to_all x1, waiting for transfers between devices, body(): moved = lax.all_to_all(sending, ('yl', 'x'), 0, 0, tiled=True)  4.66 us
    all_to_all x1, starting transfers between devices, body(): moved = lax.all_to_all(sending, ('yl', 'x'), 0, 0, tiled=True)  4.13 us
    ppermute x1, starting transfers between devices, body(): b1 = lax.ppermute(own, 'z', down)  4.03 us
    ppermute x1, starting transfers between devices, body(): b4 = lax.ppermute(after(b3, state[0]), ('z', 'yh'), cross)  3.92 us
  transfers between devices with their start and end apart: 15, of which 3 were waited for; matrix products, arithmetic and copies ran while one was open for 0% of the time, Pallas kernels for 74%

profile of v6, /device:TPU:1, one launch (start us, length us, event | category | flops | bytes accessed | tf_op | source)
XLA Modules:
  0.0 168.0 jit_solution(6528897020205267603)
XLA Ops:
  0.0 0.0 copy-start.2
  0.0 2.1 %prepare.1 = (bf16[8,2,64,128]{3,2,1,0:T(8,128)(2,1)}, bf16[144,1024]{1,0:T(8,128)(2,1)S(1)}, bf16[128,1024]{1,0:T(8,128)(2,1)S(1)}) custom-call(s32[64]{0:T(128)} %refs_0_.13, f32[4]{0:T(128)} %soft_hbm.1, bf16[64,16,128]{2,1,0:T(8,128)(2,1)} %doc_hbm.1, bf16[256,4,128]{2,1,0:T(4,128)(2,1)} %q_hbm.1), custom_call_target="tpu_custom_call" | custom-call | tf_op jit(solution)/shard_map/prepare/pallas_call | solution.py:108
  2.1 3.3 %collective-permute-start = (bf16[144,1024]{1,0:T(8,128)(2,1)S(1)}, bf16[144,1024]{1,0:T(8,128)(2,1)S(1)}, u32[]{:S(2)}, u32[]{:S(2)}) collective-permute-start(bf16[144,1024]{1,0:T(8,128)(2,1)S(1)} %get-tuple-element.44.refs_1_), channel_id=1, source_target_pairs={{0,1},{1,0},{2,3},{3,2},{4,5},{5,4},{6,7},{7,6},{8,9},{9,8},{10,11... | collective-permute-start | bytes 884744 | tf_op jit(solution)/shard_map/ppermute | solution.py:372
  5.4 1.2 collective-permute-start.1
  6.6 4.1 %all-to-all-start = ((bf16[8,2,64,128]{3,2,1,0:T(8,128)(2,1)}), bf16[8,2,64,128]{3,2,1,0:T(8,128)(2,1)S(1)}, u32[]{:S(2)}, u32[]{:S(2)}) async-start(bf16[8,2,64,128]{3,2,1,0:T(8,128)(2,1)} %get-tuple-element.48), calls=%async_computation | async-start | bytes 524288 | tf_op jit(solution)/shard_map/all_to_all | solution.py:373
  10.7 0.0 copy-start
  10.7 1.2 copy-done
  11.9 0.0 copy-start.1
  11.9 0.9 copy-done.1
  12.9 0.2 caches.1
  13.1 4.7 %all-to-all-done = bf16[8,2,64,128]{3,2,1,0:T(8,128)(2,1)S(1)} async-done(((bf16[8,2,64,128]{3,2,1,0:T(8,128)(2,1)}), bf16[8,2,64,128]{3,2,1,0:T(8,128)(2,1)S(1)}, u32[]{:S(2)}, u32[]{:S(2)}) %all-to-all-start) | async-done | bytes 262176 | tf_op jit(solution)/shard_map/all_to_all | solution.py:373
  17.7 0.0 collective-permute-done.1.refs_3_
  17.7 0.0 collective-permute-done.refs_2_
  17.8 1.7 %collective-permute-start.3 = (bf16[1344,128]{1,0:T(8,128)(2,1)S(1)}, bf16[1344,128]{1,0:T(8,128)(2,1)S(1)}, u32[]{:S(2)}, u32[]{:S(2)}) collective-permute-start(bf16[1344,128]{1,0:T(8,128)(2,1)S(1)} %pad_maximum_fusion.refs_5_), channel_id=1, source_target_pairs={{0,32},{32,64},{64,96},{96,128},{128,160},{160,192},{192,224},{224... | collective-permute-start | bytes 1032200 | tf_op jit(solution)/shard_map/ppermute | solution.py:379
  19.5 4.0 %collective-permute-start.4 = (bf16[1344,128]{1,0:T(8,128)(2,1)S(1)}, bf16[1344,128]{1,0:T(8,128)(2,1)S(1)}, u32[]{:S(2)}, u32[]{:S(2)}) collective-permute-start(bf16[1344,128]{1,0:T(8,128)(2,1)S(1)} %pad_maximum_fusion.refs_5_), channel_id=1, source_target_pairs={{0,224},{32,0},{64,32},{96,64},{128,96},{160,128},{192,160},{224,1... | collective-permute-start | bytes 1032200 | tf_op jit(solution)/shard_map/ppermute | solution.py:380
  23.5 1.5 collective-permute-start.2
  25.0 1.2 collective-permute-done.2.refs_4_
  26.2 0.0 copy-done.2
  26.2 20.4 %attend.7 = (f32[1,4096]{1,0:T(1,128)S(1)}, f32[1,4096]{1,0:T(1,128)S(1)}, f32[128,4096]{1,0:T(8,128)S(1)}, bf16[144,4096]{1,0:T(8,128)(2,1)S(1)}) custom-call(s32[64]{0:T(128)S(1)} %copy-done.2, bf16[144,1024]{1,0:T(8,128)(2,1)S(1)} %get-tuple-element.44.refs_1_, bf16[144,1024]{1,0:T(8,128)(2,1)S(1)} %collective-permute-done.refs_2_, ...), custom_call_target="tpu_custom_call" | custom-call | tf_op jit(solution)/shard_map/attend/pallas_call | solution.py:301
  46.6 0.0 collective-permute-done.3.refs_5_
  46.6 0.1 collective-permute-start.5
  46.7 0.0 collective-permute-done.4.refs_6_
  46.7 2.7 %collective-permute-start.6 = (bf16[1344,128]{1,0:T(8,128)(2,1)S(1)}, bf16[1344,128]{1,0:T(8,128)(2,1)S(1)}, u32[]{:S(2)}, u32[]{:S(2)}) collective-permute-start(bf16[1344,128]{1,0:T(8,128)(2,1)S(1)} %collective-permute-done.4.refs_6_), channel_id=1, source_target_pairs={{0,224},{32,0},{64,32},{96,64},{128,96},{160,128},{192,160},{224,1... | collective-permute-start | bytes 1032200 | tf_op jit(solution)/shard_map/ppermute | solution.py:384
  49.3 29.2 %attend.8 = (f32[1,4096]{1,0:T(1,128)S(1)}, f32[1,4096]{1,0:T(1,128)S(1)}, f32[128,4096]{1,0:T(8,128)S(1)}) custom-call(s32[64]{0:T(128)S(1)} %copy-done.2, bf16[144,4096]{1,0:T(8,128)(2,1)S(1)} %get-tuple-element.51.refs_1_, f32[1,4096]{1,0:T(1,128)S(1)} %get-tuple-element.52.refs_2_, f32[1,4096]{1,0:T(1,128)S(1)} %get-tuple-element.53.refs_3_, ...), custom_call_target="tpu_custom_call" | custom-call | tf_op jit(solution)/shard_map/attend/pallas_call | solution.py:301
  78.5 0.0 collective-permute-done.5.refs_5_
  78.5 0.1 collective-permute-start.7
  78.6 0.0 collective-permute-done.6.refs_6_
  78.6 2.7 %collective-permute-start.8 = (bf16[1344,128]{1,0:T(8,128)(2,1)S(1)}, bf16[1344,128]{1,0:T(8,128)(2,1)S(1)}, u32[]{:S(2)}, u32[]{:S(2)}) collective-permute-start(bf16[1344,128]{1,0:T(8,128)(2,1)S(1)} %collective-permute-done.6.refs_6_), channel_id=1, source_target_pairs={{0,224},{32,0},{64,32},{96,64},{128,96},{160,128},{192,160},{224,1... | collective-permute-start | bytes 1032200 | tf_op jit(solution)/shard_map/ppermute | solution.py:387
  81.3 29.0 %attend.9 = (f32[1,4096]{1,0:T(1,128)S(1)}, f32[1,4096]{1,0:T(1,128)S(1)}, f32[128,4096]{1,0:T(8,128)S(1)}) custom-call(s32[64]{0:T(128)S(1)} %copy-done.2, bf16[144,4096]{1,0:T(8,128)(2,1)S(1)} %get-tuple-element.51.refs_1_, f32[1,4096]{1,0:T(1,128)S(1)} %get-tuple-element.55.refs_2_, f32[1,4096]{1,0:T(1,128)S(1)} %get-tuple-element.56.refs_3_, ...), custom_call_target="tpu_custom_call" | custom-call | tf_op jit(solution)/shard_map/attend/pallas_call | solution.py:301
  110.3 0.0 collective-permute-done.7.refs_5_
  110.3 0.1 collective-permute-start.10
  110.4 0.0 collective-permute-done.8.refs_6_
  110.4 3.9 %collective-permute-start.11 = (bf16[1344,128]{1,0:T(8,128)(2,1)S(1)}, bf16[1344,128]{1,0:T(8,128)(2,1)S(1)}, u32[]{:S(2)}, u32[]{:S(2)}) collective-permute-start(bf16[1344,128]{1,0:T(8,128)(2,1)S(1)} %collective-permute-done.8.refs_6_), channel_id=1, source_target_pairs={{0,240},{16,224},{32,16},{48,0},{64,48},{80,32},{96,80},{112,64},{... | collective-permute-start | bytes 1032200 | tf_op jit(solution)/shard_map/ppermute | solution.py:391
  114.3 15.1 %attend.10 = (f32[1,2048]{1,0:T(1,128)S(1)}, f32[1,2048]{1,0:T(1,128)S(1)}, f32[128,2048]{1,0:T(8,128)S(1)}, bf16[144,1024]{1,0:T(8,128)(2,1)S(1)}) custom-call(s32[64]{0:T(128)S(1)} %copy-done.2, bf16[144,4096]{1,0:T(8,128)(2,1)S(1)} %get-tuple-element.51.refs_1_, f32[1,4096]{1,0:T(1,128)S(1)} %get-tuple-element.60.refs_2_, ...), custom_call_target="tpu_custom_call" | custom-call | tf_op jit(solution)/shard_map/attend/pallas_call | solution.py:301
  129.3 2.1 %collective-permute-start.9 = (bf16[144,1024]{1,0:T(8,128)(2,1)S(1)}, bf16[144,1024]{1,0:T(8,128)(2,1)S(1)}, u32[]{:S(2)}, u32[]{:S(2)}) collective-permute-start(bf16[144,1024]{1,0:T(8,128)(2,1)S(1)} %get-tuple-element.68), channel_id=1, source_target_pairs={{0,1},{1,0},{2,3},{3,2},{4,5},{5,4},{6,7},{7,6},{8,9},{9,8},{10,11... | collective-permute-start | bytes 884744 | tf_op jit(solution)/shard_map/ppermute | solution.py:395
  131.5 1.2 collective-permute-done.9.rec
  132.7 0.2 merge.1
  132.9 1.7 %collective-permute-start.13 = (bf16[144,1024]{1,0:T(8,128)(2,1)S(1)}, bf16[144,1024]{1,0:T(8,128)(2,1)S(1)}, u32[]{:S(2)}, u32[]{:S(2)}) collective-permute-start(bf16[144,1024]{1,0:T(8,128)(2,1)S(1)} %merge.1), channel_id=1, source_target_pairs={{0,16},{16,0},{1,17},{17,1},{2,18},{18,2},{3,19},{19,3},{4,20},{20... | collective-permute-start | bytes 884744 | tf_op jit(solution)/shard_map/ppermute | solution.py:397
  134.6 15.0 %attend.11 = (f32[1,2048]{1,0:T(1,128)S(1)}, f32[1,2048]{1,0:T(1,128)S(1)}, f32[128,2048]{1,0:T(8,128)S(1)}) custom-call(s32[64]{0:T(128)S(1)} %copy-done.2, bf16[144,4096]{1,0:T(8,128)(2,1)S(1)} %get-tuple-element.51.refs_1_, f32[1,4096]{1,0:T(1,128)S(1)} %get-tuple-element.60.refs_2_, f32[1,4096]{1,0:T(1,128)S(1)} %get-tuple-element.61.refs_3_, ...), custom_call_target="tpu_custom_call" | custom-call | tf_op jit(solution)/shard_map/attend/pallas_call | solution.py:301
  149.6 0.0 collective-permute-done.10.refs_5_
  149.6 0.0 collective-permute-done.11.refs_6_
  149.6 8.1 %attend.12 = bf16[144,1024]{1,0:T(8,128)(2,1)S(1)} custom-call(s32[64]{0:T(128)S(1)} %copy-done.2, bf16[144,4096]{1,0:T(8,128)(2,1)S(1)} %get-tuple-element.51.refs_1_, f32[1,2048]{1,0:T(1,128)S(1)} %get-tuple-element.70.refs_2_, f32[1,2048]{1,0:T(1,128)S(1)} %get-tuple-element.71.refs_3_, f32[128,2048]{1,0:T(8,128)S(1)} %get-tuple-element.72.refs_4_, ...), custom_call_target="tpu_custom_call" | custom-call | tf_op jit(solution)/shard_map/attend/pallas_call | solution.py:301
  157.7 0.7 collective-permute-start.12
  158.4 8.0 %attend.13 = (f32[1,1024]{1,0:T(1,128)S(1)}, f32[1,1024]{1,0:T(1,128)S(1)}, f32[128,1024]{1,0:T(8,128)S(1)}) custom-call(s32[64]{0:T(128)S(1)} %copy-done.2, bf16[144,4096]{1,0:T(8,128)(2,1)S(1)} %get-tuple-element.51.refs_1_, f32[1,2048]{1,0:T(1,128)S(1)} %get-tuple-element.70.refs_2_, f32[1,2048]{1,0:T(1,128)S(1)} %get-tuple-element.71.refs_3_, ...), custom_call_target="tpu_custom_call" | custom-call | tf_op jit(solution)/shard_map/attend/pallas_call | solution.py:301
  166.4 0.0 collective-permute-done.13.far
  166.4 0.0 collective-permute-done.12.rec
  166.4 1.5 finish.1
  (1 shorter events, 0.0 us)
Async XLA Ops:
  0.0 26.2 %copy-start.2 = (s32[64]{0:T(128)S(1)}, s32[64]{0:T(128)}, u32[]{:S(2)}) copy-start(s32[64]{0:T(128)} %refs_0_.13) | copy-start | bytes 772
  2.1 15.7 %collective-permute-start = (bf16[144,1024]{1,0:T(8,128)(2,1)S(1)}, bf16[144,1024]{1,0:T(8,128)(2,1)S(1)}, u32[]{:S(2)}, u32[]{:S(2)}) collective-permute-start(bf16[144,1024]{1,0:T(8,128)(2,1)S(1)} %get-tuple-element.44.refs_1_), channel_id=1, source_target_pairs={{0,1},{1,0},{2,3},{3,2},{4,5},{5,4},{6,7},{7,6},{8,9},{9,8},{10,11... | collective-permute-start | bytes 884744 | tf_op jit(solution)/shard_map/ppermute | solution.py:372
  5.4 12.3 %collective-permute-start.1 = (bf16[128,1024]{1,0:T(8,128)(2,1)S(1)}, bf16[128,1024]{1,0:T(8,128)(2,1)S(1)}, u32[]{:S(2)}, u32[]{:S(2)}) collective-permute-start(bf16[128,1024]{1,0:T(8,128)(2,1)S(1)} %get-tuple-element.43), channel_id=1, source_target_pairs={{0,16},{16,0},{1,17},{17,1},{2,18},{18,2},{3,19},{19,3},{4,20},{20... | collective-permute-start | bytes 786440 | tf_op jit(solution)/shard_map/ppermute | solution.py:371
  6.6 11.1 %all-to-all-start = ((bf16[8,2,64,128]{3,2,1,0:T(8,128)(2,1)}), bf16[8,2,64,128]{3,2,1,0:T(8,128)(2,1)S(1)}, u32[]{:S(2)}, u32[]{:S(2)}) async-start(bf16[8,2,64,128]{3,2,1,0:T(8,128)(2,1)} %get-tuple-element.48), calls=%async_computation | async-start | bytes 524288 | tf_op jit(solution)/shard_map/all_to_all | solution.py:373
  10.7 1.2 copy-start
  11.9 0.9 copy-start.1
  17.8 28.8 %collective-permute-start.3 = (bf16[1344,128]{1,0:T(8,128)(2,1)S(1)}, bf16[1344,128]{1,0:T(8,128)(2,1)S(1)}, u32[]{:S(2)}, u32[]{:S(2)}) collective-permute-start(bf16[1344,128]{1,0:T(8,128)(2,1)S(1)} %pad_maximum_fusion.refs_5_), channel_id=1, source_target_pairs={{0,32},{32,64},{64,96},{96,128},{128,160},{160,192},{192,224},{224... | collective-permute-start | bytes 1032200 | tf_op jit(solution)/shard_map/ppermute | solution.py:379
  19.5 27.2 %collective-permute-start.4 = (bf16[1344,128]{1,0:T(8,128)(2,1)S(1)}, bf16[1344,128]{1,0:T(8,128)(2,1)S(1)}, u32[]{:S(2)}, u32[]{:S(2)}) collective-permute-start(bf16[1344,128]{1,0:T(8,128)(2,1)S(1)} %pad_maximum_fusion.refs_5_), channel_id=1, source_target_pairs={{0,224},{32,0},{64,32},{96,64},{128,96},{160,128},{192,160},{224,1... | collective-permute-start | bytes 1032200 | tf_op jit(solution)/shard_map/ppermute | solution.py:380
  23.5 2.7 %collective-permute-start.2 = (bf16[128,1024]{1,0:T(8,128)(2,1)S(1)}, bf16[128,1024]{1,0:T(8,128)(2,1)S(1)}, u32[]{:S(2)}, u32[]{:S(2)}) collective-permute-start(bf16[128,1024]{1,0:T(8,128)(2,1)S(1)} %collective-permute-done.1.refs_3_), channel_id=1, source_target_pairs={{0,1},{1,0},{2,3},{3,2},{4,5},{5,4},{6,7},{7,6},{8,9},{9,8},{10,11... | collective-permute-start | bytes 786440 | tf_op jit(solution)/shard_map/ppermute | solution.py:375
  46.6 31.9 %collective-permute-start.5 = (bf16[1344,128]{1,0:T(8,128)(2,1)S(1)}, bf16[1344,128]{1,0:T(8,128)(2,1)S(1)}, u32[]{:S(2)}, u32[]{:S(2)}) collective-permute-start(bf16[1344,128]{1,0:T(8,128)(2,1)S(1)} %collective-permute-done.3.refs_5_), channel_id=1, source_target_pairs={{0,32},{32,64},{64,96},{96,128},{128,160},{160,192},{192,224},{224... | collective-permute-start | bytes 1032200 | tf_op jit(solution)/shard_map/ppermute | solution.py:383
  46.7 31.9 %collective-permute-start.6 = (bf16[1344,128]{1,0:T(8,128)(2,1)S(1)}, bf16[1344,128]{1,0:T(8,128)(2,1)S(1)}, u32[]{:S(2)}, u32[]{:S(2)}) collective-permute-start(bf16[1344,128]{1,0:T(8,128)(2,1)S(1)} %collective-permute-done.4.refs_6_), channel_id=1, source_target_pairs={{0,224},{32,0},{64,32},{96,64},{128,96},{160,128},{192,160},{224,1... | collective-permute-start | bytes 1032200 | tf_op jit(solution)/shard_map/ppermute | solution.py:384
  78.5 31.7 %collective-permute-start.7 = (bf16[1344,128]{1,0:T(8,128)(2,1)S(1)}, bf16[1344,128]{1,0:T(8,128)(2,1)S(1)}, u32[]{:S(2)}, u32[]{:S(2)}) collective-permute-start(bf16[1344,128]{1,0:T(8,128)(2,1)S(1)} %collective-permute-done.5.refs_5_), channel_id=1, source_target_pairs={{0,32},{32,64},{64,96},{96,128},{128,160},{160,192},{192,224},{224... | collective-permute-start | bytes 1032200 | tf_op jit(solution)/shard_map/ppermute | solution.py:386
  78.6 31.7 %collective-permute-start.8 = (bf16[1344,128]{1,0:T(8,128)(2,1)S(1)}, bf16[1344,128]{1,0:T(8,128)(2,1)S(1)}, u32[]{:S(2)}, u32[]{:S(2)}) collective-permute-start(bf16[1344,128]{1,0:T(8,128)(2,1)S(1)} %collective-permute-done.6.refs_6_), channel_id=1, source_target_pairs={{0,224},{32,0},{64,32},{96,64},{128,96},{160,128},{192,160},{224,1... | collective-permute-start | bytes 1032200 | tf_op jit(solution)/shard_map/ppermute | solution.py:387
  110.3 39.3 %collective-permute-start.10 = (bf16[1344,128]{1,0:T(8,128)(2,1)S(1)}, bf16[1344,128]{1,0:T(8,128)(2,1)S(1)}, u32[]{:S(2)}, u32[]{:S(2)}) collective-permute-start(bf16[1344,128]{1,0:T(8,128)(2,1)S(1)} %collective-permute-done.7.refs_5_), channel_id=1, source_target_pairs={{0,32},{32,64},{64,96},{96,128},{128,160},{160,192},{192,224},{224... | collective-permute-start | bytes 1032200 | tf_op jit(solution)/shard_map/ppermute | solution.py:389
  110.4 39.2 %collective-permute-start.11 = (bf16[1344,128]{1,0:T(8,128)(2,1)S(1)}, bf16[1344,128]{1,0:T(8,128)(2,1)S(1)}, u32[]{:S(2)}, u32[]{:S(2)}) collective-permute-start(bf16[1344,128]{1,0:T(8,128)(2,1)S(1)} %collective-permute-done.8.refs_6_), channel_id=1, source_target_pairs={{0,240},{16,224},{32,16},{48,0},{64,48},{80,32},{96,80},{112,64},{... | collective-permute-start | bytes 1032200 | tf_op jit(solution)/shard_map/ppermute | solution.py:391
  129.3 3.3 %collective-permute-start.9 = (bf16[144,1024]{1,0:T(8,128)(2,1)S(1)}, bf16[144,1024]{1,0:T(8,128)(2,1)S(1)}, u32[]{:S(2)}, u32[]{:S(2)}) collective-permute-start(bf16[144,1024]{1,0:T(8,128)(2,1)S(1)} %get-tuple-element.68), channel_id=1, source_target_pairs={{0,1},{1,0},{2,3},{3,2},{4,5},{5,4},{6,7},{7,6},{8,9},{9,8},{10,11... | collective-permute-start | bytes 884744 | tf_op jit(solution)/shard_map/ppermute | solution.py:395
  132.9 33.6 %collective-permute-start.13 = (bf16[144,1024]{1,0:T(8,128)(2,1)S(1)}, bf16[144,1024]{1,0:T(8,128)(2,1)S(1)}, u32[]{:S(2)}, u32[]{:S(2)}) collective-permute-start(bf16[144,1024]{1,0:T(8,128)(2,1)S(1)} %merge.1), channel_id=1, source_target_pairs={{0,16},{16,0},{1,17},{17,1},{2,18},{18,2},{3,19},{19,3},{4,20},{20... | collective-permute-start | bytes 884744 | tf_op jit(solution)/shard_map/ppermute | solution.py:397
  157.7 8.8 %collective-permute-start.12 = (bf16[144,1024]{1,0:T(8,128)(2,1)S(1)}, bf16[144,1024]{1,0:T(8,128)(2,1)S(1)}, u32[]{:S(2)}, u32[]{:S(2)}) collective-permute-start(bf16[144,1024]{1,0:T(8,128)(2,1)S(1)} %attend.12), channel_id=1, source_target_pairs={{0,1},{1,0},{2,3},{3,2},{4,5},{5,4},{6,7},{7,6},{8,9},{9,8},{10,11... | collective-permute-start | bytes 884744 | tf_op jit(solution)/shard_map/ppermute | solution.py:401
